TPU v7x, 32 devices: a whole 2x2x4 slice. The times are simulated.
32 devices in a mesh: row: 8 (over z, y), col: 4 (over x, core).
Axes of the slice: x: 2, y: 2, z: 4, core: 2. Of those that a mesh axis runs over, the one named last changes fastest.
Arguments:
- features: bfloat16 [8192, 512], P(('col', 'row')), may hold values from -6 to 6
- blocks: bfloat16 [8, 4, 12, 128, 128], P('row', 'col'), may hold values from -0.75 to 0.75
- block_rows: int32 [8, 4, 12], P('row', 'col'), may hold values from 0 to 7, as said below
- block_cols: int32 [8, 4, 12], P('row', 'col'), may hold values from 0 to 15, as said below
- block_count: int32 [8, 4], P('row', 'col'), may hold values from 2 to 12, as said below
- weight: bfloat16 [512, 512], replicated, may hold values from -0.25 to 0.25
- bias_vector: float32 [512], replicated, may hold values from -4 to 4
- upstream: bfloat16 [8192, 512], P(('row', 'col')), may hold values from -6 to 6
Outputs:
- activated: bfloat16 [8192, 512], P(('row', 'col'))
- grad_weight: float32 [512, 512], replicated
- grad_bias: float32 [512], replicated
- grad_features: bfloat16 [8192, 512], P(('col', 'row'))
Inputs may be any that keep to these rules, and one draw needn't show every extreme that they name: `block_rows`: the live (block row, block column) pairs of one device are distinct. `block_cols`: paired slot by slot with block_rows. `block_count`: live slots come first; some device has exactly 12 live slots.
All inputs are finite; a program needn't handle non-finite values.
Results may differ from a plain program's by a relative error of at most 0.0061.
Values may be sent and summed in bfloat16 or wider, within the bound.
No kernel may reach another device: no remote copies, remote signals or barrier semaphores. Data moves between devices by JAX's collectives and lax.ppermute only.
A program may use at most 64 MiB of HBM per device.

v0:
```python
import math

import jax
import jax.numpy as jnp
from jax import lax
from jax.sharding import PartitionSpec as P


def block_product(block_tiles, take_index, put_index, live_count, source, out_rows, transposed):
    slot_total = block_tiles.shape[0]
    block_size = block_tiles.shape[1]
    width = source.shape[1]
    group_size = math.gcd(slot_total, 32)
    source_blocks = source.reshape(-1, block_size, width)
    totals = jnp.zeros((out_rows // block_size, block_size, width), jnp.float32)
    form = "gji,gjh->gih" if transposed else "gij,gjh->gih"

    def one_turn(turn, totals):
        first_slot = turn * group_size
        chosen = lax.dynamic_slice_in_dim(block_tiles, first_slot, group_size, 0)
        take_now = lax.dynamic_slice_in_dim(take_index, first_slot, group_size, 0)
        put_now = lax.dynamic_slice_in_dim(put_index, first_slot, group_size, 0)
        live_mask = first_slot + jnp.arange(group_size, dtype=jnp.int32) < live_count
        chosen = jnp.where(live_mask[:, None, None], chosen, jnp.zeros_like(chosen))
        picked = source_blocks[take_now]
        product = jnp.einsum(form, chosen, picked, preferred_element_type=jnp.float32)
        return totals.at[put_now].add(product)

    last_turn = slot_total // group_size
    totals = lax.fori_loop(0, last_turn, one_turn, totals)
    return totals.reshape(out_rows, width)


def dense_part(hidden, weight, bias_vector, upstream):
    preact = jnp.dot(hidden, weight, preferred_element_type=jnp.float32) + bias_vector
    sigmoid_pre = jax.nn.sigmoid(preact)
    activated = (preact * sigmoid_pre).astype(jnp.bfloat16)
    dpre = (
        upstream.astype(jnp.float32) * sigmoid_pre * (1.0 + preact * (1.0 - sigmoid_pre))
    ).astype(jnp.bfloat16)
    grad_weight = lax.dot_general(
        hidden, dpre, (((0,), (0,)), ((), ())), preferred_element_type=jnp.float32
    )
    grad_bias = jnp.sum(dpre.astype(jnp.float32), axis=0)
    dhidden = lax.dot_general(
        dpre, weight, (((1,), (1,)), ((), ())), preferred_element_type=jnp.float32
    ).astype(jnp.bfloat16)
    return (activated, grad_weight, grad_bias, dhidden)


def shards(features, blocks, block_rows, block_cols, block_count, weight, bias_vector, upstream):
    node_dev = features.shape[0]
    row_size = lax.axis_size("row")
    col_size = lax.axis_size("col")
    node_total = node_dev * row_size * col_size
    scale_factor = 1.0 / math.sqrt(node_total)
    block_tiles = blocks[0, 0]
    rows_local = block_rows[0, 0]
    cols_local = block_cols[0, 0]
    live_count = block_count[0, 0]
    gathered = lax.all_gather(features, "row", axis=0, tiled=True)
    partial_value = block_product(
        block_tiles, cols_local, rows_local, live_count, gathered, node_dev * col_size, False
    )
    hidden_all = lax.psum(partial_value, "col").astype(jnp.bfloat16)
    upstream_all = lax.all_gather(upstream, "col", axis=0, tiled=True)
    activated_all, grad_weight, grad_bias, dhidden_rows = dense_part(
        hidden_all, weight, bias_vector, upstream_all
    )
    activated = lax.dynamic_slice_in_dim(
        activated_all, lax.axis_index("col") * node_dev, node_dev, 0
    )
    grad_weight, grad_bias = lax.psum((grad_weight, grad_bias), "row")
    grad_weight = grad_weight * scale_factor
    grad_bias = grad_bias * scale_factor
    grad_partial = block_product(
        block_tiles, rows_local, cols_local, live_count, dhidden_rows, node_dev * row_size, True
    )
    grad_features = lax.psum_scatter(grad_partial, "row", scatter_dimension=0, tiled=True).astype(
        jnp.bfloat16
    )
    return (activated, grad_weight, grad_bias, grad_features)


def solution(mesh):
    in_specs = (
        P(("col", "row"), None),
        P("row", "col", None, None, None),
        P("row", "col", None),
        P("row", "col", None),
        P("row", "col"),
        P(),
        P(),
        P(("row", "col"), None),
    )
    out_specs = (P(("row", "col"), None), P(), P(), P(("col", "row"), None))
    return jax.shard_map(shards, mesh=mesh, in_specs=in_specs, out_specs=out_specs, check_vma=False)
```

profile of v0, /device:TPU:0, one launch (start us, length us, event | category | flops | bytes accessed | tf_op | source)
XLA Modules:
  0.0 311.0 jit_solution(11424116209015850548)
XLA Ops:
  7.2 0.0 copy-start
  7.2 0.0 copy-start.1
  7.2 0.0 copy-start.2
  7.2 0.0 all-gather.3.cloned.1.call-start
  7.2 0.7 all-gather.3.cloned.1.call-update
  7.9 0.0 all-gather.5.cloned.1.call-start
  8.0 0.7 all-gather.5.cloned.1.call-update
  8.7 0.0 all-reduce.3.cloned.1.call-start
  8.7 1.2 copy.12
  10.0 52.2 %all-gather.3.cloned.1.call-done = bf16[2048,512]{1,0:T(8,128)(2,1)} async-done(((bf16[256,512]{1,0:T(8,128)(2,1)}), bf16[2048,512]{1,0:T(8,128)(2,1)}) %all-gather.3.cloned.1.call-update) | async-done | bytes 2097168 | tf_op jit(solution)/shard_map/all_gather | solution.py:61
  62.2 1.6 broadcast_in_dim.74
  63.8 0.0 copy-done.1
  63.8 0.0 copy-done.2
  63.8 21.7 %while.26 = (s32[]{:T(128)}, f32[8,128,512]{2,1,0:T(8,128)}, s32[12]{0:T(128)S(1)}, s32[]{:T(128)}, bf16[12,128,128]{2,1,0:T(8,128)(2,1)}, /*index=5*/s32[12]{0:...) while((s32[]{:T(128)}, f32[8,128,512]{2,1,0:T(8,128)}, ...), condition=%wide.region_2.3_spmd, body=%wide.region_0.2_spmd.sunk | while | flops 67437608 | bytes 5902635 | solution.py:30
  63.8 0.1 compare_select_fusion.6
  63.8 2.2 gather_fusion
  66.0 0.7 add_compare_fusion.4
  66.7 1.2 fusion.35
  67.9 3.1 scatter_fusion
  71.0 0.1 compare_select_fusion.6
  71.1 2.2 gather_fusion
  73.3 0.7 add_compare_fusion.4
  73.9 1.2 fusion.35
  75.2 3.1 scatter_fusion
  78.3 0.1 compare_select_fusion.6
  78.4 2.2 gather_fusion
  80.6 0.7 add_compare_fusion.4
  81.2 1.2 fusion.35
  82.5 3.0 scatter_fusion
  85.4 0.0 copy-start.3
  85.4 40.9 %all-reduce.4 = bf16[1024,512]{1,0:T(8,128)(2,1)S(1)} all-reduce(f32[1024,512]{1,0:T(8,128)} %bitcast.22), channel_id=1, replica_groups=mesh['row'=8,'col'=4] {'col'}, use_global_device_ids=true, to_apply=%region_3.4 | all-reduce | flops 524288 | bytes 3145728 | tf_op jit(solution)/shard_map/psum | solution.py:65
  126.3 0.0 all-gather.5.cloned.1.call-done
  126.4 0.0 copy-done
  126.4 0.0 copy-done.3
  126.4 4.6 %convert_reduce_fusion = (f32[512]{0:T(512)S(1)}, bf16[1024,512]{1,0:T(8,128)(2,1)S(1)}, f32[1024,512]{1,0:T(8,128)}, f32[1024,512]{1,0:T(8,128)}) fusion(bf16[1024,512]{1,0:T(8,128)(2,1)} %all-gather.5.cloned.1.call-done, f32[512]{0:T(512)S(1)} %copy-done.3, bf16[1024,512]{1,0:T(8,128)(2,1)S(1)} %all-reduce.4, bf16[512,512]{1,0:T(8,128)(2,1)S(1)} %copy-done), kind=kOutput, calls=%fused_computation.26 | convolution fusion | flops 543686144 | bytes 7868416 | tf_op jit(solution)/shard_map/dot_general | solution.py:35
  131.0 1.7 fusion.18
  132.7 0.7 convolution_convert_fusion
  133.4 0.0 all-reduce.3.cloned.1.call-update
  133.4 0.0 reduce-scatter.2.cloned.1.call-start
  133.5 2.5 broadcast_in_dim.75
  135.9 14.4 %while.27 = (s32[]{:T(128)}, f32[16,128,512]{2,1,0:T(8,128)}, s32[12]{0:T(128)S(1)}, s32[]{:T(128)}, bf16[12,128,128]{1,2,0:T(8,128)(2,1)S(1)}, /*index=5*/s32[1...) while((s32[]{:T(128)}, f32[16,128,512]{2,1,0:T(8,128)}, ...), condition=%wide.region_9.10_spmd, body=%wide.region_7.9_spmd.sunk | while | flops 67437608 | bytes 5903143 | solution.py:30
  136.0 0.1 compare_select_fusion.7
  136.0 0.6 gather_fusion.1
  136.6 0.7 add_compare_fusion.5
  137.3 0.3 fusion.38
  137.6 3.2 %scatter_fusion.1 = f32[16,128,512]{2,1,0:T(8,128)} fusion(f32[16,128,512]{2,1,0:T(8,128)} %get-tuple-element.436, s32[4]{0:T(128)S(1)} %get-tuple-element.389, f32[4,128,512]{2,1,0:T(8,128)S(1)} %fusion.38), kind=kCustom, calls=%fused_computation.3.clone.1 | custom fusion | flops 262144 | bytes 3145744 | tf_op jit(solution)/shard_map/while/body/eval_jaxpr/scatter-add | solution.py:27
  140.8 0.1 compare_select_fusion.7
  140.9 0.6 gather_fusion.1
  141.5 0.7 add_compare_fusion.5
  142.1 0.3 fusion.38
  142.5 3.2 %scatter_fusion.1 = f32[16,128,512]{2,1,0:T(8,128)} fusion(f32[16,128,512]{2,1,0:T(8,128)} %get-tuple-element.436, s32[4]{0:T(128)S(1)} %get-tuple-element.389, f32[4,128,512]{2,1,0:T(8,128)S(1)} %fusion.38), kind=kCustom, calls=%fused_computation.3.clone.1 | custom fusion | flops 262144 | bytes 3145744 | tf_op jit(solution)/shard_map/while/body/eval_jaxpr/scatter-add | solution.py:27
  145.6 0.1 compare_select_fusion.7
  145.7 0.6 gather_fusion.1
  146.3 0.7 add_compare_fusion.5
  147.0 0.3 fusion.38
  147.3 3.0 scatter_fusion.1
  150.3 0.0 reduce-scatter.2.cloned.1.call-update
  150.4 20.7 %psum.23 = f32[512]{0:T(512)S(1)} all-reduce(f32[512]{0:T(512)S(1)} %get-tuple-element.289), channel_id=1, replica_groups=mesh['row'=8,'col'=4] {'row'}, use_global_device_ids=true, to_apply=%region_6.7 | all-reduce | flops 512 | bytes 4096 | tf_op jit(solution)/shard_map/psum | solution.py:73
  171.0 2.0 fusion.14
  173.0 0.6 broadcast_multiply_fusion.1
  173.6 37.5 %all-reduce.3.cloned.1.call-done = f32[512,512]{1,0:T(8,128)} async-done(((f32[512,512]{1,0:T(8,128)}), f32[512,512]{1,0:T(8,128)}) %all-reduce.3.cloned.1.call-update) | async-done | bytes 1048592 | tf_op jit(solution)/shard_map/psum | solution.py:73
  211.1 2.3 broadcast_multiply_fusion
  213.4 89.3 %reduce-scatter.2.cloned.1.call-done = f32[256,512]{1,0:T(8,128)} async-done(((f32[2048,512]{1,0:T(8,128)}), f32[256,512]{1,0:T(8,128)}) %reduce-scatter.2.cloned.1.call-update) | async-done | bytes 524304 | tf_op jit(solution)/shard_map/reduce_scatter | solution.py:79
  302.7 1.8 convert_element_type.27
  (6 shorter events, 0.0 us)
Async XLA Ops:
  7.2 119.2 %copy-start = (bf16[512,512]{1,0:T(8,128)(2,1)S(1)}, bf16[512,512]{1,0:T(8,128)(2,1)}, u32[]{:S(2)}) copy-start(bf16[512,512]{1,0:T(8,128)(2,1)} %param.17) | copy-start | bytes 1572868
  7.2 56.6 %copy-start.1 = (s32[1,1,12]{2,1,0:T(1,128)S(1)}, s32[1,1,12]{2,1,0:T(1,128)}, u32[]{:S(2)}) copy-start(s32[1,1,12]{2,1,0:T(1,128)} %param.14) | copy-start | bytes 148
  7.2 56.6 %copy-start.2 = (s32[1,1,12]{2,1,0:T(1,128)S(1)}, s32[1,1,12]{2,1,0:T(1,128)}, u32[]{:S(2)}) copy-start(s32[1,1,12]{2,1,0:T(1,128)} %param.15) | copy-start | bytes 148
  7.2 55.0 %all-gather.3.cloned.1.call-start = ((), (), s32[]{:S(2)}) async-start(), calls=%async_computation.1 | async-start | bytes 2359296 | tf_op jit(solution)/shard_map/all_gather | solution.py:61
  7.9 118.4 %all-gather.5.cloned.1.call-start = ((), (), s32[]{:S(2)}) async-start(), calls=%async_computation.2 | async-start | bytes 1310720 | tf_op jit(solution)/shard_map/all_gather | solution.py:66
  8.7 202.4 %all-reduce.3.cloned.1.call-start = ((), (), s32[]{:S(2)}) async-start(), calls=%async_computation.3 | async-start | bytes 2097152 | tf_op jit(solution)/shard_map/psum | solution.py:73
  85.4 40.9 %copy-start.3 = (f32[512]{0:T(512)S(1)}, f32[512]{0:T(512)}, u32[]{:S(2)}) copy-start(f32[512]{0:T(512)} %param.18) | copy-start | bytes 6148
  133.4 169.3 %reduce-scatter.2.cloned.1.call-start = ((), (), s32[]{:S(2)}) async-start(), calls=%async_computation.4 | async-start | bytes 4718592 | tf_op jit(solution)/shard_map/reduce_scatter | solution.py:79
Sparse Core Ops, SparseCore 0:
  10.2 51.9 all-gather.2
  63.7 15.1 all-gather.4
  133.5 77.4 all-reduce.2
  215.0 87.6 reduce-scatter.1
where the time goes:
time: 312 us; the launch traced here: 311 us
  waiting for transfers between devices  180 us (58%)
  blocking collectives  61.6 us (20%)
  other arithmetic  29.6 us (9%)
  between operations  13.8 us (4%)
  local copies, waits for them, and re-layouts  13.5 us (4%)
  matrix products  11.8 us (4%)
    reduce_scatter x1, waiting for transfers between devices, shards(): lax.psum_scatter(grad_partial, 'row', scatter_dimension=0, tiled=True)  89.3 us
    all_gather x1, waiting for transfers between devices, shards(): gathered = lax.all_gather(features, 'row', axis=0, tiled=True)  52.2 us
    psum x1, blocking collectives, shards(): hidden_all = lax.psum(partial_value, 'col').astype(jnp.bfloat16)  40.9 us
    psum x1, waiting for transfers between devices, shards(): grad_weight, grad_bias = lax.psum((grad_weight, grad_bias), 'row')  37.5 us
    psum x1, blocking collectives, shards(): grad_weight, grad_bias = lax.psum((grad_weight, grad_bias), 'row')  20.7 us
    scatter-add x6, other arithmetic, one_turn(): return totals.at[put_now].add(product)  18.5 us
    gather x6, local copies, waits for them, and re-layouts, one_turn(): picked = source_blocks[take_now]  8.25 us
  transfers between devices with their start and end apart: 4, of which 3 were waited for; matrix products, arithmetic and copies ran while one was open for 15% of the time, Pallas kernels for 0%

commit v1 on v0

v1 whole, which is shorter than its diff:
```python
import math

import jax
import jax.numpy as jnp
from jax import lax
from jax.experimental import pallas as pl
from jax.experimental.pallas import tpu as pltpu
from jax.sharding import PartitionSpec as P

F32 = jnp.float32
BF16 = jnp.bfloat16
VMEM_LIMIT = 56 * 1024 * 1024
EXTRA_ROWS = 16


def vmem():
    return pl.BlockSpec(memory_space=pltpu.VMEM)


def smem():
    return pl.BlockSpec(memory_space=pltpu.SMEM)


def anywhere():
    return pl.BlockSpec(memory_space=pl.ANY)


def cost(flops, nbytes):
    return pl.CostEstimate(flops=int(flops), bytes_accessed=int(nbytes), transcendentals=0)


def params():
    return pltpu.CompilerParams(vmem_limit_bytes=VMEM_LIMIT)


def tree_sum(parts):
    while len(parts) > 1:
        half = len(parts) // 2
        parts = [parts[i] + parts[i + half] for i in range(half)]
    return parts[0]


class Layout:
    def __init__(self, row_size, col_size):
        self.rows, self.cols = row_size, col_size
        self.slow = math.gcd(row_size, 4)
        self.fast = row_size // self.slow
        self.cores = 2
        self.pairs = col_size // self.cores

    def move(self, a, slow=0, fast=0, pair=0, core=0):
        row = lambda r: ((r // self.fast + slow) % self.slow) * self.fast + (r % self.fast + fast) % self.fast
        col = lambda c: ((c // 2 + pair) % self.pairs) * 2 + (c % 2 + core) % 2
        if pair == 0 and core == 0:
            return lax.ppermute(a, "row", [(r, row(r)) for r in range(self.rows)])
        if slow == 0 and fast == 0:
            return lax.ppermute(a, "col", [(c, col(c)) for c in range(self.cols)])
        n = self.cols
        return lax.ppermute(
            a, ("row", "col"), [(r * n + c, row(r) * n + col(c)) for r in range(self.rows) for c in range(n)]
        )

    def position(self):
        r, c = lax.axis_index("row"), lax.axis_index("col")
        return r // self.fast, r % self.fast, c // 2, c % 2


def forward_product(lay, index_own, index_other, tiles_own, tiles_other, pieces, out_rows):
    slots, block, _ = tiles_own.shape
    _, node_dev, half = pieces[0].shape
    group = math.gcd(slots, 4)

    def kernel(io_ref, ix_ref, ao_ref, ax_ref, *refs):
        piece_refs, (out_ref, feats, total, sems) = refs[: lay.rows], refs[lay.rows :]
        z, y, _, _ = lay.position()
        copies = []
        for dz in range(lay.slow):
            for dy in range(lay.fast):
                at = lax.rem(z - dz + lay.slow, lay.slow) * lay.fast + lax.rem(y - dy + lay.fast, lay.fast)
                n = dz * lay.fast + dy
                copies.append(
                    pltpu.make_async_copy(
                        piece_refs[n],
                        feats.at[:, pl.ds(pl.multiple_of(at * node_dev, node_dev), node_dev), :],
                        sems.at[n],
                    )
                )
        for c in copies:
            c.start()
        total[...] = jnp.zeros_like(total)
        for c in copies:
            c.wait()
        for which, (idx, tiles) in enumerate(((io_ref, ao_ref), (ix_ref, ax_ref))):
            count = idx[2 * slots]

            def turn(g, carry, which=which, idx=idx, tiles=tiles, count=count):
                products = []
                for j in range(group):
                    s = g * group + j
                    at = pl.multiple_of(idx[slots + s] * block, block)
                    p = jnp.dot(tiles[s], feats[which, pl.ds(at, block), :], preferred_element_type=F32)
                    products.append(jnp.where(s < count, p, 0.0))
                for j, p in enumerate(products):
                    to = pl.multiple_of(idx[g * group + j] * block, block)
                    total[pl.ds(to, block), :] += p
                return carry

            lax.fori_loop(0, (count + group - 1) // group, turn, 0)
        out_ref[...] = total[...].astype(BF16)

    return pl.pallas_call(
        kernel,
        out_shape=jax.ShapeDtypeStruct((out_rows, half), BF16),
        in_specs=[smem(), smem(), vmem(), vmem()] + [anywhere()] * lay.rows,
        out_specs=vmem(),
        scratch_shapes=[
            pltpu.VMEM((2, lay.rows * node_dev, half), BF16),
            pltpu.VMEM((out_rows, half), F32),
            pltpu.SemaphoreType.DMA((lay.rows,)),
        ],
        compiler_params=params(),
        cost_estimate=cost(4 * slots * block * block * half, 4 * lay.rows * node_dev * half),
        name="forward_product",
    )(index_own, index_other, tiles_own, tiles_other, *pieces)


def dense_part(lay, hidden_own, hidden_other, weight, bias, ups):
    rows, half = hidden_own.shape
    width = weight.shape[0]
    node_dev = ups[0].shape[0]
    share = half // lay.pairs
    part = share // lay.fast

    def kernel(ho_ref, hx_ref, w_ref, b_ref, *refs):
        up_refs, refs = refs[: lay.cols], refs[lay.cols :]
        act_ref, dh_ref, refs = refs[0], refs[1], refs[2:]
        gw_refs, (up_all, gw, sems) = refs[: lay.fast], refs[lay.fast :]
        _, y, x, k = lay.position()
        copies = []
        for dx in range(lay.pairs):
            for dk in range(2):
                at = lax.rem(x - dx + lay.pairs, lay.pairs) * 2 + lax.rem(k + dk, 2)
                n = dx * 2 + dk
                copies.append(
                    pltpu.make_async_copy(
                        up_refs[n],
                        up_all.at[pl.ds(pl.multiple_of(at * node_dev, node_dev), node_dev), :],
                        sems.at[n],
                    )
                )
        for c in copies:
            c.start()
        for c in copies:
            c.wait()
        gb = jnp.zeros((1, width), F32)
        for j in range(lay.cols):
            sl = pl.ds(j * node_dev, node_dev)
            ho, hx = ho_ref[sl, :], hx_ref[sl, :]
            h = jnp.concatenate([jnp.where(k == 0, ho, hx), jnp.where(k == 0, hx, ho)], axis=1)
            pre = jnp.dot(h, w_ref[...], preferred_element_type=F32) + b_ref[...]
            sig = jax.nn.sigmoid(pre)

            @pl.when(x * 2 + k == j)
            def _(pre=pre, sig=sig):
                act_ref[...] = (pre * sig).astype(BF16)

            dpre = (up_all[sl, :].astype(F32) * sig * (1.0 + pre * (1.0 - sig))).astype(BF16)
            gb += jnp.sum(dpre.astype(F32), axis=0, keepdims=True)
            one = lax.dot_general(ho, dpre, (((0,), (0,)), ((), ())), preferred_element_type=F32)
            if j == 0:
                gw[...] = one
            else:
                gw[...] += one
            dh_ref[sl, :] = lax.dot_general(
                dpre, w_ref[...], (((1,), (1,)), ((), ())), preferred_element_type=F32
            ).astype(BF16)
        high = gb.astype(BF16).astype(F32)
        low = gb - high
        line = lax.broadcasted_iota(jnp.int32, (EXTRA_ROWS, width), 0)
        extra = jnp.where(line == 0, high, jnp.where(line == 1, low, 0.0)).astype(BF16)
        for dy in range(lay.fast):
            at = x * share + lax.rem(y + dy, lay.fast) * part
            gw_refs[dy][:part, :] = gw[pl.ds(pl.multiple_of(at, part), part), :].astype(BF16)
            gw_refs[dy][part:, :] = extra

    return pl.pallas_call(
        kernel,
        out_shape=[
            jax.ShapeDtypeStruct((node_dev, width), BF16),
            jax.ShapeDtypeStruct((rows, width), BF16),
        ]
        + [jax.ShapeDtypeStruct((part + EXTRA_ROWS, width), BF16)] * lay.fast,
        in_specs=[vmem()] * 4 + [anywhere()] * lay.cols,
        out_specs=[vmem()] * (2 + lay.fast),
        scratch_shapes=[
            pltpu.VMEM((rows, width), BF16),
            pltpu.VMEM((half, width), F32),
            pltpu.SemaphoreType.DMA((lay.cols,)),
        ],
        compiler_params=params(),
        cost_estimate=cost(5 * rows * width * width, 6 * rows * width),
        name="dense_part",
    )(hidden_own, hidden_other, weight, bias, *ups)


def backward_product(lay, index_own, tiles_own, dhidden, node_dev):
    slots, block, _ = tiles_own.shape
    rows, width = dhidden.shape
    group = math.gcd(slots, 4)

    def kernel(idx, tiles, dh_ref, *refs):
        out_refs, (total,) = refs[: lay.rows], refs[lay.rows :]
        z, y, _, _ = lay.position()
        total[...] = jnp.zeros_like(total)
        count = idx[2 * slots]

        def turn(g, carry):
            products = []
            for j in range(group):
                s = g * group + j
                at = pl.multiple_of(idx[s] * block, block)
                p = lax.dot_general(
                    tiles[s], dh_ref[pl.ds(at, block), :], (((0,), (0,)), ((), ())), preferred_element_type=F32
                )
                products.append(jnp.where(s < count, p, 0.0))
            for j, p in enumerate(products):
                to = pl.multiple_of(idx[slots + g * group + j] * block, block)
                total[pl.ds(to, block), :] += p
            return carry

        lax.fori_loop(0, (count + group - 1) // group, turn, 0)
        for dz in range(lay.slow):
            for dy in range(lay.fast):
                at = lax.rem(z + dz, lay.slow) * lay.fast + lax.rem(y + dy, lay.fast)
                out_refs[dz * lay.fast + dy][...] = total[
                    pl.ds(pl.multiple_of(at * node_dev, node_dev), node_dev), :
                ].astype(BF16)

    return pl.pallas_call(
        kernel,
        out_shape=[jax.ShapeDtypeStruct((node_dev, width), BF16)] * lay.rows,
        in_specs=[smem(), vmem(), vmem()],
        out_specs=[vmem()] * lay.rows,
        scratch_shapes=[pltpu.VMEM((lay.rows * node_dev, width), F32)],
        compiler_params=params(),
        cost_estimate=cost(2 * slots * block * block * width, 2 * lay.rows * node_dev * width),
        name="backward_product",
    )(index_own, tiles_own, dhidden)


def place_weight_gradient(lay, own, other, width):
    half = width // 2
    share = half // lay.pairs
    part = share // lay.fast

    def kernel(own_ref, other_ref, out_ref):
        _, y, x, k = lay.position()
        for dk, ref in enumerate((own_ref, other_ref)):
            for dx in range(lay.pairs):
                for dy in range(lay.fast):
                    n = dx * lay.fast + dy
                    at = (
                        lax.rem(k + dk, 2) * half
                        + lax.rem(x - dx + lay.pairs, lay.pairs) * share
                        + lax.rem(y - dy + lay.fast, lay.fast) * part
                    )
                    out_ref[pl.ds(pl.multiple_of(at, part), part), :] = ref[n * part : (n + 1) * part, :].astype(F32)

    return pl.pallas_call(
        kernel,
        out_shape=jax.ShapeDtypeStruct((width, width), F32),
        in_specs=[vmem(), vmem()],
        out_specs=vmem(),
        compiler_params=params(),
        cost_estimate=cost(width * width, 6 * width * width),
        name="place_weight_gradient",
    )(own, other)


def shards(features, blocks, block_rows, block_cols, block_count, weight, bias_vector, upstream):
    lay = Layout(lax.axis_size("row"), lax.axis_size("col"))
    node_dev, width = features.shape
    half = width // 2
    scale = 1.0 / math.sqrt(node_dev * lay.rows * lay.cols)
    tiles = blocks[0, 0]
    core = lax.axis_index("col") % 2

    index = jnp.concatenate([block_rows[0, 0], block_cols[0, 0], block_count[0]])
    low, high = features[:, :half], features[:, half:]
    keep = jnp.where(core == 0, low, high)
    give = jnp.where(core == 0, high, low)
    piece = jnp.stack([keep, lay.move(give, core=1)])
    index_other = lay.move(index, core=1)
    tiles_other = lay.move(tiles, core=1)

    gathered = {(0, 0): piece}
    for dz in [0] + [d for d in (1, 3, 2) if d < lay.slow]:
        if dz:
            gathered[dz, 0] = lay.move(piece, slow=dz)
        for dy in range(1, lay.fast):
            gathered[dz, dy] = lay.move(gathered[dz, 0], fast=dy)
    pieces = [gathered[dz, dy] for dz in range(lay.slow) for dy in range(lay.fast)]

    ups = [upstream, lay.move(upstream, core=1)]
    for dx in range(1, lay.pairs):
        ups.append(lay.move(upstream, pair=dx))
        ups.append(lay.move(ups[-1], core=1))

    partial_sum = forward_product(lay, index, index_other, tiles, tiles_other, pieces, node_dev * lay.cols)
    arrived = [partial_sum] + [lay.move(partial_sum, pair=dx) for dx in range(1, lay.pairs)]
    hidden_own = tree_sum([a.astype(F32) for a in arrived]).astype(BF16)
    hidden_other = lay.move(hidden_own, core=1)

    activated, dhidden, *gw_parts = dense_part(lay, hidden_own, hidden_other, weight, bias_vector[None], ups)

    gw = [gw_parts[0]] + [lay.move(gw_parts[dy], fast=dy) for dy in range(1, lay.fast)]
    gw_sum = tree_sum([g.astype(F32) for g in gw])
    gb_sum = gw_sum[-EXTRA_ROWS:]
    gb_line = gb_sum[0] + gb_sum[1]
    gb_high = gb_line.astype(BF16)
    gb_low = (gb_line - gb_high.astype(F32)).astype(BF16)
    line = jnp.arange(EXTRA_ROWS)[:, None]
    gb_rows = jnp.where(line == 0, gb_high[None], jnp.where(line == 1, gb_low[None], jnp.zeros((), BF16)))
    gw_send = jnp.concatenate([gw_sum[:-EXTRA_ROWS].astype(BF16), gb_rows])
    gw_all = tree_sum([g.astype(F32) for g in [gw_send] + [lay.move(gw_send, slow=dz) for dz in range(1, lay.slow)]])
    gw_all = gw_all * scale
    grad_bias = gw_all[-EXTRA_ROWS] + gw_all[1 - EXTRA_ROWS]
    gw_final = gw_all[:-EXTRA_ROWS].astype(BF16)
    shares = []
    for dx in range(lay.pairs):
        for dy in range(lay.fast):
            shares.append(gw_final if dx == 0 and dy == 0 else lay.move(gw_final, pair=dx, fast=dy))
    gw_own = jnp.concatenate(shares)
    grad_weight = place_weight_gradient(lay, gw_own, lay.move(gw_own, core=1), width)

    outs = backward_product(lay, index, tiles, dhidden, node_dev)
    sums = {}
    for dz in [d for d in (2, 1, 3, 0) if d < lay.slow]:
        s = outs[dz * lay.fast].astype(F32)
        for dy in range(1, lay.fast):
            s = s + lay.move(outs[dz * lay.fast + dy], fast=dy).astype(F32)
        sums[dz] = lay.move(s.astype(BF16), slow=dz).astype(F32) if dz else s
    grad = sums[0]
    for dz in range(1, lay.slow):
        grad = grad + sums[dz]
    return (activated, grad_weight, grad_bias, grad.astype(BF16))


def solution(mesh):
    in_specs = (
        P(("col", "row"), None),
        P("row", "col", None, None, None),
        P("row", "col", None),
        P("row", "col", None),
        P("row", "col"),
        P(),
        P(),
        P(("row", "col"), None),
    )
    out_specs = (P(("row", "col"), None), P(), P(), P(("col", "row"), None))
    return jax.shard_map(shards, mesh=mesh, in_specs=in_specs, out_specs=out_specs, check_vma=False)
```

time: 312 us -> 130 us (0.42)
  the two profiles are of different devices: /device:TPU:0 before, /device:TPU:9 now
where the time goes in v1:
time: 130 us; the launch traced here: 129 us
  waiting for transfers between devices  63.2 us (49%)
  starting transfers between devices  39.6 us (30%)
  Pallas kernels  16 us (12%)
  other arithmetic  5 us (4%)
  local copies, waits for them, and re-layouts  3.86 us (3%)
  between operations  1.63 us (1%)
    ppermute x19, waiting for transfers between devices, move(): return lax.ppermute(a, 'row', [(r, row(r)) for r in range(self.rows)])  50 us
    ppermute x19, starting transfers between devices, move(): return lax.ppermute(a, 'row', [(r, row(r)) for r in range(self.rows)])  19.5 us
    ppermute x10, starting transfers between devices, move(): return lax.ppermute(a, 'col', [(c, col(c)) for c in range(self.cols)])  19 us
    ppermute x10, waiting for transfers between devices, move(): return lax.ppermute(a, 'col', [(c, col(c)) for c in range(self.cols)])  13.2 us
    pallas_call x1, Pallas kernels, dense_part(): pl.pallas_call(kernel, out_shape=[jax.ShapeDtypeStruct((node_dev, width),...  6.46 us
    pallas_call x1, Pallas kernels, forward_product(): pl.pallas_call(kernel, out_shape=jax.ShapeDtypeStruct((out_rows, half), B...  4.03 us
    unnamed x56, local copies, waits for them, and re-layouts  3.83 us
    pallas_call x1, Pallas kernels, backward_product(): pl.pallas_call(kernel, out_shape=[jax.ShapeDtypeStruct((node_dev, width),...  3.46 us
  transfers between devices with their start and end apart: 30, of which 15 were waited for; matrix products, arithmetic and copies ran while one was open for 2% of the time, Pallas kernels for 4%

profile of v1, /device:TPU:9, one launch (start us, length us, event | category | flops | bytes accessed | tf_op | source)
XLA Modules:
  0.0 129.4 jit_solution(3725567839269121851)
XLA Ops:
  0.6 1.0 select_bitcast_fusion
  1.6 0.7 collective-permute-start.2
  2.4 1.0 collective-permute-done.2
  3.4 1.3 %collective-permute-start.4 = (bf16[2,256,256]{2,1,0:T(8,128)(2,1)S(1)}, bf16[2,256,256]{2,1,0:T(8,128)(2,1)S(1)}, u32[]{:S(2)}, u32[]{:S(2)}) collective-permute-start(bf16[2,256,256]{2,1,0:T(8,128)(2,1)S(1)} %pad_maximum_fusion.refs_0_), channel_id=1, source_target_pairs={{0,8},{4,12},{8,16},{12,20},{16,24},{20,28},{24,0},{28,4},{1,9},{5... | collective-permute-start | bytes 786440 | tf_op jit(solution)/shard_map/ppermute | solution.py:55
  4.8 1.1 collective-permute-start.6
  5.9 1.4 %collective-permute-start.8 = (bf16[2,256,256]{2,1,0:T(8,128)(2,1)S(1)}, bf16[2,256,256]{2,1,0:T(8,128)(2,1)S(1)}, u32[]{:S(2)}, u32[]{:S(2)}) collective-permute-start(bf16[2,256,256]{2,1,0:T(8,128)(2,1)S(1)} %pad_maximum_fusion.refs_0_), channel_id=1, source_target_pairs={{0,24},{4,28},{8,0},{12,4},{16,8},{20,12},{24,16},{28,20},{1,25},{... | collective-permute-start | bytes 786440 | tf_op jit(solution)/shard_map/ppermute | solution.py:55
  7.2 1.2 collective-permute-start.1
  9.1 0.6 copy-done.19
  9.8 0.0 copy-done.20
  9.8 0.1 pad_add_fusion.io_ref.idx
  9.9 0.0 collective-permute-start
  9.9 1.1 collective-permute-done.ix_ref
  11.0 1.2 collective-permute-start.3
  12.2 0.2 collective-permute-start.5
  12.5 14.5 %collective-permute-done.6.refs_4_ = bf16[2,256,256]{2,1,0:T(8,128)(2,1)S(1)} collective-permute-done((bf16[2,256,256]{2,1,0:T(8,128)(2,1)S(1)}, bf16[2,256,256]{2,1,0:T(8,128)(2,1)S(1)}, u32[]{:S(2)}, u32[]{:S(2)}) %collective-permute-start.6) | collective-permute-done | bytes 262176 | tf_op jit(solution)/shard_map/ppermute | solution.py:55
  27.0 1.2 collective-permute-start.7
  28.2 1.2 collective-permute-done.8.refs_6_
  29.4 1.2 collective-permute-start.9
  30.7 2.8 %collective-permute-done.7.refs_5_ = bf16[2,256,256]{2,1,0:T(8,128)(2,1)S(1)} collective-permute-done((bf16[2,256,256]{2,1,0:T(8,128)(2,1)S(1)}, bf16[2,256,256]{2,1,0:T(8,128)(2,1)S(1)}, u32[]{:S(2)}, u32[]{:S(2)}) %collective-permute-start.7) | collective-permute-done | bytes 262176 | tf_op jit(solution)/shard_map/ppermute | solution.py:55
  33.6 5.6 %collective-permute-done.9.refs_7_ = bf16[2,256,256]{2,1,0:T(8,128)(2,1)S(1)} collective-permute-done((bf16[2,256,256]{2,1,0:T(8,128)(2,1)S(1)}, bf16[2,256,256]{2,1,0:T(8,128)(2,1)S(1)}, u32[]{:S(2)}, u32[]{:S(2)}) %collective-permute-start.9) | collective-permute-done | bytes 262176 | tf_op jit(solution)/shard_map/ppermute | solution.py:55
  39.3 0.7 copy-done.14
  40.0 4.0 %forward_product.1 = bf16[1024,256]{1,0:T(8,128)(2,1)} custom-call(s32[25]{0:T(128)} %copy-done.17, s32[25]{0:T(128)} %copy-done.18, bf16[12,128,128]{2,1,0:T(8,128)(2,1)} %bitcast.10, bf16[12,128,128]{2,1,0:T(8,128)(2,1)} %copy-done.4, bf16[2,256,256]{2,1,0:T(8,128)(2,1)} %copy-done.1, bf16[2,256,256]{2,1,0:T(8,128)(2,1)} %copy-done.11, ...), custom_call_target="tpu_custom_call" | custom-call | flops 201326592 | bytes 2097152 | tf_op jit(solution)/shard_map/forward_product/pallas_call | solution.py:111
  44.0 1.5 %collective-permute-start.10 = (bf16[1024,256]{1,0:T(8,128)(2,1)}, bf16[1024,256]{1,0:T(8,128)(2,1)S(1)}, u32[]{:S(2)}, u32[]{:S(2)}) collective-permute-start(bf16[1024,256]{1,0:T(8,128)(2,1)} %forward_product.1), channel_id=1, source_target_pairs={{0,2},{1,3},{2,0},{3,1},{4,6},{5,7},{6,4},{7,5},{8,10},{9,11},{10,... | collective-permute-start | bytes 1572872 | tf_op jit(solution)/shard_map/ppermute | solution.py:57
  45.5 0.1 collective-permute-start.13
  45.6 10.0 %collective-permute-done.10 = bf16[1024,256]{1,0:T(8,128)(2,1)S(1)} collective-permute-done((bf16[1024,256]{1,0:T(8,128)(2,1)}, bf16[1024,256]{1,0:T(8,128)(2,1)S(1)}, u32[]{:S(2)}, u32[]{:S(2)}) %collective-permute-start.10) | collective-permute-done | bytes 524320 | tf_op jit(solution)/shard_map/ppermute | solution.py:57
  55.6 1.2 add_convert_fusion.ho_ref
  56.8 5.7 %collective-permute-start.11 = (bf16[1024,256]{1,0:T(8,128)(2,1)S(1)}, bf16[1024,256]{1,0:T(8,128)(2,1)S(1)}, u32[]{:S(2)}, u32[]{:S(2)}) collective-permute-start(bf16[1024,256]{1,0:T(8,128)(2,1)S(1)} %add_convert_fusion.ho_ref), channel_id=1, source_target_pairs={{0,1},{1,0},{2,3},{3,2},{4,5},{5,4},{6,7},{7,6},{8,9},{9,8},{10,11... | collective-permute-start | bytes 1572872 | tf_op jit(solution)/shard_map/ppermute | solution.py:57
  62.5 0.1 collective-permute-start.12
  62.6 1.6 %collective-permute-start.14 = (bf16[256,512]{1,0:T(8,128)(2,1)S(1)}, bf16[256,512]{1,0:T(8,128)(2,1)S(1)}, u32[]{:S(2)}, u32[]{:S(2)}) collective-permute-start(bf16[256,512]{1,0:T(8,128)(2,1)S(1)} %collective-permute-done.13.refs_2_), channel_id=1, source_target_pairs={{0,1},{1,0},{2,3},{3,2},{4,5},{5,4},{6,7},{7,6},{8,9},{9,8},{10,11... | collective-permute-start | bytes 786440 | tf_op jit(solution)/shard_map/ppermute | solution.py:57
  64.2 0.2 collective-permute-done.12.refs_1_
  64.4 1.0 collective-permute-done.14.refs_3_
  65.4 0.7 copy-done.27
  66.1 0.2 copy-done.21
  66.3 6.5 %dense_part.1 = (bf16[256,512]{1,0:T(8,128)(2,1)}, bf16[1024,512]{1,0:T(8,128)(2,1)}, bf16[80,512]{1,0:T(8,128)(2,1)}, bf16[80,512]{1,0:T(8,128)(2,1)}) custom-call(bf16[1024,256]{1,0:T(8,128)(2,1)} %copy-done.3, bf16[1024,256]{1,0:T(8,128)(2,1)} %copy-done.21, bf16[512,512]{1,0:T(8,128)(2,1)} %w_ref.1, f32[1,512]{1,0:T(1,128)} %bitcast.17, ...), custom_call_target="tpu_custom_call" | custom-call | flops 1342177280 | bytes 3145728 | tf_op jit(solution)/shard_map/dense_part/pallas_call | solution.py:186
  72.8 1.5 %collective-permute-start.15 = (bf16[80,512]{1,0:T(8,128)(2,1)}, bf16[80,512]{1,0:T(8,128)(2,1)S(1)}, u32[]{:S(2)}, u32[]{:S(2)}) collective-permute-start(bf16[80,512]{1,0:T(8,128)(2,1)} %get-tuple-element.18), channel_id=1, source_target_pairs={{0,4},{4,0},{8,12},{12,8},{16,20},{20,16},{24,28},{28,24},{1,5},{5... | collective-permute-start | bytes 245768 | tf_op jit(solution)/shard_map/ppermute | solution.py:55
  74.4 2.4 %collective-permute-done.15 = bf16[80,512]{1,0:T(8,128)(2,1)S(1)} collective-permute-done((bf16[80,512]{1,0:T(8,128)(2,1)}, bf16[80,512]{1,0:T(8,128)(2,1)S(1)}, u32[]{:S(2)}, u32[]{:S(2)}) %collective-permute-start.15) | collective-permute-done | bytes 81952 | tf_op jit(solution)/shard_map/ppermute | solution.py:55
  76.8 0.9 convert_add_fusion
  77.7 0.1 select_select_fusion
  77.8 3.6 %collective-permute-start.16 = (bf16[80,512]{1,0:T(8,128)(2,1)S(1)}, bf16[80,512]{1,0:T(8,128)(2,1)S(1)}, u32[]{:S(2)}, u32[]{:S(2)}) collective-permute-start(bf16[80,512]{1,0:T(8,128)(2,1)S(1)} %pad_maximum_fusion.2), channel_id=1, source_target_pairs={{0,16},{4,20},{8,24},{12,28},{16,0},{20,4},{24,8},{28,12},{1,17},{... | collective-permute-start | bytes 245768 | tf_op jit(solution)/shard_map/ppermute | solution.py:55
  81.4 1.5 %collective-permute-start.18 = (bf16[80,512]{1,0:T(8,128)(2,1)S(1)}, bf16[80,512]{1,0:T(8,128)(2,1)S(1)}, u32[]{:S(2)}, u32[]{:S(2)}) collective-permute-start(bf16[80,512]{1,0:T(8,128)(2,1)S(1)} %pad_maximum_fusion.2), channel_id=1, source_target_pairs={{0,24},{4,28},{8,0},{12,4},{16,8},{20,12},{24,16},{28,20},{1,25},{... | collective-permute-start | bytes 245768 | tf_op jit(solution)/shard_map/ppermute | solution.py:55
  82.9 3.5 %backward_product.1 = (bf16[256,512]{1,0:T(8,128)(2,1)}, bf16[256,512]{1,0:T(8,128)(2,1)}, bf16[256,512]{1,0:T(8,128)(2,1)}, bf16[256,512]{1,0:T(8,128)(2,1)}, b...) custom-call(s32[25]{0:T(128)} %copy-done.17, ...), custom_call_target="tpu_custom_call" | custom-call | flops 201326592 | bytes 2097152 | tf_op jit(solution)/shard_map/backward_product/pallas_call | solution.py:239
  86.3 0.8 collective-permute-start.24
  87.3 0.9 collective-permute-start.19
  88.2 1.1 collective-permute-start.20
  89.3 1.1 collective-permute-start.21
  90.4 0.5 collective-permute-start.26
  90.8 3.6 %collective-permute-done.19 = bf16[64,512]{1,0:T(8,128)(2,1)S(1)} collective-permute-done((bf16[64,512]{1,0:T(8,128)(2,1)S(1)}, bf16[64,512]{1,0:T(8,128)(2,1)S(1)}, u32[]{:S(2)}, u32[]{:S(2)}) %collective-permute-start.19) | collective-permute-done | bytes 65568 | tf_op jit(solution)/shard_map/ppermute | solution.py:55
  94.5 1.5 %collective-permute-start.23 = (bf16[256,512]{1,0:T(8,128)(2,1)S(1)}, bf16[256,512]{1,0:T(8,128)(2,1)S(1)}, u32[]{:S(2)}, u32[]{:S(2)}) collective-permute-start(bf16[256,512]{1,0:T(8,128)(2,1)S(1)} %copy-done.23), channel_id=1, source_target_pairs={{0,4},{4,0},{8,12},{12,8},{16,20},{20,16},{24,28},{28,24},{1,5},{5... | collective-permute-start | bytes 786440 | tf_op jit(solution)/shard_map/ppermute | solution.py:55
  96.0 6.9 %collective-permute-start.22 = (bf16[256,512]{1,0:T(8,128)(2,1)S(1)}, bf16[256,512]{1,0:T(8,128)(2,1)S(1)}, u32[]{:S(2)}, u32[]{:S(2)}) collective-permute-start(bf16[256,512]{1,0:T(8,128)(2,1)S(1)} %pad_maximum_fusion.1.own_ref), channel_id=1, source_target_pairs={{0,1},{1,0},{2,3},{3,2},{4,5},{5,4},{6,7},{7,6},{8,9},{9,8},{10,11... | collective-permute-start | bytes 786440 | tf_op jit(solution)/shard_map/ppermute | solution.py:57
  102.9 0.1 add_convert_fusion.4
  103.0 0.1 collective-permute-start.25
  103.1 0.8 copy-done.6
  103.9 0.1 add_convert_fusion.3
  103.9 1.1 collective-permute-start.27
  105.0 1.4 %collective-permute-done.28 = bf16[256,512]{1,0:T(8,128)(2,1)S(1)} collective-permute-done((bf16[256,512]{1,0:T(8,128)(2,1)S(1)}, bf16[256,512]{1,0:T(8,128)(2,1)S(1)}, u32[]{:S(2)}, u32[]{:S(2)}) %collective-permute-start.28) | collective-permute-done | bytes 262176 | tf_op jit(solution)/shard_map/ppermute | solution.py:55
  106.4 0.1 add_convert_fusion.2
  106.5 0.3 collective-permute-start.29
  106.8 0.6 slice_add_fusion
  107.4 0.7 copy-done.16
  108.1 2.1 %place_weight_gradient.1 = f32[512,512]{1,0:T(8,128)} custom-call(bf16[256,512]{1,0:T(8,128)(2,1)} %copy-done.2, bf16[256,512]{1,0:T(8,128)(2,1)} %copy-done.16), custom_call_target="tpu_custom_call" | custom-call | flops 262144 | bytes 1572864 | tf_op jit(solution)/shard_map/place_weight_gradient/pallas_call | solution.py:269
  110.2 1.8 %collective-permute-done.23 = bf16[256,512]{1,0:T(8,128)(2,1)S(1)} collective-permute-done((bf16[256,512]{1,0:T(8,128)(2,1)S(1)}, bf16[256,512]{1,0:T(8,128)(2,1)S(1)}, u32[]{:S(2)}, u32[]{:S(2)}) %collective-permute-start.23) | collective-permute-done | bytes 262176 | tf_op jit(solution)/shard_map/ppermute | solution.py:55
  112.0 13.4 %collective-permute-done.27 = bf16[256,512]{1,0:T(8,128)(2,1)S(1)} collective-permute-done((bf16[256,512]{1,0:T(8,128)(2,1)S(1)}, bf16[256,512]{1,0:T(8,128)(2,1)S(1)}, u32[]{:S(2)}, u32[]{:S(2)}) %collective-permute-start.27) | collective-permute-done | bytes 262176 | tf_op jit(solution)/shard_map/ppermute | solution.py:55
  125.4 3.1 %collective-permute-done.29 = bf16[256,512]{1,0:T(8,128)(2,1)S(1)} collective-permute-done((bf16[256,512]{1,0:T(8,128)(2,1)S(1)}, bf16[256,512]{1,0:T(8,128)(2,1)S(1)}, u32[]{:S(2)}, u32[]{:S(2)}) %collective-permute-start.29) | collective-permute-done | bytes 262176 | tf_op jit(solution)/shard_map/ppermute | solution.py:55
  128.5 0.9 add_convert_fusion.1
  (74 shorter events, 0.3 us)
Async XLA Ops:
  1.6 5.6 %copy-start = (bf16[1,1,12,128,128]{4,3,2,1,0:T(8,128)(2,1)S(1)}, bf16[1,1,12,128,128]{4,3,2,1,0:T(8,128)(2,1)}, u32[]{:S(2)}) copy-start(bf16[1,1,12,128,128]{4,3,2,1,0:T(8,128)(2,1)} %param.9) | copy-start | bytes 1179652
  1.6 1.7 %collective-permute-start.2 = (bf16[256,256]{1,0:T(8,128)(2,1)S(1)}, bf16[256,256]{1,0:T(8,128)(2,1)S(1)}, u32[]{:S(2)}, u32[]{:S(2)}) collective-permute-start(bf16[256,256]{1,0:T(8,128)(2,1)S(1)} %get-tuple-element.31), channel_id=1, source_target_pairs={{0,1},{1,0},{2,3},{3,2},{4,5},{5,4},{6,7},{7,6},{8,9},{9,8},{10,11... | collective-permute-start | bytes 393224 | tf_op jit(solution)/shard_map/ppermute | solution.py:57
  3.4 35.8 %copy-start.1 = (bf16[2,256,256]{2,1,0:T(8,128)(2,1)}, bf16[2,256,256]{2,1,0:T(8,128)(2,1)S(1)}, u32[]{:S(2)}) copy-start(bf16[2,256,256]{2,1,0:T(8,128)(2,1)S(1)} %pad_maximum_fusion.refs_0_) | copy-start | bytes 786436
  3.4 8.8 %collective-permute-start.4 = (bf16[2,256,256]{2,1,0:T(8,128)(2,1)S(1)}, bf16[2,256,256]{2,1,0:T(8,128)(2,1)S(1)}, u32[]{:S(2)}, u32[]{:S(2)}) collective-permute-start(bf16[2,256,256]{2,1,0:T(8,128)(2,1)S(1)} %pad_maximum_fusion.refs_0_), channel_id=1, source_target_pairs={{0,8},{4,12},{8,16},{12,20},{16,24},{20,28},{24,0},{28,4},{1,9},{5... | collective-permute-start | bytes 786440 | tf_op jit(solution)/shard_map/ppermute | solution.py:55
  4.8 22.2 %collective-permute-start.6 = (bf16[2,256,256]{2,1,0:T(8,128)(2,1)S(1)}, bf16[2,256,256]{2,1,0:T(8,128)(2,1)S(1)}, u32[]{:S(2)}, u32[]{:S(2)}) collective-permute-start(bf16[2,256,256]{2,1,0:T(8,128)(2,1)S(1)} %pad_maximum_fusion.refs_0_), channel_id=1, source_target_pairs={{0,16},{4,20},{8,24},{12,28},{16,0},{20,4},{24,8},{28,12},{1,17},{... | collective-permute-start | bytes 786440 | tf_op jit(solution)/shard_map/ppermute | solution.py:55
  5.9 23.6 %collective-permute-start.8 = (bf16[2,256,256]{2,1,0:T(8,128)(2,1)S(1)}, bf16[2,256,256]{2,1,0:T(8,128)(2,1)S(1)}, u32[]{:S(2)}, u32[]{:S(2)}) collective-permute-start(bf16[2,256,256]{2,1,0:T(8,128)(2,1)S(1)} %pad_maximum_fusion.refs_0_), channel_id=1, source_target_pairs={{0,24},{4,28},{8,0},{12,4},{16,8},{20,12},{24,16},{28,20},{1,25},{... | collective-permute-start | bytes 786440 | tf_op jit(solution)/shard_map/ppermute | solution.py:55
  7.2 23.4 %collective-permute-start.1 = (bf16[12,128,128]{2,1,0:T(8,128)(2,1)S(1)}, bf16[12,128,128]{2,1,0:T(8,128)(2,1)S(1)}, u32[]{:S(2)}, u32[]{:S(2)}) collective-permute-start(bf16[12,128,128]{2,1,0:T(8,128)(2,1)S(1)} %bitcast.12), channel_id=1, source_target_pairs={{0,1},{1,0},{2,3},{3,2},{4,5},{5,4},{6,7},{7,6},{8,9},{9,8},{10,11... | collective-permute-start | bytes 1179656 | tf_op jit(solution)/shard_map/ppermute | solution.py:57
  9.1 0.7 copy-start.19
  9.1 0.7 copy-start.20
  9.9 29.3 %copy-start.17 = (s32[25]{0:T(128)}, s32[25]{0:T(128)S(1)}, u32[]{:S(2)}) copy-start(s32[25]{0:T(128)S(1)} %pad_add_fusion.io_ref.idx) | copy-start | bytes 304
  9.9 35.7 %copy-start.22 = (bf16[256,512]{1,0:T(8,128)(2,1)S(1)}, bf16[256,512]{1,0:T(8,128)(2,1)}, u32[]{:S(2)}) copy-start(bf16[256,512]{1,0:T(8,128)(2,1)} %refs_0_.1) | copy-start | bytes 786436
  9.9 1.1 collective-permute-start
  11.0 28.2 %copy-start.18 = (s32[25]{0:T(128)}, s32[25]{0:T(128)S(1)}, u32[]{:S(2)}) copy-start(s32[25]{0:T(128)S(1)} %collective-permute-done.ix_ref) | copy-start | bytes 304
  11.0 19.7 %collective-permute-start.3 = (bf16[2,256,256]{2,1,0:T(8,128)(2,1)S(1)}, bf16[2,256,256]{2,1,0:T(8,128)(2,1)S(1)}, u32[]{:S(2)}, u32[]{:S(2)}) collective-permute-start(bf16[2,256,256]{2,1,0:T(8,128)(2,1)S(1)} %pad_maximum_fusion.refs_0_), channel_id=1, source_target_pairs={{0,4},{4,0},{8,12},{12,8},{16,20},{20,16},{24,28},{28,24},{1,5},{5... | collective-permute-start | bytes 786440 | tf_op jit(solution)/shard_map/ppermute | solution.py:55
  12.2 26.9 %copy-start.8 = (bf16[2,256,256]{2,1,0:T(8,128)(2,1)}, bf16[2,256,256]{2,1,0:T(8,128)(2,1)S(1)}, u32[]{:S(2)}) copy-start(bf16[2,256,256]{2,1,0:T(8,128)(2,1)S(1)} %collective-permute-done.4.refs_2_) | copy-start | bytes 786436
  12.2 18.5 %collective-permute-start.5 = (bf16[2,256,256]{2,1,0:T(8,128)(2,1)S(1)}, bf16[2,256,256]{2,1,0:T(8,128)(2,1)S(1)}, u32[]{:S(2)}, u32[]{:S(2)}) collective-permute-start(bf16[2,256,256]{2,1,0:T(8,128)(2,1)S(1)} %collective-permute-done.4.refs_2_), channel_id=1, source_target_pairs={{0,4},{4,0},{8,12},{12,8},{16,20},{20,16},{24,28},{28,24},{1,5},{5... | collective-permute-start | bytes 786440 | tf_op jit(solution)/shard_map/ppermute | solution.py:55
  26.9 12.3 %copy-start.9 = (bf16[2,256,256]{2,1,0:T(8,128)(2,1)}, bf16[2,256,256]{2,1,0:T(8,128)(2,1)S(1)}, u32[]{:S(2)}) copy-start(bf16[2,256,256]{2,1,0:T(8,128)(2,1)S(1)} %collective-permute-done.6.refs_4_) | copy-start | bytes 786436
  27.0 6.6 %collective-permute-start.7 = (bf16[2,256,256]{2,1,0:T(8,128)(2,1)S(1)}, bf16[2,256,256]{2,1,0:T(8,128)(2,1)S(1)}, u32[]{:S(2)}, u32[]{:S(2)}) collective-permute-start(bf16[2,256,256]{2,1,0:T(8,128)(2,1)S(1)} %collective-permute-done.6.refs_4_), channel_id=1, source_target_pairs={{0,4},{4,0},{8,12},{12,8},{16,20},{20,16},{24,28},{28,24},{1,5},{5... | collective-permute-start | bytes 786440 | tf_op jit(solution)/shard_map/ppermute | solution.py:55
  29.4 9.8 %copy-start.10 = (bf16[2,256,256]{2,1,0:T(8,128)(2,1)}, bf16[2,256,256]{2,1,0:T(8,128)(2,1)S(1)}, u32[]{:S(2)}) copy-start(bf16[2,256,256]{2,1,0:T(8,128)(2,1)S(1)} %collective-permute-done.8.refs_6_) | copy-start | bytes 786436
  29.4 9.7 %collective-permute-start.9 = (bf16[2,256,256]{2,1,0:T(8,128)(2,1)S(1)}, bf16[2,256,256]{2,1,0:T(8,128)(2,1)S(1)}, u32[]{:S(2)}, u32[]{:S(2)}) collective-permute-start(bf16[2,256,256]{2,1,0:T(8,128)(2,1)S(1)} %collective-permute-done.8.refs_6_), channel_id=1, source_target_pairs={{0,4},{4,0},{8,12},{12,8},{16,20},{20,16},{24,28},{28,24},{1,5},{5... | collective-permute-start | bytes 786440 | tf_op jit(solution)/shard_map/ppermute | solution.py:55
  30.7 8.5 %copy-start.11 = (bf16[2,256,256]{2,1,0:T(8,128)(2,1)}, bf16[2,256,256]{2,1,0:T(8,128)(2,1)S(1)}, u32[]{:S(2)}) copy-start(bf16[2,256,256]{2,1,0:T(8,128)(2,1)S(1)} %collective-permute-done.3.refs_1_) | copy-start | bytes 786436
  30.7 8.5 %copy-start.4 = (bf16[12,128,128]{2,1,0:T(8,128)(2,1)}, bf16[12,128,128]{2,1,0:T(8,128)(2,1)S(1)}, u32[]{:S(2)}) copy-start(bf16[12,128,128]{2,1,0:T(8,128)(2,1)S(1)} %collective-permute-done.1.ax_ref) | copy-start | bytes 1179652
  30.7 8.5 %copy-start.12 = (bf16[2,256,256]{2,1,0:T(8,128)(2,1)}, bf16[2,256,256]{2,1,0:T(8,128)(2,1)S(1)}, u32[]{:S(2)}) copy-start(bf16[2,256,256]{2,1,0:T(8,128)(2,1)S(1)} %collective-permute-done.5.refs_3_) | copy-start | bytes 786436
  33.6 5.7 %copy-start.13 = (bf16[2,256,256]{2,1,0:T(8,128)(2,1)}, bf16[2,256,256]{2,1,0:T(8,128)(2,1)S(1)}, u32[]{:S(2)}) copy-start(bf16[2,256,256]{2,1,0:T(8,128)(2,1)S(1)} %collective-permute-done.7.refs_5_) | copy-start | bytes 786436
  39.3 0.7 copy-start.14
  44.0 11.6 %collective-permute-start.10 = (bf16[1024,256]{1,0:T(8,128)(2,1)}, bf16[1024,256]{1,0:T(8,128)(2,1)S(1)}, u32[]{:S(2)}, u32[]{:S(2)}) collective-permute-start(bf16[1024,256]{1,0:T(8,128)(2,1)} %forward_product.1), channel_id=1, source_target_pairs={{0,2},{1,3},{2,0},{3,1},{4,6},{5,7},{6,4},{7,5},{8,10},{9,11},{10,... | collective-permute-start | bytes 1572872 | tf_op jit(solution)/shard_map/ppermute | solution.py:57
  45.5 17.1 %collective-permute-start.13 = (bf16[256,512]{1,0:T(8,128)(2,1)S(1)}, bf16[256,512]{1,0:T(8,128)(2,1)S(1)}, u32[]{:S(2)}, u32[]{:S(2)}) collective-permute-start(bf16[256,512]{1,0:T(8,128)(2,1)S(1)} %copy-done.22), channel_id=1, source_target_pairs={{0,2},{1,3},{2,0},{3,1},{4,6},{5,7},{6,4},{7,5},{8,10},{9,11},{10,... | collective-permute-start | bytes 786440 | tf_op jit(solution)/shard_map/ppermute | solution.py:57
  56.8 8.7 %copy-start.3 = (bf16[1024,256]{1,0:T(8,128)(2,1)}, bf16[1024,256]{1,0:T(8,128)(2,1)S(1)}, u32[]{:S(2)}) copy-start(bf16[1024,256]{1,0:T(8,128)(2,1)S(1)} %add_convert_fusion.ho_ref) | copy-start | bytes 1572868
  56.8 8.6 %collective-permute-start.11 = (bf16[1024,256]{1,0:T(8,128)(2,1)S(1)}, bf16[1024,256]{1,0:T(8,128)(2,1)S(1)}, u32[]{:S(2)}, u32[]{:S(2)}) collective-permute-start(bf16[1024,256]{1,0:T(8,128)(2,1)S(1)} %add_convert_fusion.ho_ref), channel_id=1, source_target_pairs={{0,1},{1,0},{2,3},{3,2},{4,5},{5,4},{6,7},{7,6},{8,9},{9,8},{10,11... | collective-permute-start | bytes 1572872 | tf_op jit(solution)/shard_map/ppermute | solution.py:57
  62.5 1.9 %collective-permute-start.12 = (bf16[256,512]{1,0:T(8,128)(2,1)S(1)}, bf16[256,512]{1,0:T(8,128)(2,1)S(1)}, u32[]{:S(2)}, u32[]{:S(2)}) collective-permute-start(bf16[256,512]{1,0:T(8,128)(2,1)S(1)} %copy-done.22), channel_id=1, source_target_pairs={{0,1},{1,0},{2,3},{3,2},{4,5},{5,4},{6,7},{7,6},{8,9},{9,8},{10,11... | collective-permute-start | bytes 786440 | tf_op jit(solution)/shard_map/ppermute | solution.py:57
  62.6 2.8 %copy-start.25 = (bf16[256,512]{1,0:T(8,128)(2,1)}, bf16[256,512]{1,0:T(8,128)(2,1)S(1)}, u32[]{:S(2)}) copy-start(bf16[256,512]{1,0:T(8,128)(2,1)S(1)} %collective-permute-done.13.refs_2_) | copy-start | bytes 786436
  62.6 2.8 %collective-permute-start.14 = (bf16[256,512]{1,0:T(8,128)(2,1)S(1)}, bf16[256,512]{1,0:T(8,128)(2,1)S(1)}, u32[]{:S(2)}, u32[]{:S(2)}) collective-permute-start(bf16[256,512]{1,0:T(8,128)(2,1)S(1)} %collective-permute-done.13.refs_2_), channel_id=1, source_target_pairs={{0,1},{1,0},{2,3},{3,2},{4,5},{5,4},{6,7},{7,6},{8,9},{9,8},{10,11... | collective-permute-start | bytes 786440 | tf_op jit(solution)/shard_map/ppermute | solution.py:57
  64.4 1.0 copy-start.26
  65.4 0.7 copy-start.27
  65.4 0.9 copy-start.21
  72.8 4.0 %collective-permute-start.15 = (bf16[80,512]{1,0:T(8,128)(2,1)}, bf16[80,512]{1,0:T(8,128)(2,1)S(1)}, u32[]{:S(2)}, u32[]{:S(2)}) collective-permute-start(bf16[80,512]{1,0:T(8,128)(2,1)} %get-tuple-element.18), channel_id=1, source_target_pairs={{0,4},{4,0},{8,12},{12,8},{16,20},{20,16},{24,28},{28,24},{1,5},{5... | collective-permute-start | bytes 245768 | tf_op jit(solution)/shard_map/ppermute | solution.py:55
  77.8 9.4 %collective-permute-start.16 = (bf16[80,512]{1,0:T(8,128)(2,1)S(1)}, bf16[80,512]{1,0:T(8,128)(2,1)S(1)}, u32[]{:S(2)}, u32[]{:S(2)}) collective-permute-start(bf16[80,512]{1,0:T(8,128)(2,1)S(1)} %pad_maximum_fusion.2), channel_id=1, source_target_pairs={{0,16},{4,20},{8,24},{12,28},{16,0},{20,4},{24,8},{28,12},{1,17},{... | collective-permute-start | bytes 245768 | tf_op jit(solution)/shard_map/ppermute | solution.py:55
  81.4 5.8 %collective-permute-start.17 = (bf16[80,512]{1,0:T(8,128)(2,1)S(1)}, bf16[80,512]{1,0:T(8,128)(2,1)S(1)}, u32[]{:S(2)}, u32[]{:S(2)}) collective-permute-start(bf16[80,512]{1,0:T(8,128)(2,1)S(1)} %pad_maximum_fusion.2), channel_id=1, source_target_pairs={{0,8},{4,12},{8,16},{12,20},{16,24},{20,28},{24,0},{28,4},{1,9},{5... | collective-permute-start | bytes 245768 | tf_op jit(solution)/shard_map/ppermute | solution.py:55
  81.4 5.8 %collective-permute-start.18 = (bf16[80,512]{1,0:T(8,128)(2,1)S(1)}, bf16[80,512]{1,0:T(8,128)(2,1)S(1)}, u32[]{:S(2)}, u32[]{:S(2)}) collective-permute-start(bf16[80,512]{1,0:T(8,128)(2,1)S(1)} %pad_maximum_fusion.2), channel_id=1, source_target_pairs={{0,24},{4,28},{8,0},{12,4},{16,8},{20,12},{24,16},{28,20},{1,25},{... | collective-permute-start | bytes 245768 | tf_op jit(solution)/shard_map/ppermute | solution.py:55
  86.3 8.1 %copy-start.24 = (bf16[256,512]{1,0:T(8,128)(2,1)S(1)}, bf16[256,512]{1,0:T(8,128)(2,1)}, u32[]{:S(2)}) copy-start(bf16[256,512]{1,0:T(8,128)(2,1)} %get-tuple-element.27) | copy-start | bytes 786436
  86.3 8.1 %copy-start.23 = (bf16[256,512]{1,0:T(8,128)(2,1)S(1)}, bf16[256,512]{1,0:T(8,128)(2,1)}, u32[]{:S(2)}) copy-start(bf16[256,512]{1,0:T(8,128)(2,1)} %get-tuple-element.21) | copy-start | bytes 786436
  86.3 16.6 %collective-permute-start.24 = (bf16[256,512]{1,0:T(8,128)(2,1)}, bf16[256,512]{1,0:T(8,128)(2,1)S(1)}, u32[]{:S(2)}, u32[]{:S(2)}) collective-permute-start(bf16[256,512]{1,0:T(8,128)(2,1)} %get-tuple-element.23), channel_id=1, source_target_pairs={{0,4},{4,0},{8,12},{12,8},{16,20},{20,16},{24,28},{28,24},{1,5},{5... | collective-permute-start | bytes 786440 | tf_op jit(solution)/shard_map/ppermute | solution.py:55
  87.3 7.2 %collective-permute-start.19 = (bf16[64,512]{1,0:T(8,128)(2,1)S(1)}, bf16[64,512]{1,0:T(8,128)(2,1)S(1)}, u32[]{:S(2)}, u32[]{:S(2)}) collective-permute-start(bf16[64,512]{1,0:T(8,128)(2,1)S(1)} %slice.61), channel_id=1, source_target_pairs={{0,4},{4,0},{8,12},{12,8},{16,20},{20,16},{24,28},{28,24},{1,5},{5... | collective-permute-start | bytes 196616 | tf_op jit(solution)/shard_map/ppermute | solution.py:55
  88.2 6.3 %collective-permute-start.20 = (bf16[64,512]{1,0:T(8,128)(2,1)S(1)}, bf16[64,512]{1,0:T(8,128)(2,1)S(1)}, u32[]{:S(2)}, u32[]{:S(2)}) collective-permute-start(bf16[64,512]{1,0:T(8,128)(2,1)S(1)} %slice.61), channel_id=1, source_target_pairs={{0,2},{1,3},{2,0},{3,1},{4,6},{5,7},{6,4},{7,5},{8,10},{9,11},{10,... | collective-permute-start | bytes 196616 | tf_op jit(solution)/shard_map/ppermute | solution.py:57
  89.3 6.7 %collective-permute-start.21 = (bf16[64,512]{1,0:T(8,128)(2,1)S(1)}, bf16[64,512]{1,0:T(8,128)(2,1)S(1)}, u32[]{:S(2)}, u32[]{:S(2)}) collective-permute-start(bf16[64,512]{1,0:T(8,128)(2,1)S(1)} %slice.61), channel_id=1, source_target_pairs={{0,6},{1,7},{2,4},{3,5},{4,2},{5,3},{6,0},{7,1},{8,14},{9,15},{10,... | collective-permute-start | bytes 196616 | tf_op jit(solution)/shard_map/ppermute | solution.py:59
  90.4 12.7 %collective-permute-start.26 = (bf16[256,512]{1,0:T(8,128)(2,1)}, bf16[256,512]{1,0:T(8,128)(2,1)S(1)}, u32[]{:S(2)}, u32[]{:S(2)}) collective-permute-start(bf16[256,512]{1,0:T(8,128)(2,1)} %get-tuple-element.25), channel_id=1, source_target_pairs={{0,4},{4,0},{8,12},{12,8},{16,20},{20,16},{24,28},{28,24},{1,5},{5... | collective-permute-start | bytes 786440 | tf_op jit(solution)/shard_map/ppermute | solution.py:55
  94.5 11.9 %collective-permute-start.28 = (bf16[256,512]{1,0:T(8,128)(2,1)S(1)}, bf16[256,512]{1,0:T(8,128)(2,1)S(1)}, u32[]{:S(2)}, u32[]{:S(2)}) collective-permute-start(bf16[256,512]{1,0:T(8,128)(2,1)S(1)} %copy-done.24), channel_id=1, source_target_pairs={{0,4},{4,0},{8,12},{12,8},{16,20},{20,16},{24,28},{28,24},{1,5},{5... | collective-permute-start | bytes 786440 | tf_op jit(solution)/shard_map/ppermute | solution.py:55
  94.5 8.4 %copy-start.7 = (bf16[256,512]{1,0:T(8,128)(2,1)S(1)}, bf16[256,512]{1,0:T(8,128)(2,1)}, u32[]{:S(2)}) copy-start(bf16[256,512]{1,0:T(8,128)(2,1)} %get-tuple-element.22) | copy-start | bytes 786436
  94.5 17.5 %collective-permute-start.23 = (bf16[256,512]{1,0:T(8,128)(2,1)S(1)}, bf16[256,512]{1,0:T(8,128)(2,1)S(1)}, u32[]{:S(2)}, u32[]{:S(2)}) collective-permute-start(bf16[256,512]{1,0:T(8,128)(2,1)S(1)} %copy-done.23), channel_id=1, source_target_pairs={{0,4},{4,0},{8,12},{12,8},{16,20},{20,16},{24,28},{28,24},{1,5},{5... | collective-permute-start | bytes 786440 | tf_op jit(solution)/shard_map/ppermute | solution.py:55
  96.0 7.0 %copy-start.2 = (bf16[256,512]{1,0:T(8,128)(2,1)}, bf16[256,512]{1,0:T(8,128)(2,1)S(1)}, u32[]{:S(2)}) copy-start(bf16[256,512]{1,0:T(8,128)(2,1)S(1)} %pad_maximum_fusion.1.own_ref) | copy-start | bytes 786436
  96.0 11.3 %collective-permute-start.22 = (bf16[256,512]{1,0:T(8,128)(2,1)S(1)}, bf16[256,512]{1,0:T(8,128)(2,1)S(1)}, u32[]{:S(2)}, u32[]{:S(2)}) collective-permute-start(bf16[256,512]{1,0:T(8,128)(2,1)S(1)} %pad_maximum_fusion.1.own_ref), channel_id=1, source_target_pairs={{0,1},{1,0},{2,3},{3,2},{4,5},{5,4},{6,7},{7,6},{8,9},{9,8},{10,11... | collective-permute-start | bytes 786440 | tf_op jit(solution)/shard_map/ppermute | solution.py:57
  102.9 1.0 copy-start.6
  103.0 9.0 %collective-permute-start.25 = (bf16[256,512]{1,0:T(8,128)(2,1)S(1)}, bf16[256,512]{1,0:T(8,128)(2,1)S(1)}, u32[]{:S(2)}, u32[]{:S(2)}) collective-permute-start(bf16[256,512]{1,0:T(8,128)(2,1)S(1)} %add_convert_fusion.4), channel_id=1, source_target_pairs={{0,8},{4,12},{8,16},{12,20},{16,24},{20,28},{24,0},{28,4},{1,9},{5... | collective-permute-start | bytes 786440 | tf_op jit(solution)/shard_map/ppermute | solution.py:55
  103.9 2.5 %copy-start.5 = (bf16[256,512]{1,0:T(8,128)(2,1)S(1)}, bf16[256,512]{1,0:T(8,128)(2,1)}, u32[]{:S(2)}) copy-start(bf16[256,512]{1,0:T(8,128)(2,1)} %get-tuple-element.26) | copy-start | bytes 786436
  103.9 21.5 %collective-permute-start.27 = (bf16[256,512]{1,0:T(8,128)(2,1)S(1)}, bf16[256,512]{1,0:T(8,128)(2,1)S(1)}, u32[]{:S(2)}, u32[]{:S(2)}) collective-permute-start(bf16[256,512]{1,0:T(8,128)(2,1)S(1)} %add_convert_fusion.3), channel_id=1, source_target_pairs={{0,16},{4,20},{8,24},{12,28},{16,0},{20,4},{24,8},{28,12},{1,17},{... | collective-permute-start | bytes 786440 | tf_op jit(solution)/shard_map/ppermute | solution.py:55
  106.5 22.0 %collective-permute-start.29 = (bf16[256,512]{1,0:T(8,128)(2,1)S(1)}, bf16[256,512]{1,0:T(8,128)(2,1)S(1)}, u32[]{:S(2)}, u32[]{:S(2)}) collective-permute-start(bf16[256,512]{1,0:T(8,128)(2,1)S(1)} %add_convert_fusion.2), channel_id=1, source_target_pairs={{0,24},{4,28},{8,0},{12,4},{16,8},{20,12},{24,16},{28,20},{1,25},{... | collective-permute-start | bytes 786440 | tf_op jit(solution)/shard_map/ppermute | solution.py:55
  107.4 21.1 %copy-start.15 = (bf16[256,512]{1,0:T(8,128)(2,1)S(1)}, bf16[256,512]{1,0:T(8,128)(2,1)}, u32[]{:S(2)}) copy-start(bf16[256,512]{1,0:T(8,128)(2,1)} %get-tuple-element.20) | copy-start | bytes 786436
  107.4 0.7 copy-start.16

commit v2 on v1

v2 whole, which is shorter than its diff:
```python
import math

import jax
import jax.numpy as jnp
from jax import lax
from jax.experimental import pallas as pl
from jax.experimental.pallas import tpu as pltpu
from jax.sharding import PartitionSpec as P

F32 = jnp.float32
BF16 = jnp.bfloat16
VMEM_LIMIT = 40 * 1024 * 1024
EXTRA_ROWS = 16


def vmem():
    return pl.BlockSpec(memory_space=pltpu.VMEM)


def smem():
    return pl.BlockSpec(memory_space=pltpu.SMEM)


def hbm():
    return pl.BlockSpec(memory_space=pl.ANY)


def cost(flops, nbytes):
    return pl.CostEstimate(flops=int(flops), bytes_accessed=int(nbytes), transcendentals=0)


def params():
    return pltpu.CompilerParams(vmem_limit_bytes=VMEM_LIMIT)


def xor_to(index, distance):
    return lax.bitwise_xor(index, jnp.int32(distance))


def tree_sum(parts):
    while len(parts) > 1:
        half = len(parts) // 2
        parts = [parts[i] + parts[i + half] for i in range(half)]
    return parts[0]


class Layout:
    def __init__(self, row_size, col_size):
        self.rows, self.cols = row_size, col_size
        self.slow = math.gcd(row_size, 4)
        self.fast = row_size // self.slow
        self.pairs = col_size // 2
        assert row_size & (row_size - 1) == 0 and col_size & (col_size - 1) == 0 and col_size > 1

    def move_row(self, a, slow=0, fast=0):
        d = slow * self.fast + fast
        return lax.ppermute(a, "row", [(r, r ^ d) for r in range(self.rows)])

    def move_col(self, a, pair=0, core=0):
        d = pair * 2 + core
        return lax.ppermute(a, "col", [(c, c ^ d) for c in range(self.cols)])


def forward_product(lay, index_own, index_other, tiles_own, tiles_other, pieces, out_rows):
    slots, block, _ = tiles_own.shape
    _, node_dev, half = pieces[0].shape
    group = math.gcd(slots, 4)

    def kernel(io_ref, ix_ref, ao_ref, ax_ref, *refs):
        piece_refs, (out_a, out_b, feats, total, sems) = refs[: lay.rows], refs[lay.rows :]
        row = lax.axis_index("row")
        copies = []
        for d in range(lay.rows):
            at = pl.multiple_of(xor_to(row, d) * node_dev, node_dev)
            copies.append(pltpu.make_async_copy(piece_refs[d], feats.at[:, pl.ds(at, node_dev), :], sems.at[d]))
        for c in copies:
            c.start()
        total[...] = jnp.zeros_like(total)
        for c in copies:
            c.wait()
        for which, (idx, tiles) in enumerate(((io_ref, ao_ref), (ix_ref, ax_ref))):
            count = idx[2 * slots]

            def turn(g, carry, which=which, idx=idx, tiles=tiles, count=count):
                products = []
                for j in range(group):
                    s = g * group + j
                    at = pl.multiple_of(idx[slots + s] * block, block)
                    p = jnp.dot(tiles[s], feats[which, pl.ds(at, block), :], preferred_element_type=F32)
                    products.append(jnp.where(s < count, p, 0.0))
                for j, p in enumerate(products):
                    to = pl.multiple_of(idx[g * group + j] * block, block)
                    total[pl.ds(to, block), :] += p
                return carry

            lax.fori_loop(0, (count + group - 1) // group, turn, 0)
        out_a[...] = total[: out_rows // 2, :].astype(BF16)
        out_b[...] = total[out_rows // 2 :, :].astype(BF16)

    return pl.pallas_call(
        kernel,
        out_shape=[jax.ShapeDtypeStruct((out_rows // 2, half), BF16)] * 2,
        in_specs=[smem(), smem(), vmem(), vmem()] + [hbm()] * lay.rows,
        out_specs=[vmem()] * 2,
        scratch_shapes=[
            pltpu.VMEM((2, lay.rows * node_dev, half), BF16),
            pltpu.VMEM((out_rows, half), F32),
            pltpu.SemaphoreType.DMA((lay.rows,)),
        ],
        compiler_params=params(),
        cost_estimate=cost(4 * slots * block * block * half, 4 * lay.rows * node_dev * half),
        name="forward_product",
    )(index_own, index_other, tiles_own, tiles_other, *pieces)


def dense_and_backward(lay, sums, weight, bias, index_own, tiles_own, ups):
    node_dev, width = ups[0].shape
    rows, half = node_dev * lay.cols, width // 2
    share = half // lay.pairs
    slots, block, _ = tiles_own.shape
    group = math.gcd(slots, 4)

    n_sums = len(sums)

    def kernel(w_ref, b_ref, idx, tiles, *refs):
        up_refs, sum_refs, refs = refs[: lay.cols], refs[lay.cols :][:n_sums], refs[lay.cols + n_sums :]
        act_ref, gw_ref, refs = refs[0], refs[1], refs[2:]
        out_refs, (up_all, parts, hidden, gw, dh_ref, total, sems) = refs[: lay.rows], refs[lay.rows :]
        row, col = lax.axis_index("row"), lax.axis_index("col")
        pair, core = col // 2, lax.rem(col, 2)
        copies = []
        for d in range(lay.cols):
            at = pl.multiple_of(xor_to(col, d) * node_dev, node_dev)
            copies.append(pltpu.make_async_copy(up_refs[d], up_all.at[pl.ds(at, node_dev), :], sems.at[d]))
        for n, ref in enumerate(sum_refs):
            part, dk, dx = n % 2, n // 2 % 2, n // 4
            at = pl.multiple_of(xor_to(core, dk) * half, half)
            to = parts.at[dx, pl.ds(part * (rows // 2), rows // 2), pl.ds(at, half)]
            copies.append(pltpu.make_async_copy(ref, to, sems.at[lay.cols + n]))
        for c in copies:
            c.start()
        total[...] = jnp.zeros_like(total)
        for c in copies:
            c.wait()
        own_half = pl.ds(pl.multiple_of(core * half, half), half)
        gb = jnp.zeros((1, width), F32)
        for j in range(lay.cols):
            sl = pl.ds(j * node_dev, node_dev)
            h = tree_sum([parts[dx, sl, :].astype(F32) for dx in range(lay.pairs)]).astype(BF16)
            hidden[sl, :] = h
            pre = jnp.dot(h, w_ref[...], preferred_element_type=F32) + b_ref[...]
            sig = jax.nn.sigmoid(pre)

            @pl.when(col == j)
            def _(pre=pre, sig=sig):
                act_ref[...] = (pre * sig).astype(BF16)

            dpre = (up_all[sl, :].astype(F32) * sig * (1.0 + pre * (1.0 - sig))).astype(BF16)
            gb += jnp.sum(dpre.astype(F32), axis=0, keepdims=True)
            one = lax.dot_general(hidden[sl, own_half], dpre, (((0,), (0,)), ((), ())), preferred_element_type=F32)
            if j == 0:
                gw[...] = one
            else:
                gw[...] += one
            dh_ref[sl, :] = lax.dot_general(
                dpre, w_ref[...], (((1,), (1,)), ((), ())), preferred_element_type=F32
            ).astype(BF16)
        high = gb.astype(BF16).astype(F32)
        low = gb - high
        line = lax.broadcasted_iota(jnp.int32, (EXTRA_ROWS, width), 0)
        extra = jnp.where(line == 0, high, jnp.where(line == 1, low, 0.0)).astype(BF16)
        gw_ref[:share, :] = gw[pl.ds(pl.multiple_of(pair * share, share), share), :].astype(BF16)
        gw_ref[share:, :] = extra

        count = idx[2 * slots]

        def turn(g, carry):
            products = []
            for j in range(group):
                s = g * group + j
                at = pl.multiple_of(idx[s] * block, block)
                p = lax.dot_general(
                    tiles[s], dh_ref[pl.ds(at, block), :], (((0,), (0,)), ((), ())), preferred_element_type=F32
                )
                products.append(jnp.where(s < count, p, 0.0))
            for j, p in enumerate(products):
                to = pl.multiple_of(idx[slots + g * group + j] * block, block)
                total[pl.ds(to, block), :] += p
            return carry

        lax.fori_loop(0, (count + group - 1) // group, turn, 0)
        for d in range(lay.rows):
            at = pl.multiple_of(xor_to(row, d) * node_dev, node_dev)
            out_refs[d][...] = total[pl.ds(at, node_dev), :].astype(BF16)

    return pl.pallas_call(
        kernel,
        out_shape=[
            jax.ShapeDtypeStruct((node_dev, width), BF16),
            jax.ShapeDtypeStruct((share + EXTRA_ROWS, width), BF16),
        ]
        + [jax.ShapeDtypeStruct((node_dev, width), BF16)] * lay.rows,
        in_specs=[vmem(), vmem(), smem(), vmem()] + [hbm()] * (lay.cols + n_sums),
        out_specs=[vmem()] * (2 + lay.rows),
        scratch_shapes=[
            pltpu.VMEM((rows, width), BF16),
            pltpu.VMEM((lay.pairs, rows, width), BF16),
            pltpu.VMEM((rows, width), BF16),
            pltpu.VMEM((half, width), F32),
            pltpu.VMEM((rows, width), BF16),
            pltpu.VMEM((lay.rows * node_dev, width), F32),
            pltpu.SemaphoreType.DMA((lay.cols + n_sums,)),
        ],
        compiler_params=params(),
        cost_estimate=cost(5 * rows * width * width, 8 * rows * width),
        name="dense_and_backward",
    )(weight, bias, index_own, tiles_own, *ups, *sums)


def place_weight_gradient(lay, own, other, width):
    half = width // 2
    share = half // lay.pairs

    def kernel(*refs):
        own_refs, other_refs, out_ref = refs[: lay.pairs], refs[lay.pairs : 2 * lay.pairs], refs[-1]
        col = lax.axis_index("col")
        pair, core = col // 2, lax.rem(col, 2)
        for dk, shares in enumerate((own_refs, other_refs)):
            for dx in range(lay.pairs):
                at = pl.multiple_of(xor_to(core, dk) * half + xor_to(pair, dx) * share, share)
                out_ref[pl.ds(at, share), :] = shares[dx][...].astype(F32)

    return pl.pallas_call(
        kernel,
        out_shape=jax.ShapeDtypeStruct((width, width), F32),
        in_specs=[vmem()] * (2 * lay.pairs),
        out_specs=vmem(),
        compiler_params=params(),
        cost_estimate=cost(width * width, 6 * width * width),
        name="place_weight_gradient",
    )(*own, *other)


def split_bias(total, width):
    line_sum = total[-EXTRA_ROWS] + total[1 - EXTRA_ROWS]
    high = line_sum.astype(BF16)
    low = (line_sum - high.astype(F32)).astype(BF16)
    line = jnp.arange(EXTRA_ROWS)[:, None]
    extra = jnp.where(line == 0, high[None], jnp.where(line == 1, low[None], jnp.zeros((), BF16)))
    return jnp.concatenate([total[:-EXTRA_ROWS].astype(BF16), extra])


def shards(features, blocks, block_rows, block_cols, block_count, weight, bias_vector, upstream):
    lay = Layout(lax.axis_size("row"), lax.axis_size("col"))
    node_dev, width = features.shape
    half = width // 2
    scale = 1.0 / math.sqrt(node_dev * lay.rows * lay.cols)
    tiles = blocks[0, 0]
    core = lax.axis_index("col") % 2

    index = jnp.concatenate([block_rows[0, 0], block_cols[0, 0], block_count[0]])
    low, high = features[:, :half], features[:, half:]
    keep = jnp.where(core == 0, low, high)
    give = jnp.where(core == 0, high, low)
    piece = jnp.stack([keep, lay.move_col(give, core=1)])

    piece, upstream = lax.optimization_barrier((piece, upstream))
    gathered = {0: piece}

    def over_fast(dz):
        for dy in range(1, lay.fast):
            gathered[dz * lay.fast + dy] = lay.move_row(gathered[dz * lay.fast], fast=dy)

    def over_fast_of(dz):
        return [gathered[dz * lay.fast + dy] for dy in range(1, lay.fast)]

    for dz in reversed(range(1, lay.slow)):
        if dz & (dz - 1) == 0:
            gathered[dz * lay.fast] = lay.move_row(piece, slow=dz)
    over_fast(0)
    far_ups = [lay.move_col(upstream, pair=dx, core=dk) for dx in range(1, lay.pairs) for dk in range(2)]
    one = lay.fast if lay.slow > 1 else 0
    near, gathered[one], own_upstream, own_index, own_tiles = lax.optimization_barrier(
        (over_fast_of(0), gathered[one], upstream, index, tiles)
    )
    gathered.update(zip(range(1, lay.fast), near))
    index_other = lay.move_col(own_index, core=1)
    tiles_other = lay.move_col(own_tiles, core=1)
    near_up = lay.move_col(own_upstream, core=1)
    for dz in range(1, lay.slow):
        top = 1 << (dz.bit_length() - 1)
        if dz != top:
            source, far_ups = lax.optimization_barrier((gathered[top * lay.fast], far_ups))
            gathered[top * lay.fast] = source
            gathered[dz * lay.fast] = lay.move_row(source, slow=dz ^ top)
    others = (index_other, tiles_other, near_up)
    for dz in range(1, lay.slow):
        over_fast(dz)
        if dz < lay.slow - 1:
            after = (dz + 1) * lay.fast
            extra = others if dz == lay.slow - 2 else ()
            gathered[after], done, extra = lax.optimization_barrier((gathered[after], over_fast_of(dz), extra))
            gathered.update(zip(range(dz * lay.fast + 1, after), done))
            others = extra or others
    index_other, tiles_other, near_up = others
    ups = [upstream, near_up] + list(far_ups)
    pieces = [gathered[d] for d in range(lay.rows)]

    mine = forward_product(lay, index, index_other, tiles, tiles_other, pieces, node_dev * lay.cols)
    sums = list(mine) + [lay.move_col(a, core=1) for a in mine]
    for dx in range(1, lay.pairs):
        came = [lay.move_col(a, pair=dx) for a in mine]
        sums += came + [lay.move_col(a, core=1) for a in came]

    activated, gw, *outs = dense_and_backward(
        lay, sums, weight, bias_vector[None], index, tiles, ups
    )

    def fast_sum(dz):
        arrived = [lay.move_row(outs[dz * lay.fast + dy], fast=dy) for dy in range(1, lay.fast)]
        return sum([a.astype(F32) for a in arrived], outs[dz * lay.fast].astype(F32))

    def hold(dz, until):
        span = slice(dz * lay.fast + 1, (dz + 1) * lay.fast)
        until, outs[span] = lax.optimization_barrier((until, outs[span]))
        return until

    hops = [dict(slow=1 << i) for i in range(lay.slow.bit_length() - 1)]
    hops += [dict(fast=1 << i) for i in range(lay.fast.bit_length() - 1)]
    sums = {dz: fast_sum(dz) for dz in range(2, lay.slow)}
    came = None
    for n, hop in enumerate(hops):
        if n:
            gw = split_bias(gw.astype(F32) + came.astype(F32), width)
            if hop.get("fast") == 1 and lay.slow > 2:
                gw, sums[2] = lax.optimization_barrier((gw, sums[2]))
            if hop.get("fast") == 1 and lay.slow > 1:
                gw = hold(1, gw)
        came = lay.move_row(gw, **hop)
    came = hold(0, came)
    for dz in range(min(2, lay.slow)):
        sums[dz] = fast_sum(dz)
    for dz in reversed(range(1, lay.slow)):
        top = 1 << (dz.bit_length() - 1)
        to, hop = (top, dz ^ top) if dz != top else (0, dz)
        sums[to] = sums[to] + lay.move_row(sums[dz].astype(BF16), slow=hop).astype(F32)
    grad_features = sums[0].astype(BF16)

    total = (gw.astype(F32) + came.astype(F32)) * scale
    grad_bias = total[-EXTRA_ROWS] + total[1 - EXTRA_ROWS]
    share = total[:-EXTRA_ROWS].astype(BF16)
    own = [share] + [lay.move_col(share, pair=dx) for dx in range(1, lay.pairs)]
    other = lay.move_col(jnp.stack(own), core=1)
    grad_weight = place_weight_gradient(lay, own, [other[i] for i in range(lay.pairs)], width)
    return (activated, grad_weight, grad_bias, grad_features)


def solution(mesh):
    in_specs = (
        P(("col", "row"), None),
        P("row", "col", None, None, None),
        P("row", "col", None),
        P("row", "col", None),
        P("row", "col"),
        P(),
        P(),
        P(("row", "col"), None),
    )
    out_specs = (P(("row", "col"), None), P(), P(), P(("col", "row"), None))
    return jax.shard_map(shards, mesh=mesh, in_specs=in_specs, out_specs=out_specs, check_vma=False)
```

time: 130 us -> 103 us (0.79)
  the two profiles are of different devices: /device:TPU:9 before, /device:TPU:0 now
where the time goes in v2:
time: 103 us; the launch traced here: 101 us
  waiting for transfers between devices  58 us (56%)
  starting transfers between devices  29.9 us (29%)
  Pallas kernels  7.8 us (8%)
  other arithmetic  3.2 us (3%)
  between operations  1.5 us (1%)
    ppermute x17, waiting for transfers between devices, move_row(): return lax.ppermute(a, 'row', [(r, r ^ d) for r in range(self.rows)])  44.6 us
    ppermute x17, starting transfers between devices, move_row(): return lax.ppermute(a, 'row', [(r, r ^ d) for r in range(self.rows)])  22.7 us
    ppermute x14, waiting for transfers between devices, move_col(): return lax.ppermute(a, 'col', [(c, c ^ d) for c in range(self.cols)])  13.5 us
    ppermute x14, starting transfers between devices, move_col(): return lax.ppermute(a, 'col', [(c, c ^ d) for c in range(self.cols)])  7.19 us
    pallas_call x1, Pallas kernels, dense_and_backward(): pl.pallas_call(kernel, out_shape=[jax.ShapeDtypeStruct((node_dev, width),...  5.35 us
  transfers between devices with their start and end apart: 31, of which 20 were waited for; matrix products, arithmetic and copies ran while one was open for 2% of the time, Pallas kernels for 0%

profile of v2, /device:TPU:0, one launch (start us, length us, event | category | flops | bytes accessed | tf_op | source)
XLA Modules:
  0.0 101.2 jit_solution(10497973014068999964)
XLA Ops:
  0.7 1.0 %select_bitcast_fusion = (bf16[1,256,256]{2,1,0:T(8,128)(2,1)S(1)}, bf16[256,256]{1,0:T(8,128)(2,1)S(1)}) fusion(pred[]{:T(512)S(6)} %eq.28, bf16[256,512]{1,0:T(8,128)(2,1)} %param.8), kind=kLoop, calls=%fused_computation.17 | loop fusion | flops 131072 | bytes 524289 | tf_op jit(solution)/shard_map/stack | solution.py:265
  1.7 0.0 copy-start
  1.7 0.5 collective-permute-start
  2.2 1.0 collective-permute-done
  3.2 2.9 %collective-permute-start.5 = (bf16[2,256,256]{2,1,0:T(8,128)(2,1)S(1)}, bf16[2,256,256]{2,1,0:T(8,128)(2,1)S(1)}, u32[]{:S(2)}, u32[]{:S(2)}) collective-permute-start(bf16[2,256,256]{2,1,0:T(8,128)(2,1)S(1)} %pad_maximum_fusion.refs_0_), channel_id=1, source_target_pairs={{0,4},{4,0},{8,12},{12,8},{16,20},{20,16},{24,28},{28,24},{1,5},{5... | collective-permute-start | bytes 786440 | tf_op jit(solution)/shard_map/ppermute | solution.py:57
  6.2 1.6 %collective-permute-start.6 = (bf16[2,256,256]{2,1,0:T(8,128)(2,1)S(1)}, bf16[2,256,256]{2,1,0:T(8,128)(2,1)S(1)}, u32[]{:S(2)}, u32[]{:S(2)}) collective-permute-start(bf16[2,256,256]{2,1,0:T(8,128)(2,1)S(1)} %pad_maximum_fusion.refs_0_), channel_id=1, source_target_pairs={{0,8},{4,12},{8,0},{12,4},{16,24},{20,28},{24,16},{28,20},{1,9},{5... | collective-permute-start | bytes 786440 | tf_op jit(solution)/shard_map/ppermute | solution.py:57
  8.4 0.0 copy-start.4
  8.4 0.0 copy-start.5
  8.4 0.6 copy-done.4
  9.1 0.0 copy-done.5
  9.1 0.1 pad_add_fusion.io_ref.idx
  9.2 2.6 %collective-permute-start.1 = (bf16[2,256,256]{2,1,0:T(8,128)(2,1)S(1)}, bf16[2,256,256]{2,1,0:T(8,128)(2,1)S(1)}, u32[]{:S(2)}, u32[]{:S(2)}) collective-permute-start(bf16[2,256,256]{2,1,0:T(8,128)(2,1)S(1)} %pad_maximum_fusion.refs_0_), channel_id=1, source_target_pairs={{0,16},{4,20},{8,24},{12,28},{16,0},{20,4},{24,8},{28,12},{1,17},{... | collective-permute-start | bytes 786440 | tf_op jit(solution)/shard_map/ppermute | solution.py:57
  11.7 1.5 %collective-permute-start.2 = (bf16[256,512]{1,0:T(8,128)(2,1)S(1)}, bf16[256,512]{1,0:T(8,128)(2,1)S(1)}, u32[]{:S(2)}, u32[]{:S(2)}) collective-permute-start(bf16[256,512]{1,0:T(8,128)(2,1)S(1)} %copy-done.2), channel_id=1, source_target_pairs={{0,2},{1,3},{2,0},{3,1},{4,6},{5,7},{6,4},{7,5},{8,10},{9,11},{10,... | collective-permute-start | bytes 786440 | tf_op jit(solution)/shard_map/ppermute | solution.py:61
  13.2 5.1 %collective-permute-done.6.refs_2_ = bf16[2,256,256]{2,1,0:T(8,128)(2,1)S(1)} collective-permute-done((bf16[2,256,256]{2,1,0:T(8,128)(2,1)S(1)}, bf16[2,256,256]{2,1,0:T(8,128)(2,1)S(1)}, u32[]{:S(2)}, u32[]{:S(2)}) %collective-permute-start.6) | collective-permute-done | bytes 262176 | tf_op jit(solution)/shard_map/ppermute | solution.py:57
  18.4 0.4 collective-permute-start.7
  18.7 4.8 %collective-permute-done.1.refs_4_ = bf16[2,256,256]{2,1,0:T(8,128)(2,1)S(1)} collective-permute-done((bf16[2,256,256]{2,1,0:T(8,128)(2,1)S(1)}, bf16[2,256,256]{2,1,0:T(8,128)(2,1)S(1)}, u32[]{:S(2)}, u32[]{:S(2)}) %collective-permute-start.1) | collective-permute-done | bytes 262176 | tf_op jit(solution)/shard_map/ppermute | solution.py:57
  23.5 0.4 collective-permute-done.3.refs_3_
  23.9 1.1 %collective-permute-start.11 = (bf16[256,512]{1,0:T(8,128)(2,1)S(1)}, bf16[256,512]{1,0:T(8,128)(2,1)S(1)}, u32[]{:S(2)}, u32[]{:S(2)}) collective-permute-start(bf16[256,512]{1,0:T(8,128)(2,1)S(1)} %copy-done.2), channel_id=1, source_target_pairs={{0,1},{1,0},{2,3},{3,2},{4,5},{5,4},{6,7},{7,6},{8,9},{9,8},{10,11... | collective-permute-start | bytes 786440 | tf_op jit(solution)/shard_map/ppermute | solution.py:61
  25.0 0.2 collective-permute-start.4
  25.2 0.1 collective-permute-done.7.refs_3_
  25.2 0.9 collective-permute-start.8
  26.1 1.1 %collective-permute-done.9.ix_ref = s32[25]{0:T(128)S(1)} collective-permute-done((s32[25]{0:T(128)S(1)}, s32[25]{0:T(128)S(1)}, u32[]{:S(2)}, u32[]{:S(2)}) %collective-permute-start.9) | collective-permute-done | bytes 132 | tf_op jit(solution)/shard_map/ppermute | solution.py:61
  27.2 6.0 %collective-permute-done.4.refs_6_ = bf16[2,256,256]{2,1,0:T(8,128)(2,1)S(1)} collective-permute-done((bf16[2,256,256]{2,1,0:T(8,128)(2,1)S(1)}, bf16[2,256,256]{2,1,0:T(8,128)(2,1)S(1)}, u32[]{:S(2)}, u32[]{:S(2)}) %collective-permute-start.4) | collective-permute-done | bytes 262176 | tf_op jit(solution)/shard_map/ppermute | solution.py:57
  33.2 0.1 collective-permute-done.8.refs_5_
  33.3 0.5 collective-permute-start.12
  33.8 6.8 %collective-permute-done.12.refs_7_ = bf16[2,256,256]{2,1,0:T(8,128)(2,1)S(1)} collective-permute-done((bf16[2,256,256]{2,1,0:T(8,128)(2,1)S(1)}, bf16[2,256,256]{2,1,0:T(8,128)(2,1)S(1)}, u32[]{:S(2)}, u32[]{:S(2)}) %collective-permute-start.12) | collective-permute-done | bytes 262176 | tf_op jit(solution)/shard_map/ppermute | solution.py:57
  40.6 1.4 %forward_product.1 = (bf16[512,256]{1,0:T(8,128)(2,1)S(1)}, bf16[512,256]{1,0:T(8,128)(2,1)S(1)}) custom-call(s32[25]{0:T(128)S(1)} %pad_add_fusion.io_ref.idx, s32[25]{0:T(128)S(1)} %collective-permute-done.9.ix_ref, bf16[12,128,128]{2,1,0:T(8,128)(2,1)S(1)} %bitcast.19, bf16[12,128,128]{2,1,0:T(8,128)(2,1)S(1)} %collective-permute-done.10.ax_ref, ...), custom_call_target="tpu_custom_call" | custom-call | flops 201326592 | bytes 2097152 | tf_op jit(solution)/shard_map/forward_product/pallas_call | solution.py:100
  42.0 0.0 copy-start.3
  42.0 1.8 %collective-permute-start.15 = (bf16[512,256]{1,0:T(8,128)(2,1)S(1)}, bf16[512,256]{1,0:T(8,128)(2,1)S(1)}, u32[]{:S(2)}, u32[]{:S(2)}) collective-permute-start(bf16[512,256]{1,0:T(8,128)(2,1)S(1)} %get-tuple-element.56.refs_4_), channel_id=1, source_target_pairs={{0,2},{1,3},{2,0},{3,1},{4,6},{5,7},{6,4},{7,5},{8,10},{9,11},{10,... | collective-permute-start | bytes 786440 | tf_op jit(solution)/shard_map/ppermute | solution.py:61
  43.8 0.3 collective-permute-start.16
  44.1 0.5 collective-permute-start.14
  44.6 6.6 %collective-permute-done.15.refs_8_ = bf16[512,256]{1,0:T(8,128)(2,1)S(1)} collective-permute-done((bf16[512,256]{1,0:T(8,128)(2,1)S(1)}, bf16[512,256]{1,0:T(8,128)(2,1)S(1)}, u32[]{:S(2)}, u32[]{:S(2)}) %collective-permute-start.15) | collective-permute-done | bytes 262176 | tf_op jit(solution)/shard_map/ppermute | solution.py:61
  51.3 2.8 %collective-permute-done.16.refs_9_ = bf16[512,256]{1,0:T(8,128)(2,1)S(1)} collective-permute-done((bf16[512,256]{1,0:T(8,128)(2,1)S(1)}, bf16[512,256]{1,0:T(8,128)(2,1)S(1)}, u32[]{:S(2)}, u32[]{:S(2)}) %collective-permute-start.16) | collective-permute-done | bytes 262176 | tf_op jit(solution)/shard_map/ppermute | solution.py:61
  54.1 1.5 %collective-permute-done.18.refs_11_ = bf16[512,256]{1,0:T(8,128)(2,1)S(1)} collective-permute-done((bf16[512,256]{1,0:T(8,128)(2,1)S(1)}, bf16[512,256]{1,0:T(8,128)(2,1)S(1)}, u32[]{:S(2)}, u32[]{:S(2)}) %collective-permute-start.18) | collective-permute-done | bytes 262176 | tf_op jit(solution)/shard_map/ppermute | solution.py:61
  55.6 5.3 %dense_and_backward.1 = (bf16[256,512]{1,0:T(8,128)(2,1)}, bf16[144,512]{1,0:T(8,128)(2,1)S(1)}, bf16[256,512]{1,0:T(8,128)(2,1)S(1)}, bf16[256,512]{1,0:T(8,128...) custom-call(bf16[512,512]{1,0:T(8,128)(2,1)S(1)} %copy-done.1, ...), custom_call_target="tpu_custom_call" | custom-call | flops 1342177280 | bytes 4194304 | tf_op jit(solution)/shard_map/dense_and_backward/pallas_call | solution.py:196
  61.0 1.8 %collective-permute-start.19 = (bf16[144,512]{1,0:T(8,128)(2,1)S(1)}, bf16[144,512]{1,0:T(8,128)(2,1)S(1)}, u32[]{:S(2)}, u32[]{:S(2)}) collective-permute-start(bf16[144,512]{1,0:T(8,128)(2,1)S(1)} %get-tuple-element.59), channel_id=1, source_target_pairs={{0,8},{4,12},{8,0},{12,4},{16,24},{20,28},{24,16},{28,20},{1,9},{5... | collective-permute-start | bytes 442376 | tf_op jit(solution)/shard_map/ppermute | solution.py:57
  62.8 0.7 collective-permute-start.26
  63.5 1.3 %collective-permute-start.21 = (bf16[256,512]{1,0:T(8,128)(2,1)S(1)}, bf16[256,512]{1,0:T(8,128)(2,1)S(1)}, u32[]{:S(2)}, u32[]{:S(2)}) collective-permute-start(bf16[256,512]{1,0:T(8,128)(2,1)S(1)} %get-tuple-element.61), channel_id=1, source_target_pairs={{0,4},{4,0},{8,12},{12,8},{16,20},{20,16},{24,28},{28,24},{1,5},{5... | collective-permute-start | bytes 786440 | tf_op jit(solution)/shard_map/ppermute | solution.py:57
  64.8 2.2 %collective-permute-done.19 = bf16[144,512]{1,0:T(8,128)(2,1)S(1)} collective-permute-done((bf16[144,512]{1,0:T(8,128)(2,1)S(1)}, bf16[144,512]{1,0:T(8,128)(2,1)S(1)}, u32[]{:S(2)}, u32[]{:S(2)}) %collective-permute-start.19) | collective-permute-done | bytes 147488 | tf_op jit(solution)/shard_map/ppermute | solution.py:57
  67.0 0.1 select_select_fusion.1
  67.1 2.5 %collective-permute-start.20 = (bf16[144,512]{1,0:T(8,128)(2,1)S(1)}, bf16[144,512]{1,0:T(8,128)(2,1)S(1)}, u32[]{:S(2)}, u32[]{:S(2)}) collective-permute-start(bf16[144,512]{1,0:T(8,128)(2,1)S(1)} %pad_maximum_fusion.2), channel_id=1, source_target_pairs={{0,16},{4,20},{8,24},{12,28},{16,0},{20,4},{24,8},{28,12},{1,17},{... | collective-permute-start | bytes 442376 | tf_op jit(solution)/shard_map/ppermute | solution.py:57
  69.6 6.5 %collective-permute-done.21 = bf16[256,512]{1,0:T(8,128)(2,1)S(1)} collective-permute-done((bf16[256,512]{1,0:T(8,128)(2,1)S(1)}, bf16[256,512]{1,0:T(8,128)(2,1)S(1)}, u32[]{:S(2)}, u32[]{:S(2)}) %collective-permute-start.21) | collective-permute-done | bytes 262176 | tf_op jit(solution)/shard_map/ppermute | solution.py:57
  76.1 0.1 convert_add_fusion
  76.2 0.1 collective-permute-done.20
  76.4 0.1 select_select_fusion
  76.5 1.2 %collective-permute-start.22 = (bf16[144,512]{1,0:T(8,128)(2,1)S(1)}, bf16[144,512]{1,0:T(8,128)(2,1)S(1)}, u32[]{:S(2)}, u32[]{:S(2)}) collective-permute-start(bf16[144,512]{1,0:T(8,128)(2,1)S(1)} %pad_maximum_fusion.3), channel_id=1, source_target_pairs={{0,4},{4,0},{8,12},{12,8},{16,20},{20,16},{24,28},{28,24},{1,5},{5... | collective-permute-start | bytes 442376 | tf_op jit(solution)/shard_map/ppermute | solution.py:57
  77.7 0.1 add_convert_fusion.3
  77.8 0.7 collective-permute-start.27
  78.5 0.8 collective-permute-start.29
  79.3 3.8 %collective-permute-done.22 = bf16[144,512]{1,0:T(8,128)(2,1)S(1)} collective-permute-done((bf16[144,512]{1,0:T(8,128)(2,1)S(1)}, bf16[144,512]{1,0:T(8,128)(2,1)S(1)}, u32[]{:S(2)}, u32[]{:S(2)}) %collective-permute-start.22) | collective-permute-done | bytes 147488 | tf_op jit(solution)/shard_map/ppermute | solution.py:57
  83.2 1.4 %collective-permute-start.25 = (bf16[256,512]{1,0:T(8,128)(2,1)S(1)}, bf16[256,512]{1,0:T(8,128)(2,1)S(1)}, u32[]{:S(2)}, u32[]{:S(2)}) collective-permute-start(bf16[256,512]{1,0:T(8,128)(2,1)S(1)} %get-tuple-element.68), channel_id=1, source_target_pairs={{0,4},{4,0},{8,12},{12,8},{16,20},{20,16},{24,28},{28,24},{1,5},{5... | collective-permute-start | bytes 786440 | tf_op jit(solution)/shard_map/ppermute | solution.py:57
  84.6 1.4 %collective-permute-start.23 = (bf16[128,512]{1,0:T(8,128)(2,1)S(1)}, bf16[128,512]{1,0:T(8,128)(2,1)S(1)}, u32[]{:S(2)}, u32[]{:S(2)}) collective-permute-start(bf16[128,512]{1,0:T(8,128)(2,1)S(1)} %slice.97.refs_0_), channel_id=1, source_target_pairs={{0,2},{1,3},{2,0},{3,1},{4,6},{5,7},{6,4},{7,5},{8,10},{9,11},{10,... | collective-permute-start | bytes 393224 | tf_op jit(solution)/shard_map/ppermute | solution.py:61
  86.0 0.1 add_convert_fusion.2
  86.1 2.1 %collective-permute-start.28 = (bf16[256,512]{1,0:T(8,128)(2,1)S(1)}, bf16[256,512]{1,0:T(8,128)(2,1)S(1)}, u32[]{:S(2)}, u32[]{:S(2)}) collective-permute-start(bf16[256,512]{1,0:T(8,128)(2,1)S(1)} %add_convert_fusion.2), channel_id=1, source_target_pairs={{0,16},{4,20},{8,24},{12,28},{16,0},{20,4},{24,8},{28,12},{1,17},{... | collective-permute-start | bytes 786440 | tf_op jit(solution)/shard_map/ppermute | solution.py:57
  88.2 0.5 collective-permute-done.29
  88.7 0.1 add_convert_fusion.1
  88.8 1.3 %collective-permute-start.30 = (bf16[256,512]{1,0:T(8,128)(2,1)S(1)}, bf16[256,512]{1,0:T(8,128)(2,1)S(1)}, u32[]{:S(2)}, u32[]{:S(2)}) collective-permute-start(bf16[256,512]{1,0:T(8,128)(2,1)S(1)} %add_convert_fusion.1), channel_id=1, source_target_pairs={{0,8},{4,12},{8,0},{12,4},{16,24},{20,28},{24,16},{28,20},{1,9},{5... | collective-permute-start | bytes 786440 | tf_op jit(solution)/shard_map/ppermute | solution.py:57
  90.1 0.1 collective-permute-start.24
  90.2 0.6 slice_add_fusion
  90.8 2.3 %collective-permute-done.25 = bf16[256,512]{1,0:T(8,128)(2,1)S(1)} collective-permute-done((bf16[256,512]{1,0:T(8,128)(2,1)S(1)}, bf16[256,512]{1,0:T(8,128)(2,1)S(1)}, u32[]{:S(2)}, u32[]{:S(2)}) %collective-permute-start.25) | collective-permute-done | bytes 262176 | tf_op jit(solution)/shard_map/ppermute | solution.py:57
  93.1 5.9 %collective-permute-done.28 = bf16[256,512]{1,0:T(8,128)(2,1)S(1)} collective-permute-done((bf16[256,512]{1,0:T(8,128)(2,1)S(1)}, bf16[256,512]{1,0:T(8,128)(2,1)S(1)}, u32[]{:S(2)}, u32[]{:S(2)}) %collective-permute-start.28) | collective-permute-done | bytes 262176 | tf_op jit(solution)/shard_map/ppermute | solution.py:57
  98.9 0.4 collective-permute-done.30
  99.3 0.8 add_convert_fusion
  100.2 1.1 %place_weight_gradient.1 = f32[512,512]{1,0:T(8,128)} custom-call(bf16[128,512]{1,0:T(8,128)(2,1)S(1)} %slice.97.refs_0_, bf16[128,512]{1,0:T(8,128)(2,1)S(1)} %collective-permute-done.23.refs_1_, bf16[128,512]{1,0:T(8,128)(2,1)S(1)} %get-tuple-element.79.refs_2_, bf16[128,512]{1,0:T(8,128)(2,1)S(1)} %get-tuple-element.78.refs_3_), custom_call_target="tpu_custom_call" | custom-call | flops 262144 | bytes 1572864 | tf_op jit(solution)/shard_map/place_weight_gradient/pallas_call | solution.py:233
  (38 shorter events, 0.4 us)
Async XLA Ops:
  0.6 11.1 %copy-start.2 = (bf16[256,512]{1,0:T(8,128)(2,1)S(1)}, bf16[256,512]{1,0:T(8,128)(2,1)}, u32[]{:S(2)}) copy-start(bf16[256,512]{1,0:T(8,128)(2,1)} %refs_0_) | copy-start | bytes 786436
  1.7 17.0 %copy-start = (bf16[1,1,12,128,128]{4,3,2,1,0:T(8,128)(2,1)S(1)}, bf16[1,1,12,128,128]{4,3,2,1,0:T(8,128)(2,1)}, u32[]{:S(2)}) copy-start(bf16[1,1,12,128,128]{4,3,2,1,0:T(8,128)(2,1)} %param.9) | copy-start | bytes 1179652
  1.7 1.5 %collective-permute-start = (bf16[256,256]{1,0:T(8,128)(2,1)S(1)}, bf16[256,256]{1,0:T(8,128)(2,1)S(1)}, u32[]{:S(2)}, u32[]{:S(2)}) collective-permute-start(bf16[256,256]{1,0:T(8,128)(2,1)S(1)} %get-tuple-element.81), channel_id=1, source_target_pairs={{0,1},{1,0},{2,3},{3,2},{4,5},{5,4},{6,7},{7,6},{8,9},{9,8},{10,11... | collective-permute-start | bytes 393224 | tf_op jit(solution)/shard_map/ppermute | solution.py:61
  3.2 10.0 %collective-permute-start.5 = (bf16[2,256,256]{2,1,0:T(8,128)(2,1)S(1)}, bf16[2,256,256]{2,1,0:T(8,128)(2,1)S(1)}, u32[]{:S(2)}, u32[]{:S(2)}) collective-permute-start(bf16[2,256,256]{2,1,0:T(8,128)(2,1)S(1)} %pad_maximum_fusion.refs_0_), channel_id=1, source_target_pairs={{0,4},{4,0},{8,12},{12,8},{16,20},{20,16},{24,28},{28,24},{1,5},{5... | collective-permute-start | bytes 786440 | tf_op jit(solution)/shard_map/ppermute | solution.py:57
  6.2 12.2 %collective-permute-start.6 = (bf16[2,256,256]{2,1,0:T(8,128)(2,1)S(1)}, bf16[2,256,256]{2,1,0:T(8,128)(2,1)S(1)}, u32[]{:S(2)}, u32[]{:S(2)}) collective-permute-start(bf16[2,256,256]{2,1,0:T(8,128)(2,1)S(1)} %pad_maximum_fusion.refs_0_), channel_id=1, source_target_pairs={{0,8},{4,12},{8,0},{12,4},{16,24},{20,28},{24,16},{28,20},{1,9},{5... | collective-permute-start | bytes 786440 | tf_op jit(solution)/shard_map/ppermute | solution.py:57
  8.4 0.7 copy-start.4
  8.4 0.7 copy-start.5
  9.2 14.4 %collective-permute-start.1 = (bf16[2,256,256]{2,1,0:T(8,128)(2,1)S(1)}, bf16[2,256,256]{2,1,0:T(8,128)(2,1)S(1)}, u32[]{:S(2)}, u32[]{:S(2)}) collective-permute-start(bf16[2,256,256]{2,1,0:T(8,128)(2,1)S(1)} %pad_maximum_fusion.refs_0_), channel_id=1, source_target_pairs={{0,16},{4,20},{8,24},{12,28},{16,0},{20,4},{24,8},{28,12},{1,17},{... | collective-permute-start | bytes 786440 | tf_op jit(solution)/shard_map/ppermute | solution.py:57
  11.7 11.8 %collective-permute-start.2 = (bf16[256,512]{1,0:T(8,128)(2,1)S(1)}, bf16[256,512]{1,0:T(8,128)(2,1)S(1)}, u32[]{:S(2)}, u32[]{:S(2)}) collective-permute-start(bf16[256,512]{1,0:T(8,128)(2,1)S(1)} %copy-done.2), channel_id=1, source_target_pairs={{0,2},{1,3},{2,0},{3,1},{4,6},{5,7},{6,4},{7,5},{8,10},{9,11},{10,... | collective-permute-start | bytes 786440 | tf_op jit(solution)/shard_map/ppermute | solution.py:61
  13.2 10.7 %collective-permute-start.3 = (bf16[256,512]{1,0:T(8,128)(2,1)S(1)}, bf16[256,512]{1,0:T(8,128)(2,1)S(1)}, u32[]{:S(2)}, u32[]{:S(2)}) collective-permute-start(bf16[256,512]{1,0:T(8,128)(2,1)S(1)} %copy-done.2), channel_id=1, source_target_pairs={{0,3},{1,2},{2,1},{3,0},{4,7},{5,6},{6,5},{7,4},{8,11},{9,10},{10,... | collective-permute-start | bytes 786440 | tf_op jit(solution)/shard_map/ppermute | solution.py:61
  18.4 37.2 %copy-start.1 = (bf16[512,512]{1,0:T(8,128)(2,1)S(1)}, bf16[512,512]{1,0:T(8,128)(2,1)}, u32[]{:S(2)}) copy-start(bf16[512,512]{1,0:T(8,128)(2,1)} %w_ref.1) | copy-start | bytes 1572868
  18.4 6.9 %collective-permute-start.7 = (bf16[2,256,256]{2,1,0:T(8,128)(2,1)S(1)}, bf16[2,256,256]{2,1,0:T(8,128)(2,1)S(1)}, u32[]{:S(2)}, u32[]{:S(2)}) collective-permute-start(bf16[2,256,256]{2,1,0:T(8,128)(2,1)S(1)} %collective-permute-done.6.refs_2_), channel_id=1, source_target_pairs={{0,4},{4,0},{8,12},{12,8},{16,20},{20,16},{24,28},{28,24},{1,5},{5... | collective-permute-start | bytes 786440 | tf_op jit(solution)/shard_map/ppermute | solution.py:57
  18.7 14.5 %collective-permute-start.10 = (bf16[12,128,128]{2,1,0:T(8,128)(2,1)S(1)}, bf16[12,128,128]{2,1,0:T(8,128)(2,1)S(1)}, u32[]{:S(2)}, u32[]{:S(2)}) collective-permute-start(bf16[12,128,128]{2,1,0:T(8,128)(2,1)S(1)} %bitcast.18), channel_id=1, source_target_pairs={{0,1},{1,0},{2,3},{3,2},{4,5},{5,4},{6,7},{7,6},{8,9},{9,8},{10,11... | collective-permute-start | bytes 1179656 | tf_op jit(solution)/shard_map/ppermute | solution.py:61
  23.9 3.3 %collective-permute-start.11 = (bf16[256,512]{1,0:T(8,128)(2,1)S(1)}, bf16[256,512]{1,0:T(8,128)(2,1)S(1)}, u32[]{:S(2)}, u32[]{:S(2)}) collective-permute-start(bf16[256,512]{1,0:T(8,128)(2,1)S(1)} %copy-done.2), channel_id=1, source_target_pairs={{0,1},{1,0},{2,3},{3,2},{4,5},{5,4},{6,7},{7,6},{8,9},{9,8},{10,11... | collective-permute-start | bytes 786440 | tf_op jit(solution)/shard_map/ppermute | solution.py:61
  25.0 8.2 %collective-permute-start.4 = (bf16[2,256,256]{2,1,0:T(8,128)(2,1)S(1)}, bf16[2,256,256]{2,1,0:T(8,128)(2,1)S(1)}, u32[]{:S(2)}, u32[]{:S(2)}) collective-permute-start(bf16[2,256,256]{2,1,0:T(8,128)(2,1)S(1)} %collective-permute-done.1.refs_4_), channel_id=1, source_target_pairs={{0,8},{4,12},{8,0},{12,4},{16,24},{20,28},{24,16},{28,20},{1,9},{5... | collective-permute-start | bytes 786440 | tf_op jit(solution)/shard_map/ppermute | solution.py:57
  25.2 8.1 %collective-permute-start.8 = (bf16[2,256,256]{2,1,0:T(8,128)(2,1)S(1)}, bf16[2,256,256]{2,1,0:T(8,128)(2,1)S(1)}, u32[]{:S(2)}, u32[]{:S(2)}) collective-permute-start(bf16[2,256,256]{2,1,0:T(8,128)(2,1)S(1)} %collective-permute-done.1.refs_4_), channel_id=1, source_target_pairs={{0,4},{4,0},{8,12},{12,8},{16,20},{20,16},{24,28},{28,24},{1,5},{5... | collective-permute-start | bytes 786440 | tf_op jit(solution)/shard_map/ppermute | solution.py:57
  26.1 1.1 %collective-permute-start.9 = (s32[25]{0:T(128)S(1)}, s32[25]{0:T(128)S(1)}, u32[]{:S(2)}, u32[]{:S(2)}) collective-permute-start(s32[25]{0:T(128)S(1)} %pad_add_fusion.io_ref.idx), channel_id=1, source_target_pairs={{0,1},{1,0},{2,3},{3,2},{4,5},{5,4},{6,7},{7,6},{8,9},{9,8},{10,11... | collective-permute-start | bytes 308 | tf_op jit(solution)/shard_map/ppermute | solution.py:61
  33.3 7.3 %collective-permute-start.12 = (bf16[2,256,256]{2,1,0:T(8,128)(2,1)S(1)}, bf16[2,256,256]{2,1,0:T(8,128)(2,1)S(1)}, u32[]{:S(2)}, u32[]{:S(2)}) collective-permute-start(bf16[2,256,256]{2,1,0:T(8,128)(2,1)S(1)} %collective-permute-done.4.refs_6_), channel_id=1, source_target_pairs={{0,4},{4,0},{8,12},{12,8},{16,20},{20,16},{24,28},{28,24},{1,5},{5... | collective-permute-start | bytes 786440 | tf_op jit(solution)/shard_map/ppermute | solution.py:57
  42.0 13.6 %copy-start.3 = (f32[512]{0:T(512)S(1)}, f32[512]{0:T(512)}, u32[]{:S(2)}) copy-start(f32[512]{0:T(512)} %param.14) | copy-start | bytes 6148
  42.0 9.3 %collective-permute-start.15 = (bf16[512,256]{1,0:T(8,128)(2,1)S(1)}, bf16[512,256]{1,0:T(8,128)(2,1)S(1)}, u32[]{:S(2)}, u32[]{:S(2)}) collective-permute-start(bf16[512,256]{1,0:T(8,128)(2,1)S(1)} %get-tuple-element.56.refs_4_), channel_id=1, source_target_pairs={{0,2},{1,3},{2,0},{3,1},{4,6},{5,7},{6,4},{7,5},{8,10},{9,11},{10,... | collective-permute-start | bytes 786440 | tf_op jit(solution)/shard_map/ppermute | solution.py:61
  43.8 10.3 %collective-permute-start.16 = (bf16[512,256]{1,0:T(8,128)(2,1)S(1)}, bf16[512,256]{1,0:T(8,128)(2,1)S(1)}, u32[]{:S(2)}, u32[]{:S(2)}) collective-permute-start(bf16[512,256]{1,0:T(8,128)(2,1)S(1)} %get-tuple-element.57.refs_5_), channel_id=1, source_target_pairs={{0,2},{1,3},{2,0},{3,1},{4,6},{5,7},{6,4},{7,5},{8,10},{9,11},{10,... | collective-permute-start | bytes 786440 | tf_op jit(solution)/shard_map/ppermute | solution.py:61
  44.1 10.0 %collective-permute-start.13 = (bf16[512,256]{1,0:T(8,128)(2,1)S(1)}, bf16[512,256]{1,0:T(8,128)(2,1)S(1)}, u32[]{:S(2)}, u32[]{:S(2)}) collective-permute-start(bf16[512,256]{1,0:T(8,128)(2,1)S(1)} %get-tuple-element.56.refs_4_), channel_id=1, source_target_pairs={{0,1},{1,0},{2,3},{3,2},{4,5},{5,4},{6,7},{7,6},{8,9},{9,8},{10,11... | collective-permute-start | bytes 786440 | tf_op jit(solution)/shard_map/ppermute | solution.py:61
  44.1 10.0 %collective-permute-start.14 = (bf16[512,256]{1,0:T(8,128)(2,1)S(1)}, bf16[512,256]{1,0:T(8,128)(2,1)S(1)}, u32[]{:S(2)}, u32[]{:S(2)}) collective-permute-start(bf16[512,256]{1,0:T(8,128)(2,1)S(1)} %get-tuple-element.57.refs_5_), channel_id=1, source_target_pairs={{0,1},{1,0},{2,3},{3,2},{4,5},{5,4},{6,7},{7,6},{8,9},{9,8},{10,11... | collective-permute-start | bytes 786440 | tf_op jit(solution)/shard_map/ppermute | solution.py:61
  51.3 2.8 %collective-permute-start.17 = (bf16[512,256]{1,0:T(8,128)(2,1)S(1)}, bf16[512,256]{1,0:T(8,128)(2,1)S(1)}, u32[]{:S(2)}, u32[]{:S(2)}) collective-permute-start(bf16[512,256]{1,0:T(8,128)(2,1)S(1)} %collective-permute-done.15.refs_8_), channel_id=1, source_target_pairs={{0,1},{1,0},{2,3},{3,2},{4,5},{5,4},{6,7},{7,6},{8,9},{9,8},{10,11... | collective-permute-start | bytes 786440 | tf_op jit(solution)/shard_map/ppermute | solution.py:61
  54.1 1.5 %collective-permute-start.18 = (bf16[512,256]{1,0:T(8,128)(2,1)S(1)}, bf16[512,256]{1,0:T(8,128)(2,1)S(1)}, u32[]{:S(2)}, u32[]{:S(2)}) collective-permute-start(bf16[512,256]{1,0:T(8,128)(2,1)S(1)} %collective-permute-done.16.refs_9_), channel_id=1, source_target_pairs={{0,1},{1,0},{2,3},{3,2},{4,5},{5,4},{6,7},{7,6},{8,9},{9,8},{10,11... | collective-permute-start | bytes 786440 | tf_op jit(solution)/shard_map/ppermute | solution.py:61
  61.0 6.0 %collective-permute-start.19 = (bf16[144,512]{1,0:T(8,128)(2,1)S(1)}, bf16[144,512]{1,0:T(8,128)(2,1)S(1)}, u32[]{:S(2)}, u32[]{:S(2)}) collective-permute-start(bf16[144,512]{1,0:T(8,128)(2,1)S(1)} %get-tuple-element.59), channel_id=1, source_target_pairs={{0,8},{4,12},{8,0},{12,4},{16,24},{20,28},{24,16},{28,20},{1,9},{5... | collective-permute-start | bytes 442376 | tf_op jit(solution)/shard_map/ppermute | solution.py:57
  62.8 14.9 %collective-permute-start.26 = (bf16[256,512]{1,0:T(8,128)(2,1)S(1)}, bf16[256,512]{1,0:T(8,128)(2,1)S(1)}, u32[]{:S(2)}, u32[]{:S(2)}) collective-permute-start(bf16[256,512]{1,0:T(8,128)(2,1)S(1)} %get-tuple-element.71), channel_id=1, source_target_pairs={{0,4},{4,0},{8,12},{12,8},{16,20},{20,16},{24,28},{28,24},{1,5},{5... | collective-permute-start | bytes 786440 | tf_op jit(solution)/shard_map/ppermute | solution.py:57
  63.5 12.7 %collective-permute-start.21 = (bf16[256,512]{1,0:T(8,128)(2,1)S(1)}, bf16[256,512]{1,0:T(8,128)(2,1)S(1)}, u32[]{:S(2)}, u32[]{:S(2)}) collective-permute-start(bf16[256,512]{1,0:T(8,128)(2,1)S(1)} %get-tuple-element.61), channel_id=1, source_target_pairs={{0,4},{4,0},{8,12},{12,8},{16,20},{20,16},{24,28},{28,24},{1,5},{5... | collective-permute-start | bytes 786440 | tf_op jit(solution)/shard_map/ppermute | solution.py:57
  67.1 9.2 %collective-permute-start.20 = (bf16[144,512]{1,0:T(8,128)(2,1)S(1)}, bf16[144,512]{1,0:T(8,128)(2,1)S(1)}, u32[]{:S(2)}, u32[]{:S(2)}) collective-permute-start(bf16[144,512]{1,0:T(8,128)(2,1)S(1)} %pad_maximum_fusion.2), channel_id=1, source_target_pairs={{0,16},{4,20},{8,24},{12,28},{16,0},{20,4},{24,8},{28,12},{1,17},{... | collective-permute-start | bytes 442376 | tf_op jit(solution)/shard_map/ppermute | solution.py:57
  76.5 6.6 %collective-permute-start.22 = (bf16[144,512]{1,0:T(8,128)(2,1)S(1)}, bf16[144,512]{1,0:T(8,128)(2,1)S(1)}, u32[]{:S(2)}, u32[]{:S(2)}) collective-permute-start(bf16[144,512]{1,0:T(8,128)(2,1)S(1)} %pad_maximum_fusion.3), channel_id=1, source_target_pairs={{0,4},{4,0},{8,12},{12,8},{16,20},{20,16},{24,28},{28,24},{1,5},{5... | collective-permute-start | bytes 442376 | tf_op jit(solution)/shard_map/ppermute | solution.py:57
  77.8 8.3 %collective-permute-start.27 = (bf16[256,512]{1,0:T(8,128)(2,1)S(1)}, bf16[256,512]{1,0:T(8,128)(2,1)S(1)}, u32[]{:S(2)}, u32[]{:S(2)}) collective-permute-start(bf16[256,512]{1,0:T(8,128)(2,1)S(1)} %add_convert_fusion.3), channel_id=1, source_target_pairs={{0,8},{4,12},{8,0},{12,4},{16,24},{20,28},{24,16},{28,20},{1,9},{5... | collective-permute-start | bytes 786440 | tf_op jit(solution)/shard_map/ppermute | solution.py:57
  78.5 10.2 %collective-permute-start.29 = (bf16[256,512]{1,0:T(8,128)(2,1)S(1)}, bf16[256,512]{1,0:T(8,128)(2,1)S(1)}, u32[]{:S(2)}, u32[]{:S(2)}) collective-permute-start(bf16[256,512]{1,0:T(8,128)(2,1)S(1)} %get-tuple-element.73), channel_id=1, source_target_pairs={{0,4},{4,0},{8,12},{12,8},{16,20},{20,16},{24,28},{28,24},{1,5},{5... | collective-permute-start | bytes 786440 | tf_op jit(solution)/shard_map/ppermute | solution.py:57
  83.2 9.8 %collective-permute-start.25 = (bf16[256,512]{1,0:T(8,128)(2,1)S(1)}, bf16[256,512]{1,0:T(8,128)(2,1)S(1)}, u32[]{:S(2)}, u32[]{:S(2)}) collective-permute-start(bf16[256,512]{1,0:T(8,128)(2,1)S(1)} %get-tuple-element.68), channel_id=1, source_target_pairs={{0,4},{4,0},{8,12},{12,8},{16,20},{20,16},{24,28},{28,24},{1,5},{5... | collective-permute-start | bytes 786440 | tf_op jit(solution)/shard_map/ppermute | solution.py:57
  84.6 5.4 %collective-permute-start.23 = (bf16[128,512]{1,0:T(8,128)(2,1)S(1)}, bf16[128,512]{1,0:T(8,128)(2,1)S(1)}, u32[]{:S(2)}, u32[]{:S(2)}) collective-permute-start(bf16[128,512]{1,0:T(8,128)(2,1)S(1)} %slice.97.refs_0_), channel_id=1, source_target_pairs={{0,2},{1,3},{2,0},{3,1},{4,6},{5,7},{6,4},{7,5},{8,10},{9,11},{10,... | collective-permute-start | bytes 393224 | tf_op jit(solution)/shard_map/ppermute | solution.py:61
  86.1 12.8 %collective-permute-start.28 = (bf16[256,512]{1,0:T(8,128)(2,1)S(1)}, bf16[256,512]{1,0:T(8,128)(2,1)S(1)}, u32[]{:S(2)}, u32[]{:S(2)}) collective-permute-start(bf16[256,512]{1,0:T(8,128)(2,1)S(1)} %add_convert_fusion.2), channel_id=1, source_target_pairs={{0,16},{4,20},{8,24},{12,28},{16,0},{20,4},{24,8},{28,12},{1,17},{... | collective-permute-start | bytes 786440 | tf_op jit(solution)/shard_map/ppermute | solution.py:57
  88.8 10.5 %collective-permute-start.30 = (bf16[256,512]{1,0:T(8,128)(2,1)S(1)}, bf16[256,512]{1,0:T(8,128)(2,1)S(1)}, u32[]{:S(2)}, u32[]{:S(2)}) collective-permute-start(bf16[256,512]{1,0:T(8,128)(2,1)S(1)} %add_convert_fusion.1), channel_id=1, source_target_pairs={{0,8},{4,12},{8,0},{12,4},{16,24},{20,28},{24,16},{28,20},{1,9},{5... | collective-permute-start | bytes 786440 | tf_op jit(solution)/shard_map/ppermute | solution.py:57
  90.1 10.0 %collective-permute-start.24 = (bf16[2,128,512]{2,1,0:T(8,128)(2,1)S(1)}, bf16[2,128,512]{2,1,0:T(8,128)(2,1)S(1)}, u32[]{:S(2)}, u32[]{:S(2)}) collective-permute-start(bf16[2,128,512]{2,1,0:T(8,128)(2,1)S(1)} %pad_maximum_fusion.1), channel_id=1, source_target_pairs={{0,1},{1,0},{2,3},{3,2},{4,5},{5,4},{6,7},{7,6},{8,9},{9,8},{10,11... | collective-permute-start | bytes 786440 | tf_op jit(solution)/shard_map/ppermute | solution.py:61

commit v3 on v2

--- a/solution.py
+++ b/solution.py
@@ -290,10 +290,8 @@
     for dz in range(1, lay.slow):
         top = 1 << (dz.bit_length() - 1)
         if dz != top:
-            source, far_ups = lax.optimization_barrier((gathered[top * lay.fast], far_ups))
-            gathered[top * lay.fast] = source
-            gathered[dz * lay.fast] = lay.move_row(source, slow=dz ^ top)
-    others = (index_other, tiles_other, near_up)
+            gathered[dz * lay.fast] = lay.move_row(gathered[top * lay.fast], slow=dz ^ top)
+    others = (index_other, tiles_other, near_up, far_ups)
     for dz in range(1, lay.slow):
         over_fast(dz)
         if dz < lay.slow - 1:
@@ -302,7 +300,7 @@
             gathered[after], done, extra = lax.optimization_barrier((gathered[after], over_fast_of(dz), extra))
             gathered.update(zip(range(dz * lay.fast + 1, after), done))
             others = extra or others
-    index_other, tiles_other, near_up = others
+    index_other, tiles_other, near_up, far_ups = others
     ups = [upstream, near_up] + list(far_ups)
     pieces = [gathered[d] for d in range(lay.rows)]
 
@@ -316,8 +314,10 @@
         lay, sums, weight, bias_vector[None], index, tiles, ups
     )
 
-    def fast_sum(dz):
-        arrived = [lay.move_row(outs[dz * lay.fast + dy], fast=dy) for dy in range(1, lay.fast)]
+    def fast_arrivals(dz):
+        return [lay.move_row(outs[dz * lay.fast + dy], fast=dy) for dy in range(1, lay.fast)]
+
+    def fast_sum(dz, arrived):
         return sum([a.astype(F32) for a in arrived], outs[dz * lay.fast].astype(F32))
 
     def hold(dz, until):
@@ -325,25 +325,31 @@
         until, outs[span] = lax.optimization_barrier((until, outs[span]))
         return until
 
+    def slow_sum(dz):
+        top = 1 << (dz.bit_length() - 1)
+        to, hop = (top, dz ^ top) if dz != top else (0, dz)
+        sums[to] = sums[to] + lay.move_row(sums[dz].astype(BF16), slow=hop).astype(F32)
+
     hops = [dict(slow=1 << i) for i in range(lay.slow.bit_length() - 1)]
     hops += [dict(fast=1 << i) for i in range(lay.fast.bit_length() - 1)]
-    sums = {dz: fast_sum(dz) for dz in range(2, lay.slow)}
+    sums = {}
+    if lay.slow > 2:
+        sums[3] = hold(2, fast_sum(3, fast_arrivals(3)).astype(BF16))
+        sums[2] = fast_sum(2, fast_arrivals(2))
+        slow_sum(3)
     came = None
     for n, hop in enumerate(hops):
         if n:
             gw = split_bias(gw.astype(F32) + came.astype(F32), width)
             if hop.get("fast") == 1 and lay.slow > 2:
+                gw = hold(1, gw)
                 gw, sums[2] = lax.optimization_barrier((gw, sums[2]))
-            if hop.get("fast") == 1 and lay.slow > 1:
-                gw = hold(1, gw)
         came = lay.move_row(gw, **hop)
     came = hold(0, came)
     for dz in range(min(2, lay.slow)):
-        sums[dz] = fast_sum(dz)
-    for dz in reversed(range(1, lay.slow)):
-        top = 1 << (dz.bit_length() - 1)
-        to, hop = (top, dz ^ top) if dz != top else (0, dz)
-        sums[to] = sums[to] + lay.move_row(sums[dz].astype(BF16), slow=hop).astype(F32)
+        sums[dz] = fast_sum(dz, fast_arrivals(dz))
+    for dz in reversed(range(1, min(3, lay.slow))):
+        slow_sum(dz)
     grad_features = sums[0].astype(BF16)
 
     total = (gw.astype(F32) + came.astype(F32)) * scale

time: 103 us -> 99.5 us (0.966)
  waiting for transfers between devices: 58 us -> 53.8 us
  Pallas kernels: 7.8 us -> 8.9 us
    ppermute x17, waiting for transfers between devices: 44.6 us -> 33.4 us  [move_row(): return lax.ppermute(a, 'row', [(r, r ^ d) for r in range(self.rows)])]
    ppermute x14, waiting for transfers between devices: 13.5 us -> 20.5 us  [move_col(): return lax.ppermute(a, 'col', [(c, c ^ d) for c in range(self.cols)])]
  transfers between devices with their start and end apart: 31 -> 31, of which waited for: 20 -> 21; matrix products, arithmetic and copies ran while one was open for 2% -> 2% of each run, Pallas kernels for 0% -> 0%
where the time goes in v3:
time: 99.5 us; the launch traced here: 98.5 us
  waiting for transfers between devices  53.8 us (54%)
  starting transfers between devices  30.3 us (30%)
  Pallas kernels  8.9 us (9%)
  other arithmetic  3.16 us (3%)
  between operations  1.5 us (2%)
    ppermute x17, waiting for transfers between devices, move_row(): return lax.ppermute(a, 'row', [(r, r ^ d) for r in range(self.rows)])  33.4 us
    ppermute x17, starting transfers between devices, move_row(): return lax.ppermute(a, 'row', [(r, r ^ d) for r in range(self.rows)])  23.1 us
    ppermute x14, waiting for transfers between devices, move_col(): return lax.ppermute(a, 'col', [(c, c ^ d) for c in range(self.cols)])  20.5 us
    ppermute x14, starting transfers between devices, move_col(): return lax.ppermute(a, 'col', [(c, c ^ d) for c in range(self.cols)])  7.19 us
    pallas_call x1, Pallas kernels, dense_and_backward(): pl.pallas_call(kernel, out_shape=[jax.ShapeDtypeStruct((node_dev, width),...  5.99 us
  transfers between devices with their start and end apart: 31, of which 21 were waited for; matrix products, arithmetic and copies ran while one was open for 2% of the time, Pallas kernels for 0%

profile of v3, /device:TPU:0, one launch (start us, length us, event | category | flops | bytes accessed | tf_op | source)
XLA Modules:
  0.0 98.5 jit_solution(10294015006683306474)
XLA Ops:
  0.7 1.0 %select_bitcast_fusion = (bf16[1,256,256]{2,1,0:T(8,128)(2,1)S(1)}, bf16[256,256]{1,0:T(8,128)(2,1)S(1)}) fusion(pred[]{:T(512)S(6)} %eq.28, bf16[256,512]{1,0:T(8,128)(2,1)} %param.8), kind=kLoop, calls=%fused_computation.16 | loop fusion | flops 131072 | bytes 524289 | tf_op jit(solution)/shard_map/stack | solution.py:265
  1.7 0.0 copy-start
  1.7 0.5 collective-permute-start
  2.2 1.0 %collective-permute-done = bf16[256,256]{1,0:T(8,128)(2,1)S(1)} collective-permute-done((bf16[256,256]{1,0:T(8,128)(2,1)S(1)}, bf16[256,256]{1,0:T(8,128)(2,1)S(1)}, u32[]{:S(2)}, u32[]{:S(2)}) %collective-permute-start) | collective-permute-done | bytes 131104 | tf_op jit(solution)/shard_map/ppermute | solution.py:61
  3.2 2.9 %collective-permute-start.3 = (bf16[2,256,256]{2,1,0:T(8,128)(2,1)S(1)}, bf16[2,256,256]{2,1,0:T(8,128)(2,1)S(1)}, u32[]{:S(2)}, u32[]{:S(2)}) collective-permute-start(bf16[2,256,256]{2,1,0:T(8,128)(2,1)S(1)} %pad_maximum_fusion.refs_0_), channel_id=1, source_target_pairs={{0,4},{4,0},{8,12},{12,8},{16,20},{20,16},{24,28},{28,24},{1,5},{5... | collective-permute-start | bytes 786440 | tf_op jit(solution)/shard_map/ppermute | solution.py:57
  6.2 1.6 %collective-permute-start.4 = (bf16[2,256,256]{2,1,0:T(8,128)(2,1)S(1)}, bf16[2,256,256]{2,1,0:T(8,128)(2,1)S(1)}, u32[]{:S(2)}, u32[]{:S(2)}) collective-permute-start(bf16[2,256,256]{2,1,0:T(8,128)(2,1)S(1)} %pad_maximum_fusion.refs_0_), channel_id=1, source_target_pairs={{0,8},{4,12},{8,0},{12,4},{16,24},{20,28},{24,16},{28,20},{1,9},{5... | collective-permute-start | bytes 786440 | tf_op jit(solution)/shard_map/ppermute | solution.py:57
  8.4 0.0 copy-start.4
  8.4 0.0 copy-start.5
  8.4 0.6 copy-done.4
  9.1 0.0 copy-done.5
  9.1 0.1 pad_add_fusion.io_ref.idx
  9.2 2.6 %collective-permute-start.1 = (bf16[2,256,256]{2,1,0:T(8,128)(2,1)S(1)}, bf16[2,256,256]{2,1,0:T(8,128)(2,1)S(1)}, u32[]{:S(2)}, u32[]{:S(2)}) collective-permute-start(bf16[2,256,256]{2,1,0:T(8,128)(2,1)S(1)} %pad_maximum_fusion.refs_0_), channel_id=1, source_target_pairs={{0,16},{4,20},{8,24},{12,28},{16,0},{20,4},{24,8},{28,12},{1,17},{... | collective-permute-start | bytes 786440 | tf_op jit(solution)/shard_map/ppermute | solution.py:57
  11.7 1.0 %collective-permute-done.3.refs_1_ = bf16[2,256,256]{2,1,0:T(8,128)(2,1)S(1)} collective-permute-done((bf16[2,256,256]{2,1,0:T(8,128)(2,1)S(1)}, bf16[2,256,256]{2,1,0:T(8,128)(2,1)S(1)}, u32[]{:S(2)}, u32[]{:S(2)}) %collective-permute-start.3) | collective-permute-done | bytes 262176 | tf_op jit(solution)/shard_map/ppermute | solution.py:57
  12.8 5.6 %collective-permute-done.4.refs_2_ = bf16[2,256,256]{2,1,0:T(8,128)(2,1)S(1)} collective-permute-done((bf16[2,256,256]{2,1,0:T(8,128)(2,1)S(1)}, bf16[2,256,256]{2,1,0:T(8,128)(2,1)S(1)}, u32[]{:S(2)}, u32[]{:S(2)}) %collective-permute-start.4) | collective-permute-done | bytes 262176 | tf_op jit(solution)/shard_map/ppermute | solution.py:57
  18.4 0.4 collective-permute-start.5
  18.7 1.6 %collective-permute-start.10 = (bf16[256,512]{1,0:T(8,128)(2,1)S(1)}, bf16[256,512]{1,0:T(8,128)(2,1)S(1)}, u32[]{:S(2)}, u32[]{:S(2)}) collective-permute-start(bf16[256,512]{1,0:T(8,128)(2,1)S(1)} %copy-done.2), channel_id=1, source_target_pairs={{0,2},{1,3},{2,0},{3,1},{4,6},{5,7},{6,4},{7,5},{8,10},{9,11},{10,... | collective-permute-start | bytes 786440 | tf_op jit(solution)/shard_map/ppermute | solution.py:61
  20.4 0.5 collective-permute-start.11
  20.9 2.7 %collective-permute-done.1.refs_4_ = bf16[2,256,256]{2,1,0:T(8,128)(2,1)S(1)} collective-permute-done((bf16[2,256,256]{2,1,0:T(8,128)(2,1)S(1)}, bf16[2,256,256]{2,1,0:T(8,128)(2,1)S(1)}, u32[]{:S(2)}, u32[]{:S(2)}) %collective-permute-start.1) | collective-permute-done | bytes 262176 | tf_op jit(solution)/shard_map/ppermute | solution.py:57
  23.5 1.7 %collective-permute-done.5.refs_3_ = bf16[2,256,256]{2,1,0:T(8,128)(2,1)S(1)} collective-permute-done((bf16[2,256,256]{2,1,0:T(8,128)(2,1)S(1)}, bf16[2,256,256]{2,1,0:T(8,128)(2,1)S(1)}, u32[]{:S(2)}, u32[]{:S(2)}) %collective-permute-start.5) | collective-permute-done | bytes 262176 | tf_op jit(solution)/shard_map/ppermute | solution.py:57
  25.2 2.7 %collective-permute-done.10.refs_2_ = bf16[256,512]{1,0:T(8,128)(2,1)S(1)} collective-permute-done((bf16[256,512]{1,0:T(8,128)(2,1)S(1)}, bf16[256,512]{1,0:T(8,128)(2,1)S(1)}, u32[]{:S(2)}, u32[]{:S(2)}) %collective-permute-start.10) | collective-permute-done | bytes 262176 | tf_op jit(solution)/shard_map/ppermute | solution.py:61
  28.0 1.1 %collective-permute-start.6 = (bf16[2,256,256]{2,1,0:T(8,128)(2,1)S(1)}, bf16[2,256,256]{2,1,0:T(8,128)(2,1)S(1)}, u32[]{:S(2)}, u32[]{:S(2)}) collective-permute-start(bf16[2,256,256]{2,1,0:T(8,128)(2,1)S(1)} %collective-permute-done.1.refs_4_), channel_id=1, source_target_pairs={{0,4},{4,0},{8,12},{12,8},{16,20},{20,16},{24,28},{28,24},{1,5},{5... | collective-permute-start | bytes 786440 | tf_op jit(solution)/shard_map/ppermute | solution.py:57
  29.1 1.0 %collective-permute-done.11.refs_3_ = bf16[256,512]{1,0:T(8,128)(2,1)S(1)} collective-permute-done((bf16[256,512]{1,0:T(8,128)(2,1)S(1)}, bf16[256,512]{1,0:T(8,128)(2,1)S(1)}, u32[]{:S(2)}, u32[]{:S(2)}) %collective-permute-start.11) | collective-permute-done | bytes 262176 | tf_op jit(solution)/shard_map/ppermute | solution.py:61
  30.1 1.5 %collective-permute-start.7 = (s32[25]{0:T(128)S(1)}, s32[25]{0:T(128)S(1)}, u32[]{:S(2)}, u32[]{:S(2)}) collective-permute-start(s32[25]{0:T(128)S(1)} %pad_add_fusion.io_ref.idx), channel_id=1, source_target_pairs={{0,1},{1,0},{2,3},{3,2},{4,5},{5,4},{6,7},{7,6},{8,9},{9,8},{10,11... | collective-permute-start | bytes 308 | tf_op jit(solution)/shard_map/ppermute | solution.py:61
  31.5 0.8 collective-permute-done.7.ix_ref
  32.4 2.0 %collective-permute-done.6.refs_5_ = bf16[2,256,256]{2,1,0:T(8,128)(2,1)S(1)} collective-permute-done((bf16[2,256,256]{2,1,0:T(8,128)(2,1)S(1)}, bf16[2,256,256]{2,1,0:T(8,128)(2,1)S(1)}, u32[]{:S(2)}, u32[]{:S(2)}) %collective-permute-start.6) | collective-permute-done | bytes 262176 | tf_op jit(solution)/shard_map/ppermute | solution.py:57
  34.3 1.1 %collective-permute-start.12 = (bf16[2,256,256]{2,1,0:T(8,128)(2,1)S(1)}, bf16[2,256,256]{2,1,0:T(8,128)(2,1)S(1)}, u32[]{:S(2)}, u32[]{:S(2)}) collective-permute-start(bf16[2,256,256]{2,1,0:T(8,128)(2,1)S(1)} %collective-permute-done.2.refs_6_), channel_id=1, source_target_pairs={{0,4},{4,0},{8,12},{12,8},{16,20},{20,16},{24,28},{28,24},{1,5},{5... | collective-permute-start | bytes 786440 | tf_op jit(solution)/shard_map/ppermute | solution.py:57
  35.4 5.5 %collective-permute-done.12.refs_7_ = bf16[2,256,256]{2,1,0:T(8,128)(2,1)S(1)} collective-permute-done((bf16[2,256,256]{2,1,0:T(8,128)(2,1)S(1)}, bf16[2,256,256]{2,1,0:T(8,128)(2,1)S(1)}, u32[]{:S(2)}, u32[]{:S(2)}) %collective-permute-start.12) | collective-permute-done | bytes 262176 | tf_op jit(solution)/shard_map/ppermute | solution.py:57
  40.9 1.9 %forward_product.1 = (bf16[512,256]{1,0:T(8,128)(2,1)S(1)}, bf16[512,256]{1,0:T(8,128)(2,1)S(1)}) custom-call(s32[25]{0:T(128)S(1)} %pad_add_fusion.io_ref.idx, s32[25]{0:T(128)S(1)} %collective-permute-done.7.ix_ref, bf16[12,128,128]{2,1,0:T(8,128)(2,1)S(1)} %bitcast.19, bf16[12,128,128]{2,1,0:T(8,128)(2,1)S(1)} %collective-permute-done.8.ax_ref, ...), custom_call_target="tpu_custom_call" | custom-call | flops 201326592 | bytes 2097152 | tf_op jit(solution)/shard_map/forward_product/pallas_call | solution.py:100
  42.8 0.0 copy-start.3
  42.8 1.0 %collective-permute-start.15 = (bf16[512,256]{1,0:T(8,128)(2,1)S(1)}, bf16[512,256]{1,0:T(8,128)(2,1)S(1)}, u32[]{:S(2)}, u32[]{:S(2)}) collective-permute-start(bf16[512,256]{1,0:T(8,128)(2,1)S(1)} %get-tuple-element.56.refs_4_), channel_id=1, source_target_pairs={{0,2},{1,3},{2,0},{3,1},{4,6},{5,7},{6,4},{7,5},{8,10},{9,11},{10,... | collective-permute-start | bytes 786440 | tf_op jit(solution)/shard_map/ppermute | solution.py:61
  43.8 1.1 %collective-permute-start.16 = (bf16[512,256]{1,0:T(8,128)(2,1)S(1)}, bf16[512,256]{1,0:T(8,128)(2,1)S(1)}, u32[]{:S(2)}, u32[]{:S(2)}) collective-permute-start(bf16[512,256]{1,0:T(8,128)(2,1)S(1)} %get-tuple-element.57.refs_5_), channel_id=1, source_target_pairs={{0,2},{1,3},{2,0},{3,1},{4,6},{5,7},{6,4},{7,5},{8,10},{9,11},{10,... | collective-permute-start | bytes 786440 | tf_op jit(solution)/shard_map/ppermute | solution.py:61
  44.9 0.5 collective-permute-start.14
  45.4 6.0 %collective-permute-done.15.refs_8_ = bf16[512,256]{1,0:T(8,128)(2,1)S(1)} collective-permute-done((bf16[512,256]{1,0:T(8,128)(2,1)S(1)}, bf16[512,256]{1,0:T(8,128)(2,1)S(1)}, u32[]{:S(2)}, u32[]{:S(2)}) %collective-permute-start.15) | collective-permute-done | bytes 262176 | tf_op jit(solution)/shard_map/ppermute | solution.py:61
  51.4 2.8 %collective-permute-done.16.refs_9_ = bf16[512,256]{1,0:T(8,128)(2,1)S(1)} collective-permute-done((bf16[512,256]{1,0:T(8,128)(2,1)S(1)}, bf16[512,256]{1,0:T(8,128)(2,1)S(1)}, u32[]{:S(2)}, u32[]{:S(2)}) %collective-permute-start.16) | collective-permute-done | bytes 262176 | tf_op jit(solution)/shard_map/ppermute | solution.py:61
  54.2 1.5 %collective-permute-done.18.refs_11_ = bf16[512,256]{1,0:T(8,128)(2,1)S(1)} collective-permute-done((bf16[512,256]{1,0:T(8,128)(2,1)S(1)}, bf16[512,256]{1,0:T(8,128)(2,1)S(1)}, u32[]{:S(2)}, u32[]{:S(2)}) %collective-permute-start.18) | collective-permute-done | bytes 262176 | tf_op jit(solution)/shard_map/ppermute | solution.py:61
  55.7 6.0 %dense_and_backward.1 = (bf16[256,512]{1,0:T(8,128)(2,1)}, bf16[144,512]{1,0:T(8,128)(2,1)S(1)}, bf16[256,512]{1,0:T(8,128)(2,1)S(1)}, bf16[256,512]{1,0:T(8,128...) custom-call(bf16[512,512]{1,0:T(8,128)(2,1)S(1)} %copy-done.1, ...), custom_call_target="tpu_custom_call" | custom-call | flops 1342177280 | bytes 4194304 | tf_op jit(solution)/shard_map/dense_and_backward/pallas_call | solution.py:196
  61.7 0.1 collective-permute-start.19
  61.8 1.5 %collective-permute-start.21 = (bf16[256,512]{1,0:T(8,128)(2,1)S(1)}, bf16[256,512]{1,0:T(8,128)(2,1)S(1)}, u32[]{:S(2)}, u32[]{:S(2)}) collective-permute-start(bf16[256,512]{1,0:T(8,128)(2,1)S(1)} %get-tuple-element.64), channel_id=1, source_target_pairs={{0,4},{4,0},{8,12},{12,8},{16,20},{20,16},{24,28},{28,24},{1,5},{5... | collective-permute-start | bytes 786440 | tf_op jit(solution)/shard_map/ppermute | solution.py:57
  63.4 3.7 %collective-permute-done.19 = bf16[144,512]{1,0:T(8,128)(2,1)S(1)} collective-permute-done((bf16[144,512]{1,0:T(8,128)(2,1)S(1)}, bf16[144,512]{1,0:T(8,128)(2,1)S(1)}, u32[]{:S(2)}, u32[]{:S(2)}) %collective-permute-start.19) | collective-permute-done | bytes 147488 | tf_op jit(solution)/shard_map/ppermute | solution.py:57
  67.2 0.1 select_select_fusion.1
  67.3 2.1 %collective-permute-start.20 = (bf16[144,512]{1,0:T(8,128)(2,1)S(1)}, bf16[144,512]{1,0:T(8,128)(2,1)S(1)}, u32[]{:S(2)}, u32[]{:S(2)}) collective-permute-start(bf16[144,512]{1,0:T(8,128)(2,1)S(1)} %pad_maximum_fusion.2), channel_id=1, source_target_pairs={{0,16},{4,20},{8,24},{12,28},{16,0},{20,4},{24,8},{28,12},{1,17},{... | collective-permute-start | bytes 442376 | tf_op jit(solution)/shard_map/ppermute | solution.py:57
  69.4 0.3 collective-permute-done.21
  69.7 0.1 add_convert_fusion.2
  69.8 1.8 %collective-permute-start.22 = (bf16[256,512]{1,0:T(8,128)(2,1)S(1)}, bf16[256,512]{1,0:T(8,128)(2,1)S(1)}, u32[]{:S(2)}, u32[]{:S(2)}) collective-permute-start(bf16[256,512]{1,0:T(8,128)(2,1)S(1)} %get-tuple-element.66), channel_id=1, source_target_pairs={{0,4},{4,0},{8,12},{12,8},{16,20},{20,16},{24,28},{28,24},{1,5},{5... | collective-permute-start | bytes 786440 | tf_op jit(solution)/shard_map/ppermute | solution.py:57
  71.6 1.7 %collective-permute-start.23 = (bf16[256,512]{1,0:T(8,128)(2,1)S(1)}, bf16[256,512]{1,0:T(8,128)(2,1)S(1)}, u32[]{:S(2)}, u32[]{:S(2)}) collective-permute-start(bf16[256,512]{1,0:T(8,128)(2,1)S(1)} %add_convert_fusion.2), channel_id=1, source_target_pairs={{0,8},{4,12},{8,0},{12,4},{16,24},{20,28},{24,16},{28,20},{1,9},{5... | collective-permute-start | bytes 786440 | tf_op jit(solution)/shard_map/ppermute | solution.py:57
  73.2 3.3 %collective-permute-done.20 = bf16[144,512]{1,0:T(8,128)(2,1)S(1)} collective-permute-done((bf16[144,512]{1,0:T(8,128)(2,1)S(1)}, bf16[144,512]{1,0:T(8,128)(2,1)S(1)}, u32[]{:S(2)}, u32[]{:S(2)}) %collective-permute-start.20) | collective-permute-done | bytes 147488 | tf_op jit(solution)/shard_map/ppermute | solution.py:57
  76.6 0.1 select_select_fusion
  76.7 1.6 %collective-permute-start.29 = (bf16[256,512]{1,0:T(8,128)(2,1)S(1)}, bf16[256,512]{1,0:T(8,128)(2,1)S(1)}, u32[]{:S(2)}, u32[]{:S(2)}) collective-permute-start(bf16[256,512]{1,0:T(8,128)(2,1)S(1)} %get-tuple-element.75), channel_id=1, source_target_pairs={{0,4},{4,0},{8,12},{12,8},{16,20},{20,16},{24,28},{28,24},{1,5},{5... | collective-permute-start | bytes 786440 | tf_op jit(solution)/shard_map/ppermute | solution.py:57
  78.3 2.3 %collective-permute-done.23 = bf16[256,512]{1,0:T(8,128)(2,1)S(1)} collective-permute-done((bf16[256,512]{1,0:T(8,128)(2,1)S(1)}, bf16[256,512]{1,0:T(8,128)(2,1)S(1)}, u32[]{:S(2)}, u32[]{:S(2)}) %collective-permute-start.23) | collective-permute-done | bytes 262176 | tf_op jit(solution)/shard_map/ppermute | solution.py:57
  80.6 0.1 convert_add_fusion
  80.7 1.6 %collective-permute-start.24 = (bf16[144,512]{1,0:T(8,128)(2,1)S(1)}, bf16[144,512]{1,0:T(8,128)(2,1)S(1)}, u32[]{:S(2)}, u32[]{:S(2)}) collective-permute-start(bf16[144,512]{1,0:T(8,128)(2,1)S(1)} %pad_maximum_fusion.3), channel_id=1, source_target_pairs={{0,4},{4,0},{8,12},{12,8},{16,20},{20,16},{24,28},{28,24},{1,5},{5... | collective-permute-start | bytes 442376 | tf_op jit(solution)/shard_map/ppermute | solution.py:57
  82.3 0.7 collective-permute-start.28
  83.0 3.0 %collective-permute-done.29 = bf16[256,512]{1,0:T(8,128)(2,1)S(1)} collective-permute-done((bf16[256,512]{1,0:T(8,128)(2,1)S(1)}, bf16[256,512]{1,0:T(8,128)(2,1)S(1)}, u32[]{:S(2)}, u32[]{:S(2)}) %collective-permute-start.29) | collective-permute-done | bytes 262176 | tf_op jit(solution)/shard_map/ppermute | solution.py:57
  86.0 0.1 add_convert_fusion.1
  86.1 0.7 collective-permute-start.30
  86.7 1.1 %collective-permute-done.24 = bf16[144,512]{1,0:T(8,128)(2,1)S(1)} collective-permute-done((bf16[144,512]{1,0:T(8,128)(2,1)S(1)}, bf16[144,512]{1,0:T(8,128)(2,1)S(1)}, u32[]{:S(2)}, u32[]{:S(2)}) %collective-permute-start.24) | collective-permute-done | bytes 147488 | tf_op jit(solution)/shard_map/ppermute | solution.py:57
  87.8 1.7 %collective-permute-start.27 = (bf16[256,512]{1,0:T(8,128)(2,1)S(1)}, bf16[256,512]{1,0:T(8,128)(2,1)S(1)}, u32[]{:S(2)}, u32[]{:S(2)}) collective-permute-start(bf16[256,512]{1,0:T(8,128)(2,1)S(1)} %get-tuple-element.72), channel_id=1, source_target_pairs={{0,4},{4,0},{8,12},{12,8},{16,20},{20,16},{24,28},{28,24},{1,5},{5... | collective-permute-start | bytes 786440 | tf_op jit(solution)/shard_map/ppermute | solution.py:57
  89.6 0.4 collective-permute-start.25
  90.0 4.6 %collective-permute-done.25.refs_1_ = bf16[128,512]{1,0:T(8,128)(2,1)S(1)} collective-permute-done((bf16[128,512]{1,0:T(8,128)(2,1)S(1)}, bf16[128,512]{1,0:T(8,128)(2,1)S(1)}, u32[]{:S(2)}, u32[]{:S(2)}) %collective-permute-start.25) | collective-permute-done | bytes 131104 | tf_op jit(solution)/shard_map/ppermute | solution.py:61
  94.7 0.1 collective-permute-start.26
  94.8 0.6 slice_add_fusion
  95.4 1.2 %collective-permute-done.30 = bf16[256,512]{1,0:T(8,128)(2,1)S(1)} collective-permute-done((bf16[256,512]{1,0:T(8,128)(2,1)S(1)}, bf16[256,512]{1,0:T(8,128)(2,1)S(1)}, u32[]{:S(2)}, u32[]{:S(2)}) %collective-permute-start.30) | collective-permute-done | bytes 262176 | tf_op jit(solution)/shard_map/ppermute | solution.py:57
  96.5 0.8 add_convert_fusion
  97.4 1.1 %place_weight_gradient.1 = f32[512,512]{1,0:T(8,128)} custom-call(bf16[128,512]{1,0:T(8,128)(2,1)S(1)} %slice.97.refs_0_, bf16[128,512]{1,0:T(8,128)(2,1)S(1)} %collective-permute-done.25.refs_1_, bf16[128,512]{1,0:T(8,128)(2,1)S(1)} %get-tuple-element.81.refs_2_, bf16[128,512]{1,0:T(8,128)(2,1)S(1)} %get-tuple-element.80.refs_3_), custom_call_target="tpu_custom_call" | custom-call | flops 262144 | bytes 1572864 | tf_op jit(solution)/shard_map/place_weight_gradient/pallas_call | solution.py:233
  (37 shorter events, 0.4 us)
Async XLA Ops:
  0.6 18.1 %copy-start.2 = (bf16[256,512]{1,0:T(8,128)(2,1)S(1)}, bf16[256,512]{1,0:T(8,128)(2,1)}, u32[]{:S(2)}) copy-start(bf16[256,512]{1,0:T(8,128)(2,1)} %refs_0_) | copy-start | bytes 786436
  1.7 18.7 %copy-start = (bf16[1,1,12,128,128]{4,3,2,1,0:T(8,128)(2,1)S(1)}, bf16[1,1,12,128,128]{4,3,2,1,0:T(8,128)(2,1)}, u32[]{:S(2)}) copy-start(bf16[1,1,12,128,128]{4,3,2,1,0:T(8,128)(2,1)} %param.9) | copy-start | bytes 1179652
  1.7 1.5 %collective-permute-start = (bf16[256,256]{1,0:T(8,128)(2,1)S(1)}, bf16[256,256]{1,0:T(8,128)(2,1)S(1)}, u32[]{:S(2)}, u32[]{:S(2)}) collective-permute-start(bf16[256,256]{1,0:T(8,128)(2,1)S(1)} %get-tuple-element.83), channel_id=1, source_target_pairs={{0,1},{1,0},{2,3},{3,2},{4,5},{5,4},{6,7},{7,6},{8,9},{9,8},{10,11... | collective-permute-start | bytes 393224 | tf_op jit(solution)/shard_map/ppermute | solution.py:61
  3.2 9.6 %collective-permute-start.3 = (bf16[2,256,256]{2,1,0:T(8,128)(2,1)S(1)}, bf16[2,256,256]{2,1,0:T(8,128)(2,1)S(1)}, u32[]{:S(2)}, u32[]{:S(2)}) collective-permute-start(bf16[2,256,256]{2,1,0:T(8,128)(2,1)S(1)} %pad_maximum_fusion.refs_0_), channel_id=1, source_target_pairs={{0,4},{4,0},{8,12},{12,8},{16,20},{20,16},{24,28},{28,24},{1,5},{5... | collective-permute-start | bytes 786440 | tf_op jit(solution)/shard_map/ppermute | solution.py:57
  6.2 12.2 %collective-permute-start.4 = (bf16[2,256,256]{2,1,0:T(8,128)(2,1)S(1)}, bf16[2,256,256]{2,1,0:T(8,128)(2,1)S(1)}, u32[]{:S(2)}, u32[]{:S(2)}) collective-permute-start(bf16[2,256,256]{2,1,0:T(8,128)(2,1)S(1)} %pad_maximum_fusion.refs_0_), channel_id=1, source_target_pairs={{0,8},{4,12},{8,0},{12,4},{16,24},{20,28},{24,16},{28,20},{1,9},{5... | collective-permute-start | bytes 786440 | tf_op jit(solution)/shard_map/ppermute | solution.py:57
  8.4 0.7 copy-start.4
  8.4 0.7 copy-start.5
  9.2 14.4 %collective-permute-start.1 = (bf16[2,256,256]{2,1,0:T(8,128)(2,1)S(1)}, bf16[2,256,256]{2,1,0:T(8,128)(2,1)S(1)}, u32[]{:S(2)}, u32[]{:S(2)}) collective-permute-start(bf16[2,256,256]{2,1,0:T(8,128)(2,1)S(1)} %pad_maximum_fusion.refs_0_), channel_id=1, source_target_pairs={{0,16},{4,20},{8,24},{12,28},{16,0},{20,4},{24,8},{28,12},{1,17},{... | collective-permute-start | bytes 786440 | tf_op jit(solution)/shard_map/ppermute | solution.py:57
  18.4 37.4 %copy-start.1 = (bf16[512,512]{1,0:T(8,128)(2,1)S(1)}, bf16[512,512]{1,0:T(8,128)(2,1)}, u32[]{:S(2)}) copy-start(bf16[512,512]{1,0:T(8,128)(2,1)} %w_ref.1) | copy-start | bytes 1572868
  18.4 6.9 %collective-permute-start.5 = (bf16[2,256,256]{2,1,0:T(8,128)(2,1)S(1)}, bf16[2,256,256]{2,1,0:T(8,128)(2,1)S(1)}, u32[]{:S(2)}, u32[]{:S(2)}) collective-permute-start(bf16[2,256,256]{2,1,0:T(8,128)(2,1)S(1)} %collective-permute-done.4.refs_2_), channel_id=1, source_target_pairs={{0,4},{4,0},{8,12},{12,8},{16,20},{20,16},{24,28},{28,24},{1,5},{5... | collective-permute-start | bytes 786440 | tf_op jit(solution)/shard_map/ppermute | solution.py:57
  18.7 9.2 %collective-permute-start.10 = (bf16[256,512]{1,0:T(8,128)(2,1)S(1)}, bf16[256,512]{1,0:T(8,128)(2,1)S(1)}, u32[]{:S(2)}, u32[]{:S(2)}) collective-permute-start(bf16[256,512]{1,0:T(8,128)(2,1)S(1)} %copy-done.2), channel_id=1, source_target_pairs={{0,2},{1,3},{2,0},{3,1},{4,6},{5,7},{6,4},{7,5},{8,10},{9,11},{10,... | collective-permute-start | bytes 786440 | tf_op jit(solution)/shard_map/ppermute | solution.py:61
  20.4 12.0 %collective-permute-start.8 = (bf16[12,128,128]{2,1,0:T(8,128)(2,1)S(1)}, bf16[12,128,128]{2,1,0:T(8,128)(2,1)S(1)}, u32[]{:S(2)}, u32[]{:S(2)}) collective-permute-start(bf16[12,128,128]{2,1,0:T(8,128)(2,1)S(1)} %bitcast.18), channel_id=1, source_target_pairs={{0,1},{1,0},{2,3},{3,2},{4,5},{5,4},{6,7},{7,6},{8,9},{9,8},{10,11... | collective-permute-start | bytes 1179656 | tf_op jit(solution)/shard_map/ppermute | solution.py:61
  20.4 9.7 %collective-permute-start.11 = (bf16[256,512]{1,0:T(8,128)(2,1)S(1)}, bf16[256,512]{1,0:T(8,128)(2,1)S(1)}, u32[]{:S(2)}, u32[]{:S(2)}) collective-permute-start(bf16[256,512]{1,0:T(8,128)(2,1)S(1)} %copy-done.2), channel_id=1, source_target_pairs={{0,3},{1,2},{2,1},{3,0},{4,7},{5,6},{6,5},{7,4},{8,11},{9,10},{10,... | collective-permute-start | bytes 786440 | tf_op jit(solution)/shard_map/ppermute | solution.py:61
  23.5 8.8 %collective-permute-start.9 = (bf16[256,512]{1,0:T(8,128)(2,1)S(1)}, bf16[256,512]{1,0:T(8,128)(2,1)S(1)}, u32[]{:S(2)}, u32[]{:S(2)}) collective-permute-start(bf16[256,512]{1,0:T(8,128)(2,1)S(1)} %copy-done.2), channel_id=1, source_target_pairs={{0,1},{1,0},{2,3},{3,2},{4,5},{5,4},{6,7},{7,6},{8,9},{9,8},{10,11... | collective-permute-start | bytes 786440 | tf_op jit(solution)/shard_map/ppermute | solution.py:61
  25.2 7.1 %collective-permute-start.2 = (bf16[2,256,256]{2,1,0:T(8,128)(2,1)S(1)}, bf16[2,256,256]{2,1,0:T(8,128)(2,1)S(1)}, u32[]{:S(2)}, u32[]{:S(2)}) collective-permute-start(bf16[2,256,256]{2,1,0:T(8,128)(2,1)S(1)} %collective-permute-done.1.refs_4_), channel_id=1, source_target_pairs={{0,8},{4,12},{8,0},{12,4},{16,24},{20,28},{24,16},{28,20},{1,9},{5... | collective-permute-start | bytes 786440 | tf_op jit(solution)/shard_map/ppermute | solution.py:57
  28.0 6.4 %collective-permute-start.6 = (bf16[2,256,256]{2,1,0:T(8,128)(2,1)S(1)}, bf16[2,256,256]{2,1,0:T(8,128)(2,1)S(1)}, u32[]{:S(2)}, u32[]{:S(2)}) collective-permute-start(bf16[2,256,256]{2,1,0:T(8,128)(2,1)S(1)} %collective-permute-done.1.refs_4_), channel_id=1, source_target_pairs={{0,4},{4,0},{8,12},{12,8},{16,20},{20,16},{24,28},{28,24},{1,5},{5... | collective-permute-start | bytes 786440 | tf_op jit(solution)/shard_map/ppermute | solution.py:57
  30.1 2.3 %collective-permute-start.7 = (s32[25]{0:T(128)S(1)}, s32[25]{0:T(128)S(1)}, u32[]{:S(2)}, u32[]{:S(2)}) collective-permute-start(s32[25]{0:T(128)S(1)} %pad_add_fusion.io_ref.idx), channel_id=1, source_target_pairs={{0,1},{1,0},{2,3},{3,2},{4,5},{5,4},{6,7},{7,6},{8,9},{9,8},{10,11... | collective-permute-start | bytes 308 | tf_op jit(solution)/shard_map/ppermute | solution.py:61
  34.3 6.6 %collective-permute-start.12 = (bf16[2,256,256]{2,1,0:T(8,128)(2,1)S(1)}, bf16[2,256,256]{2,1,0:T(8,128)(2,1)S(1)}, u32[]{:S(2)}, u32[]{:S(2)}) collective-permute-start(bf16[2,256,256]{2,1,0:T(8,128)(2,1)S(1)} %collective-permute-done.2.refs_6_), channel_id=1, source_target_pairs={{0,4},{4,0},{8,12},{12,8},{16,20},{20,16},{24,28},{28,24},{1,5},{5... | collective-permute-start | bytes 786440 | tf_op jit(solution)/shard_map/ppermute | solution.py:57
  42.8 12.9 %copy-start.3 = (f32[512]{0:T(512)S(1)}, f32[512]{0:T(512)}, u32[]{:S(2)}) copy-start(f32[512]{0:T(512)} %param.14) | copy-start | bytes 6148
  42.8 8.6 %collective-permute-start.15 = (bf16[512,256]{1,0:T(8,128)(2,1)S(1)}, bf16[512,256]{1,0:T(8,128)(2,1)S(1)}, u32[]{:S(2)}, u32[]{:S(2)}) collective-permute-start(bf16[512,256]{1,0:T(8,128)(2,1)S(1)} %get-tuple-element.56.refs_4_), channel_id=1, source_target_pairs={{0,2},{1,3},{2,0},{3,1},{4,6},{5,7},{6,4},{7,5},{8,10},{9,11},{10,... | collective-permute-start | bytes 786440 | tf_op jit(solution)/shard_map/ppermute | solution.py:61
  43.8 10.4 %collective-permute-start.16 = (bf16[512,256]{1,0:T(8,128)(2,1)S(1)}, bf16[512,256]{1,0:T(8,128)(2,1)S(1)}, u32[]{:S(2)}, u32[]{:S(2)}) collective-permute-start(bf16[512,256]{1,0:T(8,128)(2,1)S(1)} %get-tuple-element.57.refs_5_), channel_id=1, source_target_pairs={{0,2},{1,3},{2,0},{3,1},{4,6},{5,7},{6,4},{7,5},{8,10},{9,11},{10,... | collective-permute-start | bytes 786440 | tf_op jit(solution)/shard_map/ppermute | solution.py:61
  44.9 9.3 %collective-permute-start.13 = (bf16[512,256]{1,0:T(8,128)(2,1)S(1)}, bf16[512,256]{1,0:T(8,128)(2,1)S(1)}, u32[]{:S(2)}, u32[]{:S(2)}) collective-permute-start(bf16[512,256]{1,0:T(8,128)(2,1)S(1)} %get-tuple-element.56.refs_4_), channel_id=1, source_target_pairs={{0,1},{1,0},{2,3},{3,2},{4,5},{5,4},{6,7},{7,6},{8,9},{9,8},{10,11... | collective-permute-start | bytes 786440 | tf_op jit(solution)/shard_map/ppermute | solution.py:61
  44.9 9.3 %collective-permute-start.14 = (bf16[512,256]{1,0:T(8,128)(2,1)S(1)}, bf16[512,256]{1,0:T(8,128)(2,1)S(1)}, u32[]{:S(2)}, u32[]{:S(2)}) collective-permute-start(bf16[512,256]{1,0:T(8,128)(2,1)S(1)} %get-tuple-element.57.refs_5_), channel_id=1, source_target_pairs={{0,1},{1,0},{2,3},{3,2},{4,5},{5,4},{6,7},{7,6},{8,9},{9,8},{10,11... | collective-permute-start | bytes 786440 | tf_op jit(solution)/shard_map/ppermute | solution.py:61
  51.4 2.8 %collective-permute-start.17 = (bf16[512,256]{1,0:T(8,128)(2,1)S(1)}, bf16[512,256]{1,0:T(8,128)(2,1)S(1)}, u32[]{:S(2)}, u32[]{:S(2)}) collective-permute-start(bf16[512,256]{1,0:T(8,128)(2,1)S(1)} %collective-permute-done.15.refs_8_), channel_id=1, source_target_pairs={{0,1},{1,0},{2,3},{3,2},{4,5},{5,4},{6,7},{7,6},{8,9},{9,8},{10,11... | collective-permute-start | bytes 786440 | tf_op jit(solution)/shard_map/ppermute | solution.py:61
  54.2 1.5 %collective-permute-start.18 = (bf16[512,256]{1,0:T(8,128)(2,1)S(1)}, bf16[512,256]{1,0:T(8,128)(2,1)S(1)}, u32[]{:S(2)}, u32[]{:S(2)}) collective-permute-start(bf16[512,256]{1,0:T(8,128)(2,1)S(1)} %collective-permute-done.16.refs_9_), channel_id=1, source_target_pairs={{0,1},{1,0},{2,3},{3,2},{4,5},{5,4},{6,7},{7,6},{8,9},{9,8},{10,11... | collective-permute-start | bytes 786440 | tf_op jit(solution)/shard_map/ppermute | solution.py:61
  61.7 5.3 %collective-permute-start.19 = (bf16[144,512]{1,0:T(8,128)(2,1)S(1)}, bf16[144,512]{1,0:T(8,128)(2,1)S(1)}, u32[]{:S(2)}, u32[]{:S(2)}) collective-permute-start(bf16[144,512]{1,0:T(8,128)(2,1)S(1)} %get-tuple-element.59), channel_id=1, source_target_pairs={{0,8},{4,12},{8,0},{12,4},{16,24},{20,28},{24,16},{28,20},{1,9},{5... | collective-permute-start | bytes 442376 | tf_op jit(solution)/shard_map/ppermute | solution.py:57
  61.8 7.9 %collective-permute-start.21 = (bf16[256,512]{1,0:T(8,128)(2,1)S(1)}, bf16[256,512]{1,0:T(8,128)(2,1)S(1)}, u32[]{:S(2)}, u32[]{:S(2)}) collective-permute-start(bf16[256,512]{1,0:T(8,128)(2,1)S(1)} %get-tuple-element.64), channel_id=1, source_target_pairs={{0,4},{4,0},{8,12},{12,8},{16,20},{20,16},{24,28},{28,24},{1,5},{5... | collective-permute-start | bytes 786440 | tf_op jit(solution)/shard_map/ppermute | solution.py:57
  67.3 9.3 %collective-permute-start.20 = (bf16[144,512]{1,0:T(8,128)(2,1)S(1)}, bf16[144,512]{1,0:T(8,128)(2,1)S(1)}, u32[]{:S(2)}, u32[]{:S(2)}) collective-permute-start(bf16[144,512]{1,0:T(8,128)(2,1)S(1)} %pad_maximum_fusion.2), channel_id=1, source_target_pairs={{0,16},{4,20},{8,24},{12,28},{16,0},{20,4},{24,8},{28,12},{1,17},{... | collective-permute-start | bytes 442376 | tf_op jit(solution)/shard_map/ppermute | solution.py:57
  69.8 8.5 %collective-permute-start.22 = (bf16[256,512]{1,0:T(8,128)(2,1)S(1)}, bf16[256,512]{1,0:T(8,128)(2,1)S(1)}, u32[]{:S(2)}, u32[]{:S(2)}) collective-permute-start(bf16[256,512]{1,0:T(8,128)(2,1)S(1)} %get-tuple-element.66), channel_id=1, source_target_pairs={{0,4},{4,0},{8,12},{12,8},{16,20},{20,16},{24,28},{28,24},{1,5},{5... | collective-permute-start | bytes 786440 | tf_op jit(solution)/shard_map/ppermute | solution.py:57
  71.6 9.0 %collective-permute-start.23 = (bf16[256,512]{1,0:T(8,128)(2,1)S(1)}, bf16[256,512]{1,0:T(8,128)(2,1)S(1)}, u32[]{:S(2)}, u32[]{:S(2)}) collective-permute-start(bf16[256,512]{1,0:T(8,128)(2,1)S(1)} %add_convert_fusion.2), channel_id=1, source_target_pairs={{0,8},{4,12},{8,0},{12,4},{16,24},{20,28},{24,16},{28,20},{1,9},{5... | collective-permute-start | bytes 786440 | tf_op jit(solution)/shard_map/ppermute | solution.py:57
  76.7 9.3 %collective-permute-start.29 = (bf16[256,512]{1,0:T(8,128)(2,1)S(1)}, bf16[256,512]{1,0:T(8,128)(2,1)S(1)}, u32[]{:S(2)}, u32[]{:S(2)}) collective-permute-start(bf16[256,512]{1,0:T(8,128)(2,1)S(1)} %get-tuple-element.75), channel_id=1, source_target_pairs={{0,4},{4,0},{8,12},{12,8},{16,20},{20,16},{24,28},{28,24},{1,5},{5... | collective-permute-start | bytes 786440 | tf_op jit(solution)/shard_map/ppermute | solution.py:57
  80.7 7.1 %collective-permute-start.24 = (bf16[144,512]{1,0:T(8,128)(2,1)S(1)}, bf16[144,512]{1,0:T(8,128)(2,1)S(1)}, u32[]{:S(2)}, u32[]{:S(2)}) collective-permute-start(bf16[144,512]{1,0:T(8,128)(2,1)S(1)} %pad_maximum_fusion.3), channel_id=1, source_target_pairs={{0,4},{4,0},{8,12},{12,8},{16,20},{20,16},{24,28},{28,24},{1,5},{5... | collective-permute-start | bytes 442376 | tf_op jit(solution)/shard_map/ppermute | solution.py:57
  82.3 13.1 %collective-permute-start.28 = (bf16[256,512]{1,0:T(8,128)(2,1)S(1)}, bf16[256,512]{1,0:T(8,128)(2,1)S(1)}, u32[]{:S(2)}, u32[]{:S(2)}) collective-permute-start(bf16[256,512]{1,0:T(8,128)(2,1)S(1)} %convert_add_fusion), channel_id=1, source_target_pairs={{0,16},{4,20},{8,24},{12,28},{16,0},{20,4},{24,8},{28,12},{1,17},{... | collective-permute-start | bytes 786440 | tf_op jit(solution)/shard_map/ppermute | solution.py:57
  86.1 10.4 %collective-permute-start.30 = (bf16[256,512]{1,0:T(8,128)(2,1)S(1)}, bf16[256,512]{1,0:T(8,128)(2,1)S(1)}, u32[]{:S(2)}, u32[]{:S(2)}) collective-permute-start(bf16[256,512]{1,0:T(8,128)(2,1)S(1)} %add_convert_fusion.1), channel_id=1, source_target_pairs={{0,8},{4,12},{8,0},{12,4},{16,24},{20,28},{24,16},{28,20},{1,9},{5... | collective-permute-start | bytes 786440 | tf_op jit(solution)/shard_map/ppermute | solution.py:57
  87.8 8.7 %collective-permute-start.27 = (bf16[256,512]{1,0:T(8,128)(2,1)S(1)}, bf16[256,512]{1,0:T(8,128)(2,1)S(1)}, u32[]{:S(2)}, u32[]{:S(2)}) collective-permute-start(bf16[256,512]{1,0:T(8,128)(2,1)S(1)} %get-tuple-element.72), channel_id=1, source_target_pairs={{0,4},{4,0},{8,12},{12,8},{16,20},{20,16},{24,28},{28,24},{1,5},{5... | collective-permute-start | bytes 786440 | tf_op jit(solution)/shard_map/ppermute | solution.py:57
  89.6 5.0 %collective-permute-start.25 = (bf16[128,512]{1,0:T(8,128)(2,1)S(1)}, bf16[128,512]{1,0:T(8,128)(2,1)S(1)}, u32[]{:S(2)}, u32[]{:S(2)}) collective-permute-start(bf16[128,512]{1,0:T(8,128)(2,1)S(1)} %slice.97.refs_0_), channel_id=1, source_target_pairs={{0,2},{1,3},{2,0},{3,1},{4,6},{5,7},{6,4},{7,5},{8,10},{9,11},{10,... | collective-permute-start | bytes 393224 | tf_op jit(solution)/shard_map/ppermute | solution.py:61
  94.7 2.7 %collective-permute-start.26 = (bf16[2,128,512]{2,1,0:T(8,128)(2,1)S(1)}, bf16[2,128,512]{2,1,0:T(8,128)(2,1)S(1)}, u32[]{:S(2)}, u32[]{:S(2)}) collective-permute-start(bf16[2,128,512]{2,1,0:T(8,128)(2,1)S(1)} %pad_maximum_fusion.1), channel_id=1, source_target_pairs={{0,1},{1,0},{2,3},{3,2},{4,5},{5,4},{6,7},{7,6},{8,9},{9,8},{10,11... | collective-permute-start | bytes 786440 | tf_op jit(solution)/shard_map/ppermute | solution.py:61

commit v4 on v3

--- a/solution.py
+++ b/solution.py
@@ -113,7 +113,7 @@
     )(index_own, index_other, tiles_own, tiles_other, *pieces)
 
 
-def dense_and_backward(lay, sums, weight, bias, index_own, tiles_own, ups):
+def dense_and_backward(lay, sums, weight, bias, index_own, tiles_own, ups, ups_other):
     node_dev, width = ups[0].shape
     rows, half = node_dev * lay.cols, width // 2
     share = half // lay.pairs
@@ -123,7 +123,8 @@
     n_sums = len(sums)
 
     def kernel(w_ref, b_ref, idx, tiles, *refs):
-        up_refs, sum_refs, refs = refs[: lay.cols], refs[lay.cols :][:n_sums], refs[lay.cols + n_sums :]
+        n_ups = lay.pairs + 1
+        up_refs, sum_refs, refs = refs[:n_ups], refs[n_ups:][:n_sums], refs[n_ups + n_sums :]
         act_ref, gw_ref, refs = refs[0], refs[1], refs[2:]
         out_refs, (up_all, parts, hidden, gw, dh_ref, total, sems) = refs[: lay.rows], refs[lay.rows :]
         row, col = lax.axis_index("row"), lax.axis_index("col")
@@ -131,7 +132,8 @@
         copies = []
         for d in range(lay.cols):
             at = pl.multiple_of(xor_to(col, d) * node_dev, node_dev)
-            copies.append(pltpu.make_async_copy(up_refs[d], up_all.at[pl.ds(at, node_dev), :], sems.at[d]))
+            ref = up_refs[-1].at[d // 2] if d % 2 else up_refs[d // 2]
+            copies.append(pltpu.make_async_copy(ref, up_all.at[pl.ds(at, node_dev), :], sems.at[d]))
         for n, ref in enumerate(sum_refs):
             part, dk, dx = n % 2, n // 2 % 2, n // 4
             at = pl.multiple_of(xor_to(core, dk) * half, half)
@@ -200,7 +202,7 @@
             jax.ShapeDtypeStruct((share + EXTRA_ROWS, width), BF16),
         ]
         + [jax.ShapeDtypeStruct((node_dev, width), BF16)] * lay.rows,
-        in_specs=[vmem(), vmem(), smem(), vmem()] + [hbm()] * (lay.cols + n_sums),
+        in_specs=[vmem(), vmem(), smem(), vmem()] + [hbm()] * (lay.pairs + 1 + n_sums),
         out_specs=[vmem()] * (2 + lay.rows),
         scratch_shapes=[
             pltpu.VMEM((rows, width), BF16),
@@ -214,7 +216,7 @@
         compiler_params=params(),
         cost_estimate=cost(5 * rows * width * width, 8 * rows * width),
         name="dense_and_backward",
-    )(weight, bias, index_own, tiles_own, *ups, *sums)
+    )(weight, bias, index_own, tiles_own, *ups, ups_other, *sums)
 
 
 def place_weight_gradient(lay, own, other, width):
@@ -258,11 +260,8 @@
     tiles = blocks[0, 0]
     core = lax.axis_index("col") % 2
 
-    index = jnp.concatenate([block_rows[0, 0], block_cols[0, 0], block_count[0]])
-    low, high = features[:, :half], features[:, half:]
-    keep = jnp.where(core == 0, low, high)
-    give = jnp.where(core == 0, high, low)
-    piece = jnp.stack([keep, lay.move_col(give, core=1)])
+    mine = [jnp.where(core == 0, a[:, :half], a[:, half:]) for a in (features, lay.move_col(features, core=1))]
+    piece = jnp.stack(mine)
 
     piece, upstream = lax.optimization_barrier((piece, upstream))
     gathered = {0: piece}
@@ -278,20 +277,22 @@
         if dz & (dz - 1) == 0:
             gathered[dz * lay.fast] = lay.move_row(piece, slow=dz)
     over_fast(0)
-    far_ups = [lay.move_col(upstream, pair=dx, core=dk) for dx in range(1, lay.pairs) for dk in range(2)]
+    ups = [upstream] + [lay.move_col(upstream, pair=dx) for dx in range(1, lay.pairs)]
     one = lay.fast if lay.slow > 1 else 0
-    near, gathered[one], own_upstream, own_index, own_tiles = lax.optimization_barrier(
-        (over_fast_of(0), gathered[one], upstream, index, tiles)
+    near, gathered[one], later = lax.optimization_barrier(
+        (over_fast_of(0), gathered[one], (block_rows, block_cols, block_count, tiles))
     )
+    block_rows, block_cols, block_count, tiles = later
+    index = jnp.concatenate([block_rows[0, 0], block_cols[0, 0], block_count[0]])
     gathered.update(zip(range(1, lay.fast), near))
-    index_other = lay.move_col(own_index, core=1)
-    tiles_other = lay.move_col(own_tiles, core=1)
-    near_up = lay.move_col(own_upstream, core=1)
+    index_other = lay.move_col(index, core=1)
+    tiles_other = lay.move_col(tiles, core=1)
+    ups_other = lay.move_col(jnp.stack(ups), core=1)
     for dz in range(1, lay.slow):
         top = 1 << (dz.bit_length() - 1)
         if dz != top:
             gathered[dz * lay.fast] = lay.move_row(gathered[top * lay.fast], slow=dz ^ top)
-    others = (index_other, tiles_other, near_up, far_ups)
+    others = (index_other, tiles_other, ups_other)
     for dz in range(1, lay.slow):
         over_fast(dz)
         if dz < lay.slow - 1:
@@ -300,8 +301,7 @@
             gathered[after], done, extra = lax.optimization_barrier((gathered[after], over_fast_of(dz), extra))
             gathered.update(zip(range(dz * lay.fast + 1, after), done))
             others = extra or others
-    index_other, tiles_other, near_up, far_ups = others
-    ups = [upstream, near_up] + list(far_ups)
+    index_other, tiles_other, ups_other = others
     pieces = [gathered[d] for d in range(lay.rows)]
 
     mine = forward_product(lay, index, index_other, tiles, tiles_other, pieces, node_dev * lay.cols)
@@ -311,7 +311,7 @@
         sums += came + [lay.move_col(a, core=1) for a in came]
 
     activated, gw, *outs = dense_and_backward(
-        lay, sums, weight, bias_vector[None], index, tiles, ups
+        lay, sums, weight, bias_vector[None], index, tiles, ups, ups_other
     )
 
     def fast_arrivals(dz):

time: 99.5 us -> 95.5 us (0.960); the launches traced: 98.5 us -> 95.5 us
  starting transfers between devices: 30.3 us -> 27.1 us
    ppermute x17, waiting for transfers between devices: 33.4 us -> 40.8 us  [move_row(): return lax.ppermute(a, 'row', [(r, r ^ d) for r in range(self.rows)])]
    ppermute x14 -> x13, waiting for transfers between devices: 20.5 us -> 13.3 us  [move_col(): return lax.ppermute(a, 'col', [(c, c ^ d) for c in range(self.cols)])]
    ppermute x17, starting transfers between devices: 23.1 us -> 17.9 us  [move_row(): return lax.ppermute(a, 'row', [(r, r ^ d) for r in range(self.rows)])]
    ppermute x14 -> x13, starting transfers between devices: 7.19 us -> 9.14 us  [move_col(): return lax.ppermute(a, 'col', [(c, c ^ d) for c in range(self.cols)])]
  transfers between devices with their start and end apart: 31 -> 30, of which waited for: 21 -> 21; matrix products, arithmetic and copies ran while one was open for 2% -> 3% of each run, Pallas kernels for 0% -> 0%
where the time goes in v4:
time: 95.5 us
  waiting for transfers between devices  54.1 us (57%)
  starting transfers between devices  27.1 us (28%)
  Pallas kernels  8 us (8%)
  other arithmetic  3.17 us (3%)
  local copies, waits for them, and re-layouts  1.63 us (2%)
  between operations  1.51 us (2%)
    ppermute x17, waiting for transfers between devices, move_row(): return lax.ppermute(a, 'row', [(r, r ^ d) for r in range(self.rows)])  40.8 us
    ppermute x17, starting transfers between devices, move_row(): return lax.ppermute(a, 'row', [(r, r ^ d) for r in range(self.rows)])  17.9 us
    ppermute x13, waiting for transfers between devices, move_col(): return lax.ppermute(a, 'col', [(c, c ^ d) for c in range(self.cols)])  13.3 us
    ppermute x13, starting transfers between devices, move_col(): return lax.ppermute(a, 'col', [(c, c ^ d) for c in range(self.cols)])  9.14 us
    pallas_call x1, Pallas kernels, dense_and_backward(): pl.pallas_call(kernel, out_shape=[jax.ShapeDtypeStruct((node_dev, width),...  5.31 us
  transfers between devices with their start and end apart: 30, of which 21 were waited for; matrix products, arithmetic and copies ran while one was open for 3% of the time, Pallas kernels for 0%

profile of v4, /device:TPU:0, one launch (start us, length us, event | category | flops | bytes accessed | tf_op | source)
XLA Modules:
  0.0 95.5 jit_solution(15458103304498059535)
XLA Ops:
  0.6 0.5 collective-permute-start
  1.1 1.0 %select_bitcast_fusion = bf16[1,256,256]{2,1,0:T(8,128)(2,1)S(1)} fusion(bf16[256,512]{1,0:T(8,128)(2,1)} %param.8, pred[]{:T(512)S(6)} %eq.28), kind=kLoop, calls=%fused_computation.19 | loop fusion | flops 65536 | bytes 393217 | tf_op jit(solution)/shard_map/stack | solution.py:264
  2.1 0.4 collective-permute-done
  2.5 0.0 copy-start.1
  2.6 3.0 %collective-permute-start.1 = (bf16[2,256,256]{2,1,0:T(8,128)(2,1)S(1)}, bf16[2,256,256]{2,1,0:T(8,128)(2,1)S(1)}, u32[]{:S(2)}, u32[]{:S(2)}) collective-permute-start(bf16[2,256,256]{2,1,0:T(8,128)(2,1)S(1)} %pad_maximum_fusion.1.refs_0_), channel_id=1, source_target_pairs={{0,4},{4,0},{8,12},{12,8},{16,20},{20,16},{24,28},{28,24},{1,5},{5... | collective-permute-start | bytes 786440 | tf_op jit(solution)/shard_map/ppermute | solution.py:57
  5.5 1.6 %collective-permute-start.2 = (bf16[2,256,256]{2,1,0:T(8,128)(2,1)S(1)}, bf16[2,256,256]{2,1,0:T(8,128)(2,1)S(1)}, u32[]{:S(2)}, u32[]{:S(2)}) collective-permute-start(bf16[2,256,256]{2,1,0:T(8,128)(2,1)S(1)} %pad_maximum_fusion.1.refs_0_), channel_id=1, source_target_pairs={{0,8},{4,12},{8,0},{12,4},{16,24},{20,28},{24,16},{28,20},{1,9},{5... | collective-permute-start | bytes 786440 | tf_op jit(solution)/shard_map/ppermute | solution.py:57
  7.1 1.5 %collective-permute-start.3 = (bf16[256,512]{1,0:T(8,128)(2,1)S(1)}, bf16[256,512]{1,0:T(8,128)(2,1)S(1)}, u32[]{:S(2)}, u32[]{:S(2)}) collective-permute-start(bf16[256,512]{1,0:T(8,128)(2,1)S(1)} %copy-done.1), channel_id=1, source_target_pairs={{0,2},{1,3},{2,0},{3,1},{4,6},{5,7},{6,4},{7,5},{8,10},{9,11},{10,... | collective-permute-start | bytes 786440 | tf_op jit(solution)/shard_map/ppermute | solution.py:61
  8.6 2.6 %collective-permute-start.4 = (bf16[2,256,256]{2,1,0:T(8,128)(2,1)S(1)}, bf16[2,256,256]{2,1,0:T(8,128)(2,1)S(1)}, u32[]{:S(2)}, u32[]{:S(2)}) collective-permute-start(bf16[2,256,256]{2,1,0:T(8,128)(2,1)S(1)} %pad_maximum_fusion.1.refs_0_), channel_id=1, source_target_pairs={{0,16},{4,20},{8,24},{12,28},{16,0},{20,4},{24,8},{28,12},{1,17},{... | collective-permute-start | bytes 786440 | tf_op jit(solution)/shard_map/ppermute | solution.py:57
  11.2 0.9 collective-permute-done.1.refs_1_
  12.1 5.8 %collective-permute-done.2.refs_2_ = bf16[2,256,256]{2,1,0:T(8,128)(2,1)S(1)} collective-permute-done((bf16[2,256,256]{2,1,0:T(8,128)(2,1)S(1)}, bf16[2,256,256]{2,1,0:T(8,128)(2,1)S(1)}, u32[]{:S(2)}, u32[]{:S(2)}) %collective-permute-start.2) | collective-permute-done | bytes 262176 | tf_op jit(solution)/shard_map/ppermute | solution.py:57
  17.9 0.4 collective-permute-start.6
  18.3 0.1 pad_maximum_fusion
  18.3 0.1 collective-permute-start.10
  18.4 0.9 copy-done
  19.3 3.5 %collective-permute-done.4.refs_4_ = bf16[2,256,256]{2,1,0:T(8,128)(2,1)S(1)} collective-permute-done((bf16[2,256,256]{2,1,0:T(8,128)(2,1)S(1)}, bf16[2,256,256]{2,1,0:T(8,128)(2,1)S(1)}, u32[]{:S(2)}, u32[]{:S(2)}) %collective-permute-start.4) | collective-permute-done | bytes 262176 | tf_op jit(solution)/shard_map/ppermute | solution.py:57
  22.7 2.2 %collective-permute-done.6.refs_3_ = bf16[2,256,256]{2,1,0:T(8,128)(2,1)S(1)} collective-permute-done((bf16[2,256,256]{2,1,0:T(8,128)(2,1)S(1)}, bf16[2,256,256]{2,1,0:T(8,128)(2,1)S(1)}, u32[]{:S(2)}, u32[]{:S(2)}) %collective-permute-start.6) | collective-permute-done | bytes 262176 | tf_op jit(solution)/shard_map/ppermute | solution.py:57
  24.9 0.9 collective-permute-start.7
  26.4 0.0 copy-start.5
  26.5 0.6 copy-done.4
  27.1 0.0 copy-done.5
  27.1 0.1 pad_add_fusion.io_ref.idx
  27.2 0.0 collective-permute-start.8
  27.2 1.1 %collective-permute-done.8.ix_ref = s32[25]{0:T(128)S(1)} collective-permute-done((s32[25]{0:T(128)S(1)}, s32[25]{0:T(128)S(1)}, u32[]{:S(2)}, u32[]{:S(2)}) %collective-permute-start.8) | collective-permute-done | bytes 132 | tf_op jit(solution)/shard_map/ppermute | solution.py:61
  28.3 0.8 collective-permute-done.5.refs_6_
  29.1 2.2 %collective-permute-done.7.refs_5_ = bf16[2,256,256]{2,1,0:T(8,128)(2,1)S(1)} collective-permute-done((bf16[2,256,256]{2,1,0:T(8,128)(2,1)S(1)}, bf16[2,256,256]{2,1,0:T(8,128)(2,1)S(1)}, u32[]{:S(2)}, u32[]{:S(2)}) %collective-permute-start.7) | collective-permute-done | bytes 262176 | tf_op jit(solution)/shard_map/ppermute | solution.py:57
  31.3 1.1 %collective-permute-start.11 = (bf16[2,256,256]{2,1,0:T(8,128)(2,1)S(1)}, bf16[2,256,256]{2,1,0:T(8,128)(2,1)S(1)}, u32[]{:S(2)}, u32[]{:S(2)}) collective-permute-start(bf16[2,256,256]{2,1,0:T(8,128)(2,1)S(1)} %collective-permute-done.5.refs_6_), channel_id=1, source_target_pairs={{0,4},{4,0},{8,12},{12,8},{16,20},{20,16},{24,28},{28,24},{1,5},{5... | collective-permute-start | bytes 786440 | tf_op jit(solution)/shard_map/ppermute | solution.py:57
  32.4 5.3 %collective-permute-done.11.refs_7_ = bf16[2,256,256]{2,1,0:T(8,128)(2,1)S(1)} collective-permute-done((bf16[2,256,256]{2,1,0:T(8,128)(2,1)S(1)}, bf16[2,256,256]{2,1,0:T(8,128)(2,1)S(1)}, u32[]{:S(2)}, u32[]{:S(2)}) %collective-permute-start.11) | collective-permute-done | bytes 262176 | tf_op jit(solution)/shard_map/ppermute | solution.py:57
  37.6 1.6 %forward_product.1 = (bf16[512,256]{1,0:T(8,128)(2,1)S(1)}, bf16[512,256]{1,0:T(8,128)(2,1)S(1)}) custom-call(s32[25]{0:T(128)S(1)} %pad_add_fusion.io_ref.idx, s32[25]{0:T(128)S(1)} %collective-permute-done.8.ix_ref, bf16[12,128,128]{2,1,0:T(8,128)(2,1)S(1)} %bitcast.22, bf16[12,128,128]{2,1,0:T(8,128)(2,1)S(1)} %collective-permute-done.9.ax_ref, ...), custom_call_target="tpu_custom_call" | custom-call | flops 201326592 | bytes 2097152 | tf_op jit(solution)/shard_map/forward_product/pallas_call | solution.py:100
  39.3 3.3 %collective-permute-start.14 = (bf16[512,256]{1,0:T(8,128)(2,1)S(1)}, bf16[512,256]{1,0:T(8,128)(2,1)S(1)}, u32[]{:S(2)}, u32[]{:S(2)}) collective-permute-start(bf16[512,256]{1,0:T(8,128)(2,1)S(1)} %get-tuple-element.54.refs_3_), channel_id=1, source_target_pairs={{0,2},{1,3},{2,0},{3,1},{4,6},{5,7},{6,4},{7,5},{8,10},{9,11},{10,... | collective-permute-start | bytes 786440 | tf_op jit(solution)/shard_map/ppermute | solution.py:61
  42.6 0.1 collective-permute-start.15
  42.7 0.5 collective-permute-start.13
  43.2 4.6 %collective-permute-done.14.refs_7_ = bf16[512,256]{1,0:T(8,128)(2,1)S(1)} collective-permute-done((bf16[512,256]{1,0:T(8,128)(2,1)S(1)}, bf16[512,256]{1,0:T(8,128)(2,1)S(1)}, u32[]{:S(2)}, u32[]{:S(2)}) %collective-permute-start.14) | collective-permute-done | bytes 262176 | tf_op jit(solution)/shard_map/ppermute | solution.py:61
  47.8 2.8 %collective-permute-done.15.refs_8_ = bf16[512,256]{1,0:T(8,128)(2,1)S(1)} collective-permute-done((bf16[512,256]{1,0:T(8,128)(2,1)S(1)}, bf16[512,256]{1,0:T(8,128)(2,1)S(1)}, u32[]{:S(2)}, u32[]{:S(2)}) %collective-permute-start.15) | collective-permute-done | bytes 262176 | tf_op jit(solution)/shard_map/ppermute | solution.py:61
  50.6 1.5 %collective-permute-done.17.refs_10_ = bf16[512,256]{1,0:T(8,128)(2,1)S(1)} collective-permute-done((bf16[512,256]{1,0:T(8,128)(2,1)S(1)}, bf16[512,256]{1,0:T(8,128)(2,1)S(1)}, u32[]{:S(2)}, u32[]{:S(2)}) %collective-permute-start.17) | collective-permute-done | bytes 262176 | tf_op jit(solution)/shard_map/ppermute | solution.py:61
  52.1 5.3 %dense_and_backward.1 = (bf16[256,512]{1,0:T(8,128)(2,1)}, bf16[144,512]{1,0:T(8,128)(2,1)S(1)}, bf16[256,512]{1,0:T(8,128)(2,1)S(1)}, bf16[256,512]{1,0:T(8,128...) custom-call(bf16[512,512]{1,0:T(8,128)(2,1)S(1)} %copy-done.2, ...), custom_call_target="tpu_custom_call" | custom-call | flops 1342177280 | bytes 4194304 | tf_op jit(solution)/shard_map/dense_and_backward/pallas_call | solution.py:198
  57.4 0.1 collective-permute-start.18
  57.5 1.8 %collective-permute-start.20 = (bf16[256,512]{1,0:T(8,128)(2,1)S(1)}, bf16[256,512]{1,0:T(8,128)(2,1)S(1)}, u32[]{:S(2)}, u32[]{:S(2)}) collective-permute-start(bf16[256,512]{1,0:T(8,128)(2,1)S(1)} %get-tuple-element.62), channel_id=1, source_target_pairs={{0,4},{4,0},{8,12},{12,8},{16,20},{20,16},{24,28},{28,24},{1,5},{5... | collective-permute-start | bytes 786440 | tf_op jit(solution)/shard_map/ppermute | solution.py:57
  59.3 4.4 %collective-permute-done.18 = bf16[144,512]{1,0:T(8,128)(2,1)S(1)} collective-permute-done((bf16[144,512]{1,0:T(8,128)(2,1)S(1)}, bf16[144,512]{1,0:T(8,128)(2,1)S(1)}, u32[]{:S(2)}, u32[]{:S(2)}) %collective-permute-start.18) | collective-permute-done | bytes 147488 | tf_op jit(solution)/shard_map/ppermute | solution.py:57
  63.8 0.1 select_select_fusion.1
  63.9 1.0 %collective-permute-start.19 = (bf16[144,512]{1,0:T(8,128)(2,1)S(1)}, bf16[144,512]{1,0:T(8,128)(2,1)S(1)}, u32[]{:S(2)}, u32[]{:S(2)}) collective-permute-start(bf16[144,512]{1,0:T(8,128)(2,1)S(1)} %pad_maximum_fusion.3), channel_id=1, source_target_pairs={{0,16},{4,20},{8,24},{12,28},{16,0},{20,4},{24,8},{28,12},{1,17},{... | collective-permute-start | bytes 442376 | tf_op jit(solution)/shard_map/ppermute | solution.py:57
  65.0 1.3 %collective-permute-done.20 = bf16[256,512]{1,0:T(8,128)(2,1)S(1)} collective-permute-done((bf16[256,512]{1,0:T(8,128)(2,1)S(1)}, bf16[256,512]{1,0:T(8,128)(2,1)S(1)}, u32[]{:S(2)}, u32[]{:S(2)}) %collective-permute-start.20) | collective-permute-done | bytes 262176 | tf_op jit(solution)/shard_map/ppermute | solution.py:57
  66.3 0.1 add_convert_fusion.2
  66.4 0.8 collective-permute-start.21
  67.2 1.7 %collective-permute-start.22 = (bf16[256,512]{1,0:T(8,128)(2,1)S(1)}, bf16[256,512]{1,0:T(8,128)(2,1)S(1)}, u32[]{:S(2)}, u32[]{:S(2)}) collective-permute-start(bf16[256,512]{1,0:T(8,128)(2,1)S(1)} %add_convert_fusion.2), channel_id=1, source_target_pairs={{0,8},{4,12},{8,0},{12,4},{16,24},{20,28},{24,16},{28,20},{1,9},{5... | collective-permute-start | bytes 786440 | tf_op jit(solution)/shard_map/ppermute | solution.py:57
  68.9 4.7 %collective-permute-done.19 = bf16[144,512]{1,0:T(8,128)(2,1)S(1)} collective-permute-done((bf16[144,512]{1,0:T(8,128)(2,1)S(1)}, bf16[144,512]{1,0:T(8,128)(2,1)S(1)}, u32[]{:S(2)}, u32[]{:S(2)}) %collective-permute-start.19) | collective-permute-done | bytes 147488 | tf_op jit(solution)/shard_map/ppermute | solution.py:57
  73.6 0.1 select_select_fusion
  73.7 0.4 collective-permute-start.28
  74.1 0.2 collective-permute-done.21
  74.3 3.1 %collective-permute-done.22 = bf16[256,512]{1,0:T(8,128)(2,1)S(1)} collective-permute-done((bf16[256,512]{1,0:T(8,128)(2,1)S(1)}, bf16[256,512]{1,0:T(8,128)(2,1)S(1)}, u32[]{:S(2)}, u32[]{:S(2)}) %collective-permute-start.22) | collective-permute-done | bytes 262176 | tf_op jit(solution)/shard_map/ppermute | solution.py:57
  77.5 0.1 convert_add_fusion
  77.6 0.8 collective-permute-start.23
  78.3 1.6 %collective-permute-start.27 = (bf16[256,512]{1,0:T(8,128)(2,1)S(1)}, bf16[256,512]{1,0:T(8,128)(2,1)S(1)}, u32[]{:S(2)}, u32[]{:S(2)}) collective-permute-start(bf16[256,512]{1,0:T(8,128)(2,1)S(1)} %convert_add_fusion), channel_id=1, source_target_pairs={{0,16},{4,20},{8,24},{12,28},{16,0},{20,4},{24,8},{28,12},{1,17},{... | collective-permute-start | bytes 786440 | tf_op jit(solution)/shard_map/ppermute | solution.py:57
  79.9 3.0 %collective-permute-done.28 = bf16[256,512]{1,0:T(8,128)(2,1)S(1)} collective-permute-done((bf16[256,512]{1,0:T(8,128)(2,1)S(1)}, bf16[256,512]{1,0:T(8,128)(2,1)S(1)}, u32[]{:S(2)}, u32[]{:S(2)}) %collective-permute-start.28) | collective-permute-done | bytes 262176 | tf_op jit(solution)/shard_map/ppermute | solution.py:57
  83.0 0.1 add_convert_fusion.1
  83.0 0.1 collective-permute-start.29
  83.1 2.0 %collective-permute-done.23 = bf16[144,512]{1,0:T(8,128)(2,1)S(1)} collective-permute-done((bf16[144,512]{1,0:T(8,128)(2,1)S(1)}, bf16[144,512]{1,0:T(8,128)(2,1)S(1)}, u32[]{:S(2)}, u32[]{:S(2)}) %collective-permute-start.23) | collective-permute-done | bytes 147488 | tf_op jit(solution)/shard_map/ppermute | solution.py:57
  85.1 0.3 collective-permute-start.26
  85.5 3.1 %collective-permute-start.24 = (bf16[128,512]{1,0:T(8,128)(2,1)S(1)}, bf16[128,512]{1,0:T(8,128)(2,1)S(1)}, u32[]{:S(2)}, u32[]{:S(2)}) collective-permute-start(bf16[128,512]{1,0:T(8,128)(2,1)S(1)} %slice.109.refs_0_), channel_id=1, source_target_pairs={{0,2},{1,3},{2,0},{3,1},{4,6},{5,7},{6,4},{7,5},{8,10},{9,11},{10,... | collective-permute-start | bytes 393224 | tf_op jit(solution)/shard_map/ppermute | solution.py:61
  88.6 2.9 %collective-permute-done.24.refs_1_ = bf16[128,512]{1,0:T(8,128)(2,1)S(1)} collective-permute-done((bf16[128,512]{1,0:T(8,128)(2,1)S(1)}, bf16[128,512]{1,0:T(8,128)(2,1)S(1)}, u32[]{:S(2)}, u32[]{:S(2)}) %collective-permute-start.24) | collective-permute-done | bytes 131104 | tf_op jit(solution)/shard_map/ppermute | solution.py:61
  91.5 0.1 collective-permute-start.25
  91.6 0.6 slice_add_fusion
  92.2 1.4 %collective-permute-done.29 = bf16[256,512]{1,0:T(8,128)(2,1)S(1)} collective-permute-done((bf16[256,512]{1,0:T(8,128)(2,1)S(1)}, bf16[256,512]{1,0:T(8,128)(2,1)S(1)}, u32[]{:S(2)}, u32[]{:S(2)}) %collective-permute-start.29) | collective-permute-done | bytes 262176 | tf_op jit(solution)/shard_map/ppermute | solution.py:57
  93.6 0.8 add_convert_fusion
  94.4 1.1 %place_weight_gradient.1 = f32[512,512]{1,0:T(8,128)} custom-call(bf16[128,512]{1,0:T(8,128)(2,1)S(1)} %slice.109.refs_0_, bf16[128,512]{1,0:T(8,128)(2,1)S(1)} %collective-permute-done.24.refs_1_, bf16[128,512]{1,0:T(8,128)(2,1)S(1)} %get-tuple-element.79.refs_2_, bf16[128,512]{1,0:T(8,128)(2,1)S(1)} %get-tuple-element.78.refs_3_), custom_call_target="tpu_custom_call" | custom-call | flops 262144 | bytes 1572864 | tf_op jit(solution)/shard_map/place_weight_gradient/pallas_call | solution.py:235
  (37 shorter events, 0.4 us)
Async XLA Ops:
  0.6 1.9 %collective-permute-start = (bf16[256,512]{1,0:T(8,128)(2,1)}, bf16[256,512]{1,0:T(8,128)(2,1)S(1)}, u32[]{:S(2)}, u32[]{:S(2)}) collective-permute-start(bf16[256,512]{1,0:T(8,128)(2,1)} %param.8), channel_id=1, source_target_pairs={{0,1},{1,0},{2,3},{3,2},{4,5},{5,4},{6,7},{7,6},{8,9},{9,8},{10,11... | collective-permute-start | bytes 786440 | tf_op jit(solution)/shard_map/ppermute | solution.py:61
  2.5 4.6 %copy-start.1 = (bf16[256,512]{1,0:T(8,128)(2,1)S(1)}, bf16[256,512]{1,0:T(8,128)(2,1)}, u32[]{:S(2)}) copy-start(bf16[256,512]{1,0:T(8,128)(2,1)} %refs_0_) | copy-start | bytes 786436
  2.6 9.6 %collective-permute-start.1 = (bf16[2,256,256]{2,1,0:T(8,128)(2,1)S(1)}, bf16[2,256,256]{2,1,0:T(8,128)(2,1)S(1)}, u32[]{:S(2)}, u32[]{:S(2)}) collective-permute-start(bf16[2,256,256]{2,1,0:T(8,128)(2,1)S(1)} %pad_maximum_fusion.1.refs_0_), channel_id=1, source_target_pairs={{0,4},{4,0},{8,12},{12,8},{16,20},{20,16},{24,28},{28,24},{1,5},{5... | collective-permute-start | bytes 786440 | tf_op jit(solution)/shard_map/ppermute | solution.py:57
  5.5 12.4 %collective-permute-start.2 = (bf16[2,256,256]{2,1,0:T(8,128)(2,1)S(1)}, bf16[2,256,256]{2,1,0:T(8,128)(2,1)S(1)}, u32[]{:S(2)}, u32[]{:S(2)}) collective-permute-start(bf16[2,256,256]{2,1,0:T(8,128)(2,1)S(1)} %pad_maximum_fusion.1.refs_0_), channel_id=1, source_target_pairs={{0,8},{4,12},{8,0},{12,4},{16,24},{20,28},{24,16},{28,20},{1,9},{5... | collective-permute-start | bytes 786440 | tf_op jit(solution)/shard_map/ppermute | solution.py:57
  7.1 11.1 %collective-permute-start.3 = (bf16[256,512]{1,0:T(8,128)(2,1)S(1)}, bf16[256,512]{1,0:T(8,128)(2,1)S(1)}, u32[]{:S(2)}, u32[]{:S(2)}) collective-permute-start(bf16[256,512]{1,0:T(8,128)(2,1)S(1)} %copy-done.1), channel_id=1, source_target_pairs={{0,2},{1,3},{2,0},{3,1},{4,6},{5,7},{6,4},{7,5},{8,10},{9,11},{10,... | collective-permute-start | bytes 786440 | tf_op jit(solution)/shard_map/ppermute | solution.py:61
  8.6 14.1 %collective-permute-start.4 = (bf16[2,256,256]{2,1,0:T(8,128)(2,1)S(1)}, bf16[2,256,256]{2,1,0:T(8,128)(2,1)S(1)}, u32[]{:S(2)}, u32[]{:S(2)}) collective-permute-start(bf16[2,256,256]{2,1,0:T(8,128)(2,1)S(1)} %pad_maximum_fusion.1.refs_0_), channel_id=1, source_target_pairs={{0,16},{4,20},{8,24},{12,28},{16,0},{20,4},{24,8},{28,12},{1,17},{... | collective-permute-start | bytes 786440 | tf_op jit(solution)/shard_map/ppermute | solution.py:57
  17.9 7.0 %collective-permute-start.6 = (bf16[2,256,256]{2,1,0:T(8,128)(2,1)S(1)}, bf16[2,256,256]{2,1,0:T(8,128)(2,1)S(1)}, u32[]{:S(2)}, u32[]{:S(2)}) collective-permute-start(bf16[2,256,256]{2,1,0:T(8,128)(2,1)S(1)} %collective-permute-done.2.refs_2_), channel_id=1, source_target_pairs={{0,4},{4,0},{8,12},{12,8},{16,20},{20,16},{24,28},{28,24},{1,5},{5... | collective-permute-start | bytes 786440 | tf_op jit(solution)/shard_map/ppermute | solution.py:57
  18.3 1.0 %copy-start = (bf16[1,1,12,128,128]{4,3,2,1,0:T(8,128)(2,1)S(1)}, bf16[1,1,12,128,128]{4,3,2,1,0:T(8,128)(2,1)}, u32[]{:S(2)}) copy-start(bf16[1,1,12,128,128]{4,3,2,1,0:T(8,128)(2,1)} %param.9) | copy-start | bytes 1179652
  18.3 10.8 %collective-permute-start.10 = (bf16[2,256,512]{2,1,0:T(8,128)(2,1)S(1)}, bf16[2,256,512]{2,1,0:T(8,128)(2,1)S(1)}, u32[]{:S(2)}, u32[]{:S(2)}) collective-permute-start(bf16[2,256,512]{2,1,0:T(8,128)(2,1)S(1)} %pad_maximum_fusion), channel_id=1, source_target_pairs={{0,1},{1,0},{2,3},{3,2},{4,5},{5,4},{6,7},{7,6},{8,9},{9,8},{10,11... | collective-permute-start | bytes 1572872 | tf_op jit(solution)/shard_map/ppermute | solution.py:61
  19.3 9.8 %collective-permute-start.9 = (bf16[12,128,128]{2,1,0:T(8,128)(2,1)S(1)}, bf16[12,128,128]{2,1,0:T(8,128)(2,1)S(1)}, u32[]{:S(2)}, u32[]{:S(2)}) collective-permute-start(bf16[12,128,128]{2,1,0:T(8,128)(2,1)S(1)} %bitcast.21), channel_id=1, source_target_pairs={{0,1},{1,0},{2,3},{3,2},{4,5},{5,4},{6,7},{7,6},{8,9},{9,8},{10,11... | collective-permute-start | bytes 1179656 | tf_op jit(solution)/shard_map/ppermute | solution.py:61
  22.7 6.4 %collective-permute-start.5 = (bf16[2,256,256]{2,1,0:T(8,128)(2,1)S(1)}, bf16[2,256,256]{2,1,0:T(8,128)(2,1)S(1)}, u32[]{:S(2)}, u32[]{:S(2)}) collective-permute-start(bf16[2,256,256]{2,1,0:T(8,128)(2,1)S(1)} %collective-permute-done.4.refs_4_), channel_id=1, source_target_pairs={{0,8},{4,12},{8,0},{12,4},{16,24},{20,28},{24,16},{28,20},{1,9},{5... | collective-permute-start | bytes 786440 | tf_op jit(solution)/shard_map/ppermute | solution.py:57
  24.9 6.4 %collective-permute-start.7 = (bf16[2,256,256]{2,1,0:T(8,128)(2,1)S(1)}, bf16[2,256,256]{2,1,0:T(8,128)(2,1)S(1)}, u32[]{:S(2)}, u32[]{:S(2)}) collective-permute-start(bf16[2,256,256]{2,1,0:T(8,128)(2,1)S(1)} %collective-permute-done.4.refs_4_), channel_id=1, source_target_pairs={{0,4},{4,0},{8,12},{12,8},{16,20},{20,16},{24,28},{28,24},{1,5},{5... | collective-permute-start | bytes 786440 | tf_op jit(solution)/shard_map/ppermute | solution.py:57
  26.4 0.7 copy-start.4
  26.4 0.7 copy-start.5
  27.2 24.9 %copy-start.2 = (bf16[512,512]{1,0:T(8,128)(2,1)S(1)}, bf16[512,512]{1,0:T(8,128)(2,1)}, u32[]{:S(2)}) copy-start(bf16[512,512]{1,0:T(8,128)(2,1)} %w_ref.1) | copy-start | bytes 1572868
  27.2 1.1 %collective-permute-start.8 = (s32[25]{0:T(128)S(1)}, s32[25]{0:T(128)S(1)}, u32[]{:S(2)}, u32[]{:S(2)}) collective-permute-start(s32[25]{0:T(128)S(1)} %pad_add_fusion.io_ref.idx), channel_id=1, source_target_pairs={{0,1},{1,0},{2,3},{3,2},{4,5},{5,4},{6,7},{7,6},{8,9},{9,8},{10,11... | collective-permute-start | bytes 308 | tf_op jit(solution)/shard_map/ppermute | solution.py:61
  31.3 6.4 %collective-permute-start.11 = (bf16[2,256,256]{2,1,0:T(8,128)(2,1)S(1)}, bf16[2,256,256]{2,1,0:T(8,128)(2,1)S(1)}, u32[]{:S(2)}, u32[]{:S(2)}) collective-permute-start(bf16[2,256,256]{2,1,0:T(8,128)(2,1)S(1)} %collective-permute-done.5.refs_6_), channel_id=1, source_target_pairs={{0,4},{4,0},{8,12},{12,8},{16,20},{20,16},{24,28},{28,24},{1,5},{5... | collective-permute-start | bytes 786440 | tf_op jit(solution)/shard_map/ppermute | solution.py:57
  39.3 12.8 %copy-start.3 = (f32[512]{0:T(512)S(1)}, f32[512]{0:T(512)}, u32[]{:S(2)}) copy-start(f32[512]{0:T(512)} %param.14) | copy-start | bytes 6148
  39.3 8.5 %collective-permute-start.14 = (bf16[512,256]{1,0:T(8,128)(2,1)S(1)}, bf16[512,256]{1,0:T(8,128)(2,1)S(1)}, u32[]{:S(2)}, u32[]{:S(2)}) collective-permute-start(bf16[512,256]{1,0:T(8,128)(2,1)S(1)} %get-tuple-element.54.refs_3_), channel_id=1, source_target_pairs={{0,2},{1,3},{2,0},{3,1},{4,6},{5,7},{6,4},{7,5},{8,10},{9,11},{10,... | collective-permute-start | bytes 786440 | tf_op jit(solution)/shard_map/ppermute | solution.py:61
  42.6 8.0 %collective-permute-start.15 = (bf16[512,256]{1,0:T(8,128)(2,1)S(1)}, bf16[512,256]{1,0:T(8,128)(2,1)S(1)}, u32[]{:S(2)}, u32[]{:S(2)}) collective-permute-start(bf16[512,256]{1,0:T(8,128)(2,1)S(1)} %get-tuple-element.55.refs_4_), channel_id=1, source_target_pairs={{0,2},{1,3},{2,0},{3,1},{4,6},{5,7},{6,4},{7,5},{8,10},{9,11},{10,... | collective-permute-start | bytes 786440 | tf_op jit(solution)/shard_map/ppermute | solution.py:61
  42.7 7.9 %collective-permute-start.12 = (bf16[512,256]{1,0:T(8,128)(2,1)S(1)}, bf16[512,256]{1,0:T(8,128)(2,1)S(1)}, u32[]{:S(2)}, u32[]{:S(2)}) collective-permute-start(bf16[512,256]{1,0:T(8,128)(2,1)S(1)} %get-tuple-element.54.refs_3_), channel_id=1, source_target_pairs={{0,1},{1,0},{2,3},{3,2},{4,5},{5,4},{6,7},{7,6},{8,9},{9,8},{10,11... | collective-permute-start | bytes 786440 | tf_op jit(solution)/shard_map/ppermute | solution.py:61
  42.7 7.9 %collective-permute-start.13 = (bf16[512,256]{1,0:T(8,128)(2,1)S(1)}, bf16[512,256]{1,0:T(8,128)(2,1)S(1)}, u32[]{:S(2)}, u32[]{:S(2)}) collective-permute-start(bf16[512,256]{1,0:T(8,128)(2,1)S(1)} %get-tuple-element.55.refs_4_), channel_id=1, source_target_pairs={{0,1},{1,0},{2,3},{3,2},{4,5},{5,4},{6,7},{7,6},{8,9},{9,8},{10,11... | collective-permute-start | bytes 786440 | tf_op jit(solution)/shard_map/ppermute | solution.py:61
  47.8 2.8 %collective-permute-start.16 = (bf16[512,256]{1,0:T(8,128)(2,1)S(1)}, bf16[512,256]{1,0:T(8,128)(2,1)S(1)}, u32[]{:S(2)}, u32[]{:S(2)}) collective-permute-start(bf16[512,256]{1,0:T(8,128)(2,1)S(1)} %collective-permute-done.14.refs_7_), channel_id=1, source_target_pairs={{0,1},{1,0},{2,3},{3,2},{4,5},{5,4},{6,7},{7,6},{8,9},{9,8},{10,11... | collective-permute-start | bytes 786440 | tf_op jit(solution)/shard_map/ppermute | solution.py:61
  50.6 1.5 %collective-permute-start.17 = (bf16[512,256]{1,0:T(8,128)(2,1)S(1)}, bf16[512,256]{1,0:T(8,128)(2,1)S(1)}, u32[]{:S(2)}, u32[]{:S(2)}) collective-permute-start(bf16[512,256]{1,0:T(8,128)(2,1)S(1)} %collective-permute-done.15.refs_8_), channel_id=1, source_target_pairs={{0,1},{1,0},{2,3},{3,2},{4,5},{5,4},{6,7},{7,6},{8,9},{9,8},{10,11... | collective-permute-start | bytes 786440 | tf_op jit(solution)/shard_map/ppermute | solution.py:61
  57.4 6.3 %collective-permute-start.18 = (bf16[144,512]{1,0:T(8,128)(2,1)S(1)}, bf16[144,512]{1,0:T(8,128)(2,1)S(1)}, u32[]{:S(2)}, u32[]{:S(2)}) collective-permute-start(bf16[144,512]{1,0:T(8,128)(2,1)S(1)} %get-tuple-element.57), channel_id=1, source_target_pairs={{0,8},{4,12},{8,0},{12,4},{16,24},{20,28},{24,16},{28,20},{1,9},{5... | collective-permute-start | bytes 442376 | tf_op jit(solution)/shard_map/ppermute | solution.py:57
  57.5 8.8 %collective-permute-start.20 = (bf16[256,512]{1,0:T(8,128)(2,1)S(1)}, bf16[256,512]{1,0:T(8,128)(2,1)S(1)}, u32[]{:S(2)}, u32[]{:S(2)}) collective-permute-start(bf16[256,512]{1,0:T(8,128)(2,1)S(1)} %get-tuple-element.62), channel_id=1, source_target_pairs={{0,4},{4,0},{8,12},{12,8},{16,20},{20,16},{24,28},{28,24},{1,5},{5... | collective-permute-start | bytes 786440 | tf_op jit(solution)/shard_map/ppermute | solution.py:57
  63.9 9.6 %collective-permute-start.19 = (bf16[144,512]{1,0:T(8,128)(2,1)S(1)}, bf16[144,512]{1,0:T(8,128)(2,1)S(1)}, u32[]{:S(2)}, u32[]{:S(2)}) collective-permute-start(bf16[144,512]{1,0:T(8,128)(2,1)S(1)} %pad_maximum_fusion.3), channel_id=1, source_target_pairs={{0,16},{4,20},{8,24},{12,28},{16,0},{20,4},{24,8},{28,12},{1,17},{... | collective-permute-start | bytes 442376 | tf_op jit(solution)/shard_map/ppermute | solution.py:57
  66.4 8.0 %collective-permute-start.21 = (bf16[256,512]{1,0:T(8,128)(2,1)S(1)}, bf16[256,512]{1,0:T(8,128)(2,1)S(1)}, u32[]{:S(2)}, u32[]{:S(2)}) collective-permute-start(bf16[256,512]{1,0:T(8,128)(2,1)S(1)} %get-tuple-element.64), channel_id=1, source_target_pairs={{0,4},{4,0},{8,12},{12,8},{16,20},{20,16},{24,28},{28,24},{1,5},{5... | collective-permute-start | bytes 786440 | tf_op jit(solution)/shard_map/ppermute | solution.py:57
  67.2 10.3 %collective-permute-start.22 = (bf16[256,512]{1,0:T(8,128)(2,1)S(1)}, bf16[256,512]{1,0:T(8,128)(2,1)S(1)}, u32[]{:S(2)}, u32[]{:S(2)}) collective-permute-start(bf16[256,512]{1,0:T(8,128)(2,1)S(1)} %add_convert_fusion.2), channel_id=1, source_target_pairs={{0,8},{4,12},{8,0},{12,4},{16,24},{20,28},{24,16},{28,20},{1,9},{5... | collective-permute-start | bytes 786440 | tf_op jit(solution)/shard_map/ppermute | solution.py:57
  73.7 9.2 %collective-permute-start.28 = (bf16[256,512]{1,0:T(8,128)(2,1)S(1)}, bf16[256,512]{1,0:T(8,128)(2,1)S(1)}, u32[]{:S(2)}, u32[]{:S(2)}) collective-permute-start(bf16[256,512]{1,0:T(8,128)(2,1)S(1)} %get-tuple-element.73), channel_id=1, source_target_pairs={{0,4},{4,0},{8,12},{12,8},{16,20},{20,16},{24,28},{28,24},{1,5},{5... | collective-permute-start | bytes 786440 | tf_op jit(solution)/shard_map/ppermute | solution.py:57
  77.6 7.5 %collective-permute-start.23 = (bf16[144,512]{1,0:T(8,128)(2,1)S(1)}, bf16[144,512]{1,0:T(8,128)(2,1)S(1)}, u32[]{:S(2)}, u32[]{:S(2)}) collective-permute-start(bf16[144,512]{1,0:T(8,128)(2,1)S(1)} %pad_maximum_fusion.4), channel_id=1, source_target_pairs={{0,4},{4,0},{8,12},{12,8},{16,20},{20,16},{24,28},{28,24},{1,5},{5... | collective-permute-start | bytes 442376 | tf_op jit(solution)/shard_map/ppermute | solution.py:57
  78.3 13.8 %collective-permute-start.27 = (bf16[256,512]{1,0:T(8,128)(2,1)S(1)}, bf16[256,512]{1,0:T(8,128)(2,1)S(1)}, u32[]{:S(2)}, u32[]{:S(2)}) collective-permute-start(bf16[256,512]{1,0:T(8,128)(2,1)S(1)} %convert_add_fusion), channel_id=1, source_target_pairs={{0,16},{4,20},{8,24},{12,28},{16,0},{20,4},{24,8},{28,12},{1,17},{... | collective-permute-start | bytes 786440 | tf_op jit(solution)/shard_map/ppermute | solution.py:57
  83.0 10.5 %collective-permute-start.29 = (bf16[256,512]{1,0:T(8,128)(2,1)S(1)}, bf16[256,512]{1,0:T(8,128)(2,1)S(1)}, u32[]{:S(2)}, u32[]{:S(2)}) collective-permute-start(bf16[256,512]{1,0:T(8,128)(2,1)S(1)} %add_convert_fusion.1), channel_id=1, source_target_pairs={{0,8},{4,12},{8,0},{12,4},{16,24},{20,28},{24,16},{28,20},{1,9},{5... | collective-permute-start | bytes 786440 | tf_op jit(solution)/shard_map/ppermute | solution.py:57
  85.1 8.5 %collective-permute-start.26 = (bf16[256,512]{1,0:T(8,128)(2,1)S(1)}, bf16[256,512]{1,0:T(8,128)(2,1)S(1)}, u32[]{:S(2)}, u32[]{:S(2)}) collective-permute-start(bf16[256,512]{1,0:T(8,128)(2,1)S(1)} %get-tuple-element.70), channel_id=1, source_target_pairs={{0,4},{4,0},{8,12},{12,8},{16,20},{20,16},{24,28},{28,24},{1,5},{5... | collective-permute-start | bytes 786440 | tf_op jit(solution)/shard_map/ppermute | solution.py:57
  85.5 6.0 %collective-permute-start.24 = (bf16[128,512]{1,0:T(8,128)(2,1)S(1)}, bf16[128,512]{1,0:T(8,128)(2,1)S(1)}, u32[]{:S(2)}, u32[]{:S(2)}) collective-permute-start(bf16[128,512]{1,0:T(8,128)(2,1)S(1)} %slice.109.refs_0_), channel_id=1, source_target_pairs={{0,2},{1,3},{2,0},{3,1},{4,6},{5,7},{6,4},{7,5},{8,10},{9,11},{10,... | collective-permute-start | bytes 393224 | tf_op jit(solution)/shard_map/ppermute | solution.py:61
  91.5 2.9 %collective-permute-start.25 = (bf16[2,128,512]{2,1,0:T(8,128)(2,1)S(1)}, bf16[2,128,512]{2,1,0:T(8,128)(2,1)S(1)}, u32[]{:S(2)}, u32[]{:S(2)}) collective-permute-start(bf16[2,128,512]{2,1,0:T(8,128)(2,1)S(1)} %pad_maximum_fusion.2), channel_id=1, source_target_pairs={{0,1},{1,0},{2,3},{3,2},{4,5},{5,4},{6,7},{7,6},{8,9},{9,8},{10,11... | collective-permute-start | bytes 786440 | tf_op jit(solution)/shard_map/ppermute | solution.py:61

commit v5 on v4

--- a/solution.py
+++ b/solution.py
@@ -330,8 +330,9 @@
         to, hop = (top, dz ^ top) if dz != top else (0, dz)
         sums[to] = sums[to] + lay.move_row(sums[dz].astype(BF16), slow=hop).astype(F32)
 
-    hops = [dict(slow=1 << i) for i in range(lay.slow.bit_length() - 1)]
+    hops = [dict(slow=1)] * (lay.slow > 1)
     hops += [dict(fast=1 << i) for i in range(lay.fast.bit_length() - 1)]
+    hops += [dict(slow=2)] * (lay.slow > 2)
     sums = {}
     if lay.slow > 2:
         sums[3] = hold(2, fast_sum(3, fast_arrivals(3)).astype(BF16))
@@ -341,13 +342,15 @@
     for n, hop in enumerate(hops):
         if n:
             gw = split_bias(gw.astype(F32) + came.astype(F32), width)
-            if hop.get("fast") == 1 and lay.slow > 2:
+            if n == len(hops) - 1 and lay.slow > 2:
                 gw = hold(1, gw)
-                gw, sums[2] = lax.optimization_barrier((gw, sums[2]))
         came = lay.move_row(gw, **hop)
-    came = hold(0, came)
-    for dz in range(min(2, lay.slow)):
-        sums[dz] = fast_sum(dz, fast_arrivals(dz))
+    if lay.slow > 1:
+        sums[1] = hold(0, fast_sum(1, fast_arrivals(1)).astype(BF16))
+    for dz in sorted(sums, reverse=True):
+        if dz < 3:
+            came, sums[dz] = lax.optimization_barrier((came, sums[dz]))
+    sums[0] = fast_sum(0, fast_arrivals(0))
     for dz in reversed(range(1, min(3, lay.slow))):
         slow_sum(dz)
     grad_features = sums[0].astype(BF16)

time: 95.5 us -> 95 us (level)
  waiting for transfers between devices: 54.1 us -> 48.1 us
  starting transfers between devices: 27.1 us -> 32.4 us
    ppermute x17, starting transfers between devices: 17.9 us -> 26.2 us  [move_row(): return lax.ppermute(a, 'row', [(r, r ^ d) for r in range(self.rows)])]
    ppermute x17, waiting for transfers between devices: 40.8 us -> 32.8 us  [move_row(): return lax.ppermute(a, 'row', [(r, r ^ d) for r in range(self.rows)])]
    ppermute x13, starting transfers between devices: 9.14 us -> 6.14 us  [move_col(): return lax.ppermute(a, 'col', [(c, c ^ d) for c in range(self.cols)])]
    ppermute x13, waiting for transfers between devices: 13.3 us -> 15.3 us  [move_col(): return lax.ppermute(a, 'col', [(c, c ^ d) for c in range(self.cols)])]
  transfers between devices with their start and end apart: 30 -> 30, of which waited for: 21 -> 20; matrix products, arithmetic and copies ran while one was open for 3% -> 3% of each run, Pallas kernels for 0% -> 0%
where the time goes in v5:
time: 95 us; the launch traced here: 95.1 us
  waiting for transfers between devices  48.1 us (51%)
  starting transfers between devices  32.4 us (34%)
  Pallas kernels  8.32 us (9%)
  other arithmetic  3.17 us (3%)
  local copies, waits for them, and re-layouts  1.63 us (2%)
  between operations  1.52 us (2%)
    ppermute x17, waiting for transfers between devices, move_row(): return lax.ppermute(a, 'row', [(r, r ^ d) for r in range(self.rows)])  32.8 us
    ppermute x17, starting transfers between devices, move_row(): return lax.ppermute(a, 'row', [(r, r ^ d) for r in range(self.rows)])  26.2 us
    ppermute x13, waiting for transfers between devices, move_col(): return lax.ppermute(a, 'col', [(c, c ^ d) for c in range(self.cols)])  15.3 us
    ppermute x13, starting transfers between devices, move_col(): return lax.ppermute(a, 'col', [(c, c ^ d) for c in range(self.cols)])  6.14 us
    pallas_call x1, Pallas kernels, dense_and_backward(): pl.pallas_call(kernel, out_shape=[jax.ShapeDtypeStruct((node_dev, width),...  5.63 us
  transfers between devices with their start and end apart: 30, of which 20 were waited for; matrix products, arithmetic and copies ran while one was open for 3% of the time, Pallas kernels for 0%

profile of v5, /device:TPU:0, one launch (start us, length us, event | category | flops | bytes accessed | tf_op | source)
XLA Modules:
  0.0 95.1 jit_solution(12458641048380764083)
XLA Ops:
  0.6 0.5 collective-permute-start
  1.1 1.0 %select_bitcast_fusion = bf16[1,256,256]{2,1,0:T(8,128)(2,1)S(1)} fusion(bf16[256,512]{1,0:T(8,128)(2,1)} %param.8, pred[]{:T(512)S(6)} %eq.28), kind=kLoop, calls=%fused_computation.19 | loop fusion | flops 65536 | bytes 393217 | tf_op jit(solution)/shard_map/stack | solution.py:264
  2.1 0.4 collective-permute-done
  2.5 0.0 copy-start.1
  2.6 3.0 %collective-permute-start.1 = (bf16[2,256,256]{2,1,0:T(8,128)(2,1)S(1)}, bf16[2,256,256]{2,1,0:T(8,128)(2,1)S(1)}, u32[]{:S(2)}, u32[]{:S(2)}) collective-permute-start(bf16[2,256,256]{2,1,0:T(8,128)(2,1)S(1)} %pad_maximum_fusion.1.refs_0_), channel_id=1, source_target_pairs={{0,4},{4,0},{8,12},{12,8},{16,20},{20,16},{24,28},{28,24},{1,5},{5... | collective-permute-start | bytes 786440 | tf_op jit(solution)/shard_map/ppermute | solution.py:57
  5.5 1.6 %collective-permute-start.2 = (bf16[2,256,256]{2,1,0:T(8,128)(2,1)S(1)}, bf16[2,256,256]{2,1,0:T(8,128)(2,1)S(1)}, u32[]{:S(2)}, u32[]{:S(2)}) collective-permute-start(bf16[2,256,256]{2,1,0:T(8,128)(2,1)S(1)} %pad_maximum_fusion.1.refs_0_), channel_id=1, source_target_pairs={{0,8},{4,12},{8,0},{12,4},{16,24},{20,28},{24,16},{28,20},{1,9},{5... | collective-permute-start | bytes 786440 | tf_op jit(solution)/shard_map/ppermute | solution.py:57
  7.1 1.5 %collective-permute-start.3 = (bf16[256,512]{1,0:T(8,128)(2,1)S(1)}, bf16[256,512]{1,0:T(8,128)(2,1)S(1)}, u32[]{:S(2)}, u32[]{:S(2)}) collective-permute-start(bf16[256,512]{1,0:T(8,128)(2,1)S(1)} %copy-done.1), channel_id=1, source_target_pairs={{0,2},{1,3},{2,0},{3,1},{4,6},{5,7},{6,4},{7,5},{8,10},{9,11},{10,... | collective-permute-start | bytes 786440 | tf_op jit(solution)/shard_map/ppermute | solution.py:61
  8.6 2.6 %collective-permute-start.4 = (bf16[2,256,256]{2,1,0:T(8,128)(2,1)S(1)}, bf16[2,256,256]{2,1,0:T(8,128)(2,1)S(1)}, u32[]{:S(2)}, u32[]{:S(2)}) collective-permute-start(bf16[2,256,256]{2,1,0:T(8,128)(2,1)S(1)} %pad_maximum_fusion.1.refs_0_), channel_id=1, source_target_pairs={{0,16},{4,20},{8,24},{12,28},{16,0},{20,4},{24,8},{28,12},{1,17},{... | collective-permute-start | bytes 786440 | tf_op jit(solution)/shard_map/ppermute | solution.py:57
  11.2 0.9 collective-permute-done.1.refs_1_
  12.1 5.8 %collective-permute-done.2.refs_2_ = bf16[2,256,256]{2,1,0:T(8,128)(2,1)S(1)} collective-permute-done((bf16[2,256,256]{2,1,0:T(8,128)(2,1)S(1)}, bf16[2,256,256]{2,1,0:T(8,128)(2,1)S(1)}, u32[]{:S(2)}, u32[]{:S(2)}) %collective-permute-start.2) | collective-permute-done | bytes 262176 | tf_op jit(solution)/shard_map/ppermute | solution.py:57
  17.9 0.4 collective-permute-start.6
  18.3 0.1 pad_maximum_fusion
  18.3 0.1 collective-permute-start.10
  18.4 0.9 copy-done
  19.3 3.5 %collective-permute-done.4.refs_4_ = bf16[2,256,256]{2,1,0:T(8,128)(2,1)S(1)} collective-permute-done((bf16[2,256,256]{2,1,0:T(8,128)(2,1)S(1)}, bf16[2,256,256]{2,1,0:T(8,128)(2,1)S(1)}, u32[]{:S(2)}, u32[]{:S(2)}) %collective-permute-start.4) | collective-permute-done | bytes 262176 | tf_op jit(solution)/shard_map/ppermute | solution.py:57
  22.7 2.2 %collective-permute-done.6.refs_3_ = bf16[2,256,256]{2,1,0:T(8,128)(2,1)S(1)} collective-permute-done((bf16[2,256,256]{2,1,0:T(8,128)(2,1)S(1)}, bf16[2,256,256]{2,1,0:T(8,128)(2,1)S(1)}, u32[]{:S(2)}, u32[]{:S(2)}) %collective-permute-start.6) | collective-permute-done | bytes 262176 | tf_op jit(solution)/shard_map/ppermute | solution.py:57
  24.9 0.9 collective-permute-start.7
  26.4 0.0 copy-start.4
  26.4 0.0 copy-start.5
  26.5 0.6 copy-done.4
  27.1 0.0 copy-done.5
  27.1 0.1 pad_add_fusion.io_ref.idx
  27.2 0.0 collective-permute-start.8
  27.2 1.1 %collective-permute-done.8.ix_ref = s32[25]{0:T(128)S(1)} collective-permute-done((s32[25]{0:T(128)S(1)}, s32[25]{0:T(128)S(1)}, u32[]{:S(2)}, u32[]{:S(2)}) %collective-permute-start.8) | collective-permute-done | bytes 132 | tf_op jit(solution)/shard_map/ppermute | solution.py:61
  28.3 0.8 collective-permute-done.5.refs_6_
  29.1 2.2 %collective-permute-done.7.refs_5_ = bf16[2,256,256]{2,1,0:T(8,128)(2,1)S(1)} collective-permute-done((bf16[2,256,256]{2,1,0:T(8,128)(2,1)S(1)}, bf16[2,256,256]{2,1,0:T(8,128)(2,1)S(1)}, u32[]{:S(2)}, u32[]{:S(2)}) %collective-permute-start.7) | collective-permute-done | bytes 262176 | tf_op jit(solution)/shard_map/ppermute | solution.py:57
  31.3 1.1 %collective-permute-start.11 = (bf16[2,256,256]{2,1,0:T(8,128)(2,1)S(1)}, bf16[2,256,256]{2,1,0:T(8,128)(2,1)S(1)}, u32[]{:S(2)}, u32[]{:S(2)}) collective-permute-start(bf16[2,256,256]{2,1,0:T(8,128)(2,1)S(1)} %collective-permute-done.5.refs_6_), channel_id=1, source_target_pairs={{0,4},{4,0},{8,12},{12,8},{16,20},{20,16},{24,28},{28,24},{1,5},{5... | collective-permute-start | bytes 786440 | tf_op jit(solution)/shard_map/ppermute | solution.py:57
  32.4 5.3 %collective-permute-done.11.refs_7_ = bf16[2,256,256]{2,1,0:T(8,128)(2,1)S(1)} collective-permute-done((bf16[2,256,256]{2,1,0:T(8,128)(2,1)S(1)}, bf16[2,256,256]{2,1,0:T(8,128)(2,1)S(1)}, u32[]{:S(2)}, u32[]{:S(2)}) %collective-permute-start.11) | collective-permute-done | bytes 262176 | tf_op jit(solution)/shard_map/ppermute | solution.py:57
  37.6 1.6 %forward_product.1 = (bf16[512,256]{1,0:T(8,128)(2,1)S(1)}, bf16[512,256]{1,0:T(8,128)(2,1)S(1)}) custom-call(s32[25]{0:T(128)S(1)} %pad_add_fusion.io_ref.idx, s32[25]{0:T(128)S(1)} %collective-permute-done.8.ix_ref, bf16[12,128,128]{2,1,0:T(8,128)(2,1)S(1)} %bitcast.22, bf16[12,128,128]{2,1,0:T(8,128)(2,1)S(1)} %collective-permute-done.9.ax_ref, ...), custom_call_target="tpu_custom_call" | custom-call | flops 201326592 | bytes 2097152 | tf_op jit(solution)/shard_map/forward_product/pallas_call | solution.py:100
  39.3 0.0 copy-start.3
  39.3 3.3 %collective-permute-start.14 = (bf16[512,256]{1,0:T(8,128)(2,1)S(1)}, bf16[512,256]{1,0:T(8,128)(2,1)S(1)}, u32[]{:S(2)}, u32[]{:S(2)}) collective-permute-start(bf16[512,256]{1,0:T(8,128)(2,1)S(1)} %get-tuple-element.56.refs_3_), channel_id=1, source_target_pairs={{0,2},{1,3},{2,0},{3,1},{4,6},{5,7},{6,4},{7,5},{8,10},{9,11},{10,... | collective-permute-start | bytes 786440 | tf_op jit(solution)/shard_map/ppermute | solution.py:61
  42.6 0.1 collective-permute-start.15
  42.7 0.5 collective-permute-start.13
  43.2 4.6 %collective-permute-done.14.refs_7_ = bf16[512,256]{1,0:T(8,128)(2,1)S(1)} collective-permute-done((bf16[512,256]{1,0:T(8,128)(2,1)S(1)}, bf16[512,256]{1,0:T(8,128)(2,1)S(1)}, u32[]{:S(2)}, u32[]{:S(2)}) %collective-permute-start.14) | collective-permute-done | bytes 262176 | tf_op jit(solution)/shard_map/ppermute | solution.py:61
  47.8 2.8 %collective-permute-done.15.refs_8_ = bf16[512,256]{1,0:T(8,128)(2,1)S(1)} collective-permute-done((bf16[512,256]{1,0:T(8,128)(2,1)S(1)}, bf16[512,256]{1,0:T(8,128)(2,1)S(1)}, u32[]{:S(2)}, u32[]{:S(2)}) %collective-permute-start.15) | collective-permute-done | bytes 262176 | tf_op jit(solution)/shard_map/ppermute | solution.py:61
  50.6 1.5 %collective-permute-done.17.refs_10_ = bf16[512,256]{1,0:T(8,128)(2,1)S(1)} collective-permute-done((bf16[512,256]{1,0:T(8,128)(2,1)S(1)}, bf16[512,256]{1,0:T(8,128)(2,1)S(1)}, u32[]{:S(2)}, u32[]{:S(2)}) %collective-permute-start.17) | collective-permute-done | bytes 262176 | tf_op jit(solution)/shard_map/ppermute | solution.py:61
  52.1 5.6 %dense_and_backward.1 = (bf16[256,512]{1,0:T(8,128)(2,1)}, bf16[144,512]{1,0:T(8,128)(2,1)S(1)}, bf16[256,512]{1,0:T(8,128)(2,1)S(1)}, bf16[256,512]{1,0:T(8,128...) custom-call(bf16[512,512]{1,0:T(8,128)(2,1)S(1)} %copy-done.2, ...), custom_call_target="tpu_custom_call" | custom-call | flops 1342177280 | bytes 4194304 | tf_op jit(solution)/shard_map/dense_and_backward/pallas_call | solution.py:198
  57.8 0.1 collective-permute-start.18
  57.9 0.4 collective-permute-start.21
  58.2 5.2 %collective-permute-done.18 = bf16[144,512]{1,0:T(8,128)(2,1)S(1)} collective-permute-done((bf16[144,512]{1,0:T(8,128)(2,1)S(1)}, bf16[144,512]{1,0:T(8,128)(2,1)S(1)}, u32[]{:S(2)}, u32[]{:S(2)}) %collective-permute-start.18) | collective-permute-done | bytes 147488 | tf_op jit(solution)/shard_map/ppermute | solution.py:57
  63.5 0.1 select_select_fusion.1
  63.6 0.7 collective-permute-start.19
  64.3 2.4 %collective-permute-done.21 = bf16[256,512]{1,0:T(8,128)(2,1)S(1)} collective-permute-done((bf16[256,512]{1,0:T(8,128)(2,1)S(1)}, bf16[256,512]{1,0:T(8,128)(2,1)S(1)}, u32[]{:S(2)}, u32[]{:S(2)}) %collective-permute-start.21) | collective-permute-done | bytes 262176 | tf_op jit(solution)/shard_map/ppermute | solution.py:57
  66.6 0.1 add_convert_fusion.2
  66.7 0.4 collective-permute-start.22
  67.2 2.3 %collective-permute-start.23 = (bf16[256,512]{1,0:T(8,128)(2,1)S(1)}, bf16[256,512]{1,0:T(8,128)(2,1)S(1)}, u32[]{:S(2)}, u32[]{:S(2)}) collective-permute-start(bf16[256,512]{1,0:T(8,128)(2,1)S(1)} %add_convert_fusion.2), channel_id=1, source_target_pairs={{0,8},{4,12},{8,0},{12,4},{16,24},{20,28},{24,16},{28,20},{1,9},{5... | collective-permute-start | bytes 786440 | tf_op jit(solution)/shard_map/ppermute | solution.py:57
  69.5 1.0 %collective-permute-done.19 = bf16[144,512]{1,0:T(8,128)(2,1)S(1)} collective-permute-done((bf16[144,512]{1,0:T(8,128)(2,1)S(1)}, bf16[144,512]{1,0:T(8,128)(2,1)S(1)}, u32[]{:S(2)}, u32[]{:S(2)}) %collective-permute-start.19) | collective-permute-done | bytes 147488 | tf_op jit(solution)/shard_map/ppermute | solution.py:57
  70.6 0.1 select_select_fusion
  70.6 0.9 collective-permute-start.24
  71.5 3.0 %collective-permute-start.20 = (bf16[144,512]{1,0:T(8,128)(2,1)S(1)}, bf16[144,512]{1,0:T(8,128)(2,1)S(1)}, u32[]{:S(2)}, u32[]{:S(2)}) collective-permute-start(bf16[144,512]{1,0:T(8,128)(2,1)S(1)} %pad_maximum_fusion.4), channel_id=1, source_target_pairs={{0,16},{4,20},{8,24},{12,28},{16,0},{20,4},{24,8},{28,12},{1,17},{... | collective-permute-start | bytes 442376 | tf_op jit(solution)/shard_map/ppermute | solution.py:57
  74.5 1.6 %collective-permute-done.22 = bf16[256,512]{1,0:T(8,128)(2,1)S(1)} collective-permute-done((bf16[256,512]{1,0:T(8,128)(2,1)S(1)}, bf16[256,512]{1,0:T(8,128)(2,1)S(1)}, u32[]{:S(2)}, u32[]{:S(2)}) %collective-permute-start.22) | collective-permute-done | bytes 262176 | tf_op jit(solution)/shard_map/ppermute | solution.py:57
  76.1 0.1 convert_add_fusion
  76.2 1.5 %collective-permute-done.20 = bf16[144,512]{1,0:T(8,128)(2,1)S(1)} collective-permute-done((bf16[144,512]{1,0:T(8,128)(2,1)S(1)}, bf16[144,512]{1,0:T(8,128)(2,1)S(1)}, u32[]{:S(2)}, u32[]{:S(2)}) %collective-permute-start.20) | collective-permute-done | bytes 147488 | tf_op jit(solution)/shard_map/ppermute | solution.py:57
  77.7 2.9 %collective-permute-start.28 = (bf16[256,512]{1,0:T(8,128)(2,1)S(1)}, bf16[256,512]{1,0:T(8,128)(2,1)S(1)}, u32[]{:S(2)}, u32[]{:S(2)}) collective-permute-start(bf16[256,512]{1,0:T(8,128)(2,1)S(1)} %convert_add_fusion), channel_id=1, source_target_pairs={{0,16},{4,20},{8,24},{12,28},{16,0},{20,4},{24,8},{28,12},{1,17},{... | collective-permute-start | bytes 786440 | tf_op jit(solution)/shard_map/ppermute | solution.py:57
  80.6 0.1 add_convert_fusion.1
  80.7 6.1 %collective-permute-start.29 = (bf16[256,512]{1,0:T(8,128)(2,1)S(1)}, bf16[256,512]{1,0:T(8,128)(2,1)S(1)}, u32[]{:S(2)}, u32[]{:S(2)}) collective-permute-start(bf16[256,512]{1,0:T(8,128)(2,1)S(1)} %add_convert_fusion.1), channel_id=1, source_target_pairs={{0,8},{4,12},{8,0},{12,4},{16,24},{20,28},{24,16},{28,20},{1,9},{5... | collective-permute-start | bytes 786440 | tf_op jit(solution)/shard_map/ppermute | solution.py:57
  86.9 0.1 collective-permute-start.25
  87.0 4.9 %collective-permute-done.25.refs_1_ = bf16[128,512]{1,0:T(8,128)(2,1)S(1)} collective-permute-done((bf16[128,512]{1,0:T(8,128)(2,1)S(1)}, bf16[128,512]{1,0:T(8,128)(2,1)S(1)}, u32[]{:S(2)}, u32[]{:S(2)}) %collective-permute-start.25) | collective-permute-done | bytes 131104 | tf_op jit(solution)/shard_map/ppermute | solution.py:61
  92.0 0.1 collective-permute-start.26
  92.0 0.6 slice_add_fusion
  92.6 0.4 collective-permute-done.29
  93.0 0.2 collective-permute-done.27
  93.2 0.8 add_convert_fusion
  94.1 1.1 %place_weight_gradient.1 = f32[512,512]{1,0:T(8,128)} custom-call(bf16[128,512]{1,0:T(8,128)(2,1)S(1)} %slice.109.refs_0_, bf16[128,512]{1,0:T(8,128)(2,1)S(1)} %collective-permute-done.25.refs_1_, bf16[128,512]{1,0:T(8,128)(2,1)S(1)} %get-tuple-element.83.refs_2_, bf16[128,512]{1,0:T(8,128)(2,1)S(1)} %get-tuple-element.82.refs_3_), custom_call_target="tpu_custom_call" | custom-call | flops 262144 | bytes 1572864 | tf_op jit(solution)/shard_map/place_weight_gradient/pallas_call | solution.py:235
  (37 shorter events, 0.4 us)
Async XLA Ops:
  0.6 1.9 %collective-permute-start = (bf16[256,512]{1,0:T(8,128)(2,1)}, bf16[256,512]{1,0:T(8,128)(2,1)S(1)}, u32[]{:S(2)}, u32[]{:S(2)}) collective-permute-start(bf16[256,512]{1,0:T(8,128)(2,1)} %param.8), channel_id=1, source_target_pairs={{0,1},{1,0},{2,3},{3,2},{4,5},{5,4},{6,7},{7,6},{8,9},{9,8},{10,11... | collective-permute-start | bytes 786440 | tf_op jit(solution)/shard_map/ppermute | solution.py:61
  2.5 4.6 %copy-start.1 = (bf16[256,512]{1,0:T(8,128)(2,1)S(1)}, bf16[256,512]{1,0:T(8,128)(2,1)}, u32[]{:S(2)}) copy-start(bf16[256,512]{1,0:T(8,128)(2,1)} %refs_0_) | copy-start | bytes 786436
  2.6 9.6 %collective-permute-start.1 = (bf16[2,256,256]{2,1,0:T(8,128)(2,1)S(1)}, bf16[2,256,256]{2,1,0:T(8,128)(2,1)S(1)}, u32[]{:S(2)}, u32[]{:S(2)}) collective-permute-start(bf16[2,256,256]{2,1,0:T(8,128)(2,1)S(1)} %pad_maximum_fusion.1.refs_0_), channel_id=1, source_target_pairs={{0,4},{4,0},{8,12},{12,8},{16,20},{20,16},{24,28},{28,24},{1,5},{5... | collective-permute-start | bytes 786440 | tf_op jit(solution)/shard_map/ppermute | solution.py:57
  5.5 12.4 %collective-permute-start.2 = (bf16[2,256,256]{2,1,0:T(8,128)(2,1)S(1)}, bf16[2,256,256]{2,1,0:T(8,128)(2,1)S(1)}, u32[]{:S(2)}, u32[]{:S(2)}) collective-permute-start(bf16[2,256,256]{2,1,0:T(8,128)(2,1)S(1)} %pad_maximum_fusion.1.refs_0_), channel_id=1, source_target_pairs={{0,8},{4,12},{8,0},{12,4},{16,24},{20,28},{24,16},{28,20},{1,9},{5... | collective-permute-start | bytes 786440 | tf_op jit(solution)/shard_map/ppermute | solution.py:57
  7.1 11.1 %collective-permute-start.3 = (bf16[256,512]{1,0:T(8,128)(2,1)S(1)}, bf16[256,512]{1,0:T(8,128)(2,1)S(1)}, u32[]{:S(2)}, u32[]{:S(2)}) collective-permute-start(bf16[256,512]{1,0:T(8,128)(2,1)S(1)} %copy-done.1), channel_id=1, source_target_pairs={{0,2},{1,3},{2,0},{3,1},{4,6},{5,7},{6,4},{7,5},{8,10},{9,11},{10,... | collective-permute-start | bytes 786440 | tf_op jit(solution)/shard_map/ppermute | solution.py:61
  8.6 14.1 %collective-permute-start.4 = (bf16[2,256,256]{2,1,0:T(8,128)(2,1)S(1)}, bf16[2,256,256]{2,1,0:T(8,128)(2,1)S(1)}, u32[]{:S(2)}, u32[]{:S(2)}) collective-permute-start(bf16[2,256,256]{2,1,0:T(8,128)(2,1)S(1)} %pad_maximum_fusion.1.refs_0_), channel_id=1, source_target_pairs={{0,16},{4,20},{8,24},{12,28},{16,0},{20,4},{24,8},{28,12},{1,17},{... | collective-permute-start | bytes 786440 | tf_op jit(solution)/shard_map/ppermute | solution.py:57
  17.9 7.0 %collective-permute-start.6 = (bf16[2,256,256]{2,1,0:T(8,128)(2,1)S(1)}, bf16[2,256,256]{2,1,0:T(8,128)(2,1)S(1)}, u32[]{:S(2)}, u32[]{:S(2)}) collective-permute-start(bf16[2,256,256]{2,1,0:T(8,128)(2,1)S(1)} %collective-permute-done.2.refs_2_), channel_id=1, source_target_pairs={{0,4},{4,0},{8,12},{12,8},{16,20},{20,16},{24,28},{28,24},{1,5},{5... | collective-permute-start | bytes 786440 | tf_op jit(solution)/shard_map/ppermute | solution.py:57
  18.3 1.0 %copy-start = (bf16[1,1,12,128,128]{4,3,2,1,0:T(8,128)(2,1)S(1)}, bf16[1,1,12,128,128]{4,3,2,1,0:T(8,128)(2,1)}, u32[]{:S(2)}) copy-start(bf16[1,1,12,128,128]{4,3,2,1,0:T(8,128)(2,1)} %param.9) | copy-start | bytes 1179652
  18.3 10.8 %collective-permute-start.10 = (bf16[2,256,512]{2,1,0:T(8,128)(2,1)S(1)}, bf16[2,256,512]{2,1,0:T(8,128)(2,1)S(1)}, u32[]{:S(2)}, u32[]{:S(2)}) collective-permute-start(bf16[2,256,512]{2,1,0:T(8,128)(2,1)S(1)} %pad_maximum_fusion), channel_id=1, source_target_pairs={{0,1},{1,0},{2,3},{3,2},{4,5},{5,4},{6,7},{7,6},{8,9},{9,8},{10,11... | collective-permute-start | bytes 1572872 | tf_op jit(solution)/shard_map/ppermute | solution.py:61
  19.3 9.8 %collective-permute-start.9 = (bf16[12,128,128]{2,1,0:T(8,128)(2,1)S(1)}, bf16[12,128,128]{2,1,0:T(8,128)(2,1)S(1)}, u32[]{:S(2)}, u32[]{:S(2)}) collective-permute-start(bf16[12,128,128]{2,1,0:T(8,128)(2,1)S(1)} %bitcast.21), channel_id=1, source_target_pairs={{0,1},{1,0},{2,3},{3,2},{4,5},{5,4},{6,7},{7,6},{8,9},{9,8},{10,11... | collective-permute-start | bytes 1179656 | tf_op jit(solution)/shard_map/ppermute | solution.py:61
  22.7 6.4 %collective-permute-start.5 = (bf16[2,256,256]{2,1,0:T(8,128)(2,1)S(1)}, bf16[2,256,256]{2,1,0:T(8,128)(2,1)S(1)}, u32[]{:S(2)}, u32[]{:S(2)}) collective-permute-start(bf16[2,256,256]{2,1,0:T(8,128)(2,1)S(1)} %collective-permute-done.4.refs_4_), channel_id=1, source_target_pairs={{0,8},{4,12},{8,0},{12,4},{16,24},{20,28},{24,16},{28,20},{1,9},{5... | collective-permute-start | bytes 786440 | tf_op jit(solution)/shard_map/ppermute | solution.py:57
  24.9 6.4 %collective-permute-start.7 = (bf16[2,256,256]{2,1,0:T(8,128)(2,1)S(1)}, bf16[2,256,256]{2,1,0:T(8,128)(2,1)S(1)}, u32[]{:S(2)}, u32[]{:S(2)}) collective-permute-start(bf16[2,256,256]{2,1,0:T(8,128)(2,1)S(1)} %collective-permute-done.4.refs_4_), channel_id=1, source_target_pairs={{0,4},{4,0},{8,12},{12,8},{16,20},{20,16},{24,28},{28,24},{1,5},{5... | collective-permute-start | bytes 786440 | tf_op jit(solution)/shard_map/ppermute | solution.py:57
  26.4 0.7 copy-start.4
  26.4 0.7 copy-start.5
  27.2 24.9 %copy-start.2 = (bf16[512,512]{1,0:T(8,128)(2,1)S(1)}, bf16[512,512]{1,0:T(8,128)(2,1)}, u32[]{:S(2)}) copy-start(bf16[512,512]{1,0:T(8,128)(2,1)} %w_ref.1) | copy-start | bytes 1572868
  27.2 1.1 %collective-permute-start.8 = (s32[25]{0:T(128)S(1)}, s32[25]{0:T(128)S(1)}, u32[]{:S(2)}, u32[]{:S(2)}) collective-permute-start(s32[25]{0:T(128)S(1)} %pad_add_fusion.io_ref.idx), channel_id=1, source_target_pairs={{0,1},{1,0},{2,3},{3,2},{4,5},{5,4},{6,7},{7,6},{8,9},{9,8},{10,11... | collective-permute-start | bytes 308 | tf_op jit(solution)/shard_map/ppermute | solution.py:61
  31.3 6.4 %collective-permute-start.11 = (bf16[2,256,256]{2,1,0:T(8,128)(2,1)S(1)}, bf16[2,256,256]{2,1,0:T(8,128)(2,1)S(1)}, u32[]{:S(2)}, u32[]{:S(2)}) collective-permute-start(bf16[2,256,256]{2,1,0:T(8,128)(2,1)S(1)} %collective-permute-done.5.refs_6_), channel_id=1, source_target_pairs={{0,4},{4,0},{8,12},{12,8},{16,20},{20,16},{24,28},{28,24},{1,5},{5... | collective-permute-start | bytes 786440 | tf_op jit(solution)/shard_map/ppermute | solution.py:57
  39.3 12.8 %copy-start.3 = (f32[512]{0:T(512)S(1)}, f32[512]{0:T(512)}, u32[]{:S(2)}) copy-start(f32[512]{0:T(512)} %param.14) | copy-start | bytes 6148
  39.3 8.5 %collective-permute-start.14 = (bf16[512,256]{1,0:T(8,128)(2,1)S(1)}, bf16[512,256]{1,0:T(8,128)(2,1)S(1)}, u32[]{:S(2)}, u32[]{:S(2)}) collective-permute-start(bf16[512,256]{1,0:T(8,128)(2,1)S(1)} %get-tuple-element.56.refs_3_), channel_id=1, source_target_pairs={{0,2},{1,3},{2,0},{3,1},{4,6},{5,7},{6,4},{7,5},{8,10},{9,11},{10,... | collective-permute-start | bytes 786440 | tf_op jit(solution)/shard_map/ppermute | solution.py:61
  42.6 8.0 %collective-permute-start.15 = (bf16[512,256]{1,0:T(8,128)(2,1)S(1)}, bf16[512,256]{1,0:T(8,128)(2,1)S(1)}, u32[]{:S(2)}, u32[]{:S(2)}) collective-permute-start(bf16[512,256]{1,0:T(8,128)(2,1)S(1)} %get-tuple-element.57.refs_4_), channel_id=1, source_target_pairs={{0,2},{1,3},{2,0},{3,1},{4,6},{5,7},{6,4},{7,5},{8,10},{9,11},{10,... | collective-permute-start | bytes 786440 | tf_op jit(solution)/shard_map/ppermute | solution.py:61
  42.7 7.9 %collective-permute-start.12 = (bf16[512,256]{1,0:T(8,128)(2,1)S(1)}, bf16[512,256]{1,0:T(8,128)(2,1)S(1)}, u32[]{:S(2)}, u32[]{:S(2)}) collective-permute-start(bf16[512,256]{1,0:T(8,128)(2,1)S(1)} %get-tuple-element.56.refs_3_), channel_id=1, source_target_pairs={{0,1},{1,0},{2,3},{3,2},{4,5},{5,4},{6,7},{7,6},{8,9},{9,8},{10,11... | collective-permute-start | bytes 786440 | tf_op jit(solution)/shard_map/ppermute | solution.py:61
  42.7 7.9 %collective-permute-start.13 = (bf16[512,256]{1,0:T(8,128)(2,1)S(1)}, bf16[512,256]{1,0:T(8,128)(2,1)S(1)}, u32[]{:S(2)}, u32[]{:S(2)}) collective-permute-start(bf16[512,256]{1,0:T(8,128)(2,1)S(1)} %get-tuple-element.57.refs_4_), channel_id=1, source_target_pairs={{0,1},{1,0},{2,3},{3,2},{4,5},{5,4},{6,7},{7,6},{8,9},{9,8},{10,11... | collective-permute-start | bytes 786440 | tf_op jit(solution)/shard_map/ppermute | solution.py:61
  47.8 2.8 %collective-permute-start.16 = (bf16[512,256]{1,0:T(8,128)(2,1)S(1)}, bf16[512,256]{1,0:T(8,128)(2,1)S(1)}, u32[]{:S(2)}, u32[]{:S(2)}) collective-permute-start(bf16[512,256]{1,0:T(8,128)(2,1)S(1)} %collective-permute-done.14.refs_7_), channel_id=1, source_target_pairs={{0,1},{1,0},{2,3},{3,2},{4,5},{5,4},{6,7},{7,6},{8,9},{9,8},{10,11... | collective-permute-start | bytes 786440 | tf_op jit(solution)/shard_map/ppermute | solution.py:61
  50.6 1.5 %collective-permute-start.17 = (bf16[512,256]{1,0:T(8,128)(2,1)S(1)}, bf16[512,256]{1,0:T(8,128)(2,1)S(1)}, u32[]{:S(2)}, u32[]{:S(2)}) collective-permute-start(bf16[512,256]{1,0:T(8,128)(2,1)S(1)} %collective-permute-done.15.refs_8_), channel_id=1, source_target_pairs={{0,1},{1,0},{2,3},{3,2},{4,5},{5,4},{6,7},{7,6},{8,9},{9,8},{10,11... | collective-permute-start | bytes 786440 | tf_op jit(solution)/shard_map/ppermute | solution.py:61
  57.8 5.7 %collective-permute-start.18 = (bf16[144,512]{1,0:T(8,128)(2,1)S(1)}, bf16[144,512]{1,0:T(8,128)(2,1)S(1)}, u32[]{:S(2)}, u32[]{:S(2)}) collective-permute-start(bf16[144,512]{1,0:T(8,128)(2,1)S(1)} %get-tuple-element.59), channel_id=1, source_target_pairs={{0,8},{4,12},{8,0},{12,4},{16,24},{20,28},{24,16},{28,20},{1,9},{5... | collective-permute-start | bytes 442376 | tf_op jit(solution)/shard_map/ppermute | solution.py:57
  57.9 8.8 %collective-permute-start.21 = (bf16[256,512]{1,0:T(8,128)(2,1)S(1)}, bf16[256,512]{1,0:T(8,128)(2,1)S(1)}, u32[]{:S(2)}, u32[]{:S(2)}) collective-permute-start(bf16[256,512]{1,0:T(8,128)(2,1)S(1)} %get-tuple-element.64), channel_id=1, source_target_pairs={{0,4},{4,0},{8,12},{12,8},{16,20},{20,16},{24,28},{28,24},{1,5},{5... | collective-permute-start | bytes 786440 | tf_op jit(solution)/shard_map/ppermute | solution.py:57
  63.6 6.9 %collective-permute-start.19 = (bf16[144,512]{1,0:T(8,128)(2,1)S(1)}, bf16[144,512]{1,0:T(8,128)(2,1)S(1)}, u32[]{:S(2)}, u32[]{:S(2)}) collective-permute-start(bf16[144,512]{1,0:T(8,128)(2,1)S(1)} %pad_maximum_fusion.3), channel_id=1, source_target_pairs={{0,4},{4,0},{8,12},{12,8},{16,20},{20,16},{24,28},{28,24},{1,5},{5... | collective-permute-start | bytes 442376 | tf_op jit(solution)/shard_map/ppermute | solution.py:57
  66.7 9.4 %collective-permute-start.22 = (bf16[256,512]{1,0:T(8,128)(2,1)S(1)}, bf16[256,512]{1,0:T(8,128)(2,1)S(1)}, u32[]{:S(2)}, u32[]{:S(2)}) collective-permute-start(bf16[256,512]{1,0:T(8,128)(2,1)S(1)} %get-tuple-element.66), channel_id=1, source_target_pairs={{0,4},{4,0},{8,12},{12,8},{16,20},{20,16},{24,28},{28,24},{1,5},{5... | collective-permute-start | bytes 786440 | tf_op jit(solution)/shard_map/ppermute | solution.py:57
  67.2 8.9 %collective-permute-start.23 = (bf16[256,512]{1,0:T(8,128)(2,1)S(1)}, bf16[256,512]{1,0:T(8,128)(2,1)S(1)}, u32[]{:S(2)}, u32[]{:S(2)}) collective-permute-start(bf16[256,512]{1,0:T(8,128)(2,1)S(1)} %add_convert_fusion.2), channel_id=1, source_target_pairs={{0,8},{4,12},{8,0},{12,4},{16,24},{20,28},{24,16},{28,20},{1,9},{5... | collective-permute-start | bytes 786440 | tf_op jit(solution)/shard_map/ppermute | solution.py:57
  70.6 10.0 %collective-permute-start.24 = (bf16[256,512]{1,0:T(8,128)(2,1)S(1)}, bf16[256,512]{1,0:T(8,128)(2,1)S(1)}, u32[]{:S(2)}, u32[]{:S(2)}) collective-permute-start(bf16[256,512]{1,0:T(8,128)(2,1)S(1)} %get-tuple-element.70), channel_id=1, source_target_pairs={{0,4},{4,0},{8,12},{12,8},{16,20},{20,16},{24,28},{28,24},{1,5},{5... | collective-permute-start | bytes 786440 | tf_op jit(solution)/shard_map/ppermute | solution.py:57
  71.5 6.2 %collective-permute-start.20 = (bf16[144,512]{1,0:T(8,128)(2,1)S(1)}, bf16[144,512]{1,0:T(8,128)(2,1)S(1)}, u32[]{:S(2)}, u32[]{:S(2)}) collective-permute-start(bf16[144,512]{1,0:T(8,128)(2,1)S(1)} %pad_maximum_fusion.4), channel_id=1, source_target_pairs={{0,16},{4,20},{8,24},{12,28},{16,0},{20,4},{24,8},{28,12},{1,17},{... | collective-permute-start | bytes 442376 | tf_op jit(solution)/shard_map/ppermute | solution.py:57
  77.7 14.9 %collective-permute-start.28 = (bf16[256,512]{1,0:T(8,128)(2,1)S(1)}, bf16[256,512]{1,0:T(8,128)(2,1)S(1)}, u32[]{:S(2)}, u32[]{:S(2)}) collective-permute-start(bf16[256,512]{1,0:T(8,128)(2,1)S(1)} %convert_add_fusion), channel_id=1, source_target_pairs={{0,16},{4,20},{8,24},{12,28},{16,0},{20,4},{24,8},{28,12},{1,17},{... | collective-permute-start | bytes 786440 | tf_op jit(solution)/shard_map/ppermute | solution.py:57
  80.7 12.3 %collective-permute-start.29 = (bf16[256,512]{1,0:T(8,128)(2,1)S(1)}, bf16[256,512]{1,0:T(8,128)(2,1)S(1)}, u32[]{:S(2)}, u32[]{:S(2)}) collective-permute-start(bf16[256,512]{1,0:T(8,128)(2,1)S(1)} %add_convert_fusion.1), channel_id=1, source_target_pairs={{0,8},{4,12},{8,0},{12,4},{16,24},{20,28},{24,16},{28,20},{1,9},{5... | collective-permute-start | bytes 786440 | tf_op jit(solution)/shard_map/ppermute | solution.py:57
  86.8 6.4 %collective-permute-start.27 = (bf16[256,512]{1,0:T(8,128)(2,1)S(1)}, bf16[256,512]{1,0:T(8,128)(2,1)S(1)}, u32[]{:S(2)}, u32[]{:S(2)}) collective-permute-start(bf16[256,512]{1,0:T(8,128)(2,1)S(1)} %get-tuple-element.75), channel_id=1, source_target_pairs={{0,4},{4,0},{8,12},{12,8},{16,20},{20,16},{24,28},{28,24},{1,5},{5... | collective-permute-start | bytes 786440 | tf_op jit(solution)/shard_map/ppermute | solution.py:57
  86.9 5.0 %collective-permute-start.25 = (bf16[128,512]{1,0:T(8,128)(2,1)S(1)}, bf16[128,512]{1,0:T(8,128)(2,1)S(1)}, u32[]{:S(2)}, u32[]{:S(2)}) collective-permute-start(bf16[128,512]{1,0:T(8,128)(2,1)S(1)} %slice.109.refs_0_), channel_id=1, source_target_pairs={{0,2},{1,3},{2,0},{3,1},{4,6},{5,7},{6,4},{7,5},{8,10},{9,11},{10,... | collective-permute-start | bytes 393224 | tf_op jit(solution)/shard_map/ppermute | solution.py:61
  92.0 2.1 %collective-permute-start.26 = (bf16[2,128,512]{2,1,0:T(8,128)(2,1)S(1)}, bf16[2,128,512]{2,1,0:T(8,128)(2,1)S(1)}, u32[]{:S(2)}, u32[]{:S(2)}) collective-permute-start(bf16[2,128,512]{2,1,0:T(8,128)(2,1)S(1)} %pad_maximum_fusion.2), channel_id=1, source_target_pairs={{0,1},{1,0},{2,3},{3,2},{4,5},{5,4},{6,7},{7,6},{8,9},{9,8},{10,11... | collective-permute-start | bytes 786440 | tf_op jit(solution)/shard_map/ppermute | solution.py:61

commit v6 on v4

--- a/solution.py
+++ b/solution.py
@@ -139,10 +139,11 @@
             at = pl.multiple_of(xor_to(core, dk) * half, half)
             to = parts.at[dx, pl.ds(part * (rows // 2), rows // 2), pl.ds(at, half)]
             copies.append(pltpu.make_async_copy(ref, to, sems.at[lay.cols + n]))
-        for c in copies:
+        ups_copies, sum_copies = copies[: lay.cols], copies[lay.cols :]
+        for c in sum_copies + ups_copies:
             c.start()
         total[...] = jnp.zeros_like(total)
-        for c in copies:
+        for c in sum_copies:
             c.wait()
         own_half = pl.ds(pl.multiple_of(core * half, half), half)
         gb = jnp.zeros((1, width), F32)
@@ -157,6 +158,9 @@
             def _(pre=pre, sig=sig):
                 act_ref[...] = (pre * sig).astype(BF16)
 
+            if j == 0:
+                for c in ups_copies:
+                    c.wait()
             dpre = (up_all[sl, :].astype(F32) * sig * (1.0 + pre * (1.0 - sig))).astype(BF16)
             gb += jnp.sum(dpre.astype(F32), axis=0, keepdims=True)
             one = lax.dot_general(hidden[sl, own_half], dpre, (((0,), (0,)), ((), ())), preferred_element_type=F32)

time: 95.5 us -> 96.7 us (1.013)
  waiting for transfers between devices: 54.1 us -> 57.6 us
  starting transfers between devices: 27.1 us -> 24.3 us
    ppermute x13, starting transfers between devices: 9.14 us -> 6.62 us  [move_col(): return lax.ppermute(a, 'col', [(c, c ^ d) for c in range(self.cols)])]
    ppermute x17, waiting for transfers between devices: 40.8 us -> 43 us  [move_row(): return lax.ppermute(a, 'row', [(r, r ^ d) for r in range(self.rows)])]
    ppermute x13, waiting for transfers between devices: 13.3 us -> 14.6 us  [move_col(): return lax.ppermute(a, 'col', [(c, c ^ d) for c in range(self.cols)])]
where the time goes in v6:
time: 96.7 us; the launch traced here: 96.2 us
  waiting for transfers between devices  57.6 us (60%)
  starting transfers between devices  24.3 us (25%)
  Pallas kernels  8 us (8%)
  other arithmetic  3.17 us (3%)
  local copies, waits for them, and re-layouts  1.63 us (2%)
  between operations  1.5 us (2%)
    ppermute x17, waiting for transfers between devices, move_row(): return lax.ppermute(a, 'row', [(r, r ^ d) for r in range(self.rows)])  43 us
    ppermute x17, starting transfers between devices, move_row(): return lax.ppermute(a, 'row', [(r, r ^ d) for r in range(self.rows)])  17.7 us
    ppermute x13, waiting for transfers between devices, move_col(): return lax.ppermute(a, 'col', [(c, c ^ d) for c in range(self.cols)])  14.6 us
    ppermute x13, starting transfers between devices, move_col(): return lax.ppermute(a, 'col', [(c, c ^ d) for c in range(self.cols)])  6.62 us
    pallas_call x1, Pallas kernels, dense_and_backward(): pl.pallas_call(kernel, out_shape=[jax.ShapeDtypeStruct((node_dev, width),...  5.32 us
  transfers between devices with their start and end apart: 30, of which 21 were waited for; matrix products, arithmetic and copies ran while one was open for 3% of the time, Pallas kernels for 0%

profile of v6, /device:TPU:0, one launch (start us, length us, event | category | flops | bytes accessed | tf_op | source)
XLA Modules:
  0.0 96.2 jit_solution(16026238490393938391)
XLA Ops:
  0.6 0.5 collective-permute-start
  1.1 1.0 %select_bitcast_fusion = bf16[1,256,256]{2,1,0:T(8,128)(2,1)S(1)} fusion(bf16[256,512]{1,0:T(8,128)(2,1)} %param.8, pred[]{:T(512)S(6)} %eq.28), kind=kLoop, calls=%fused_computation.19 | loop fusion | flops 65536 | bytes 393217 | tf_op jit(solution)/shard_map/stack | solution.py:268
  2.1 0.4 collective-permute-done
  2.5 0.0 copy-start.1
  2.6 3.0 %collective-permute-start.1 = (bf16[2,256,256]{2,1,0:T(8,128)(2,1)S(1)}, bf16[2,256,256]{2,1,0:T(8,128)(2,1)S(1)}, u32[]{:S(2)}, u32[]{:S(2)}) collective-permute-start(bf16[2,256,256]{2,1,0:T(8,128)(2,1)S(1)} %pad_maximum_fusion.1.refs_0_), channel_id=1, source_target_pairs={{0,4},{4,0},{8,12},{12,8},{16,20},{20,16},{24,28},{28,24},{1,5},{5... | collective-permute-start | bytes 786440 | tf_op jit(solution)/shard_map/ppermute | solution.py:57
  5.5 1.6 %collective-permute-start.2 = (bf16[2,256,256]{2,1,0:T(8,128)(2,1)S(1)}, bf16[2,256,256]{2,1,0:T(8,128)(2,1)S(1)}, u32[]{:S(2)}, u32[]{:S(2)}) collective-permute-start(bf16[2,256,256]{2,1,0:T(8,128)(2,1)S(1)} %pad_maximum_fusion.1.refs_0_), channel_id=1, source_target_pairs={{0,8},{4,12},{8,0},{12,4},{16,24},{20,28},{24,16},{28,20},{1,9},{5... | collective-permute-start | bytes 786440 | tf_op jit(solution)/shard_map/ppermute | solution.py:57
  7.1 1.5 %collective-permute-start.3 = (bf16[256,512]{1,0:T(8,128)(2,1)S(1)}, bf16[256,512]{1,0:T(8,128)(2,1)S(1)}, u32[]{:S(2)}, u32[]{:S(2)}) collective-permute-start(bf16[256,512]{1,0:T(8,128)(2,1)S(1)} %copy-done.1), channel_id=1, source_target_pairs={{0,2},{1,3},{2,0},{3,1},{4,6},{5,7},{6,4},{7,5},{8,10},{9,11},{10,... | collective-permute-start | bytes 786440 | tf_op jit(solution)/shard_map/ppermute | solution.py:61
  8.6 2.6 %collective-permute-start.4 = (bf16[2,256,256]{2,1,0:T(8,128)(2,1)S(1)}, bf16[2,256,256]{2,1,0:T(8,128)(2,1)S(1)}, u32[]{:S(2)}, u32[]{:S(2)}) collective-permute-start(bf16[2,256,256]{2,1,0:T(8,128)(2,1)S(1)} %pad_maximum_fusion.1.refs_0_), channel_id=1, source_target_pairs={{0,16},{4,20},{8,24},{12,28},{16,0},{20,4},{24,8},{28,12},{1,17},{... | collective-permute-start | bytes 786440 | tf_op jit(solution)/shard_map/ppermute | solution.py:57
  11.2 0.9 collective-permute-done.1.refs_1_
  12.1 5.8 %collective-permute-done.2.refs_2_ = bf16[2,256,256]{2,1,0:T(8,128)(2,1)S(1)} collective-permute-done((bf16[2,256,256]{2,1,0:T(8,128)(2,1)S(1)}, bf16[2,256,256]{2,1,0:T(8,128)(2,1)S(1)}, u32[]{:S(2)}, u32[]{:S(2)}) %collective-permute-start.2) | collective-permute-done | bytes 262176 | tf_op jit(solution)/shard_map/ppermute | solution.py:57
  17.9 0.4 collective-permute-start.6
  18.3 0.1 pad_maximum_fusion
  18.3 0.1 collective-permute-start.10
  18.4 0.9 copy-done
  19.3 3.5 %collective-permute-done.4.refs_4_ = bf16[2,256,256]{2,1,0:T(8,128)(2,1)S(1)} collective-permute-done((bf16[2,256,256]{2,1,0:T(8,128)(2,1)S(1)}, bf16[2,256,256]{2,1,0:T(8,128)(2,1)S(1)}, u32[]{:S(2)}, u32[]{:S(2)}) %collective-permute-start.4) | collective-permute-done | bytes 262176 | tf_op jit(solution)/shard_map/ppermute | solution.py:57
  22.7 2.2 %collective-permute-done.6.refs_3_ = bf16[2,256,256]{2,1,0:T(8,128)(2,1)S(1)} collective-permute-done((bf16[2,256,256]{2,1,0:T(8,128)(2,1)S(1)}, bf16[2,256,256]{2,1,0:T(8,128)(2,1)S(1)}, u32[]{:S(2)}, u32[]{:S(2)}) %collective-permute-start.6) | collective-permute-done | bytes 262176 | tf_op jit(solution)/shard_map/ppermute | solution.py:57
  24.9 0.9 collective-permute-start.7
  26.4 0.0 copy-start.5
  26.5 0.6 copy-done.4
  27.1 0.0 copy-done.5
  27.1 0.1 pad_add_fusion.io_ref.idx
  27.2 0.0 collective-permute-start.8
  27.2 1.1 %collective-permute-done.8.ix_ref = s32[25]{0:T(128)S(1)} collective-permute-done((s32[25]{0:T(128)S(1)}, s32[25]{0:T(128)S(1)}, u32[]{:S(2)}, u32[]{:S(2)}) %collective-permute-start.8) | collective-permute-done | bytes 132 | tf_op jit(solution)/shard_map/ppermute | solution.py:61
  28.3 0.8 collective-permute-done.5.refs_6_
  29.1 2.2 %collective-permute-done.7.refs_5_ = bf16[2,256,256]{2,1,0:T(8,128)(2,1)S(1)} collective-permute-done((bf16[2,256,256]{2,1,0:T(8,128)(2,1)S(1)}, bf16[2,256,256]{2,1,0:T(8,128)(2,1)S(1)}, u32[]{:S(2)}, u32[]{:S(2)}) %collective-permute-start.7) | collective-permute-done | bytes 262176 | tf_op jit(solution)/shard_map/ppermute | solution.py:57
  31.3 1.1 %collective-permute-start.11 = (bf16[2,256,256]{2,1,0:T(8,128)(2,1)S(1)}, bf16[2,256,256]{2,1,0:T(8,128)(2,1)S(1)}, u32[]{:S(2)}, u32[]{:S(2)}) collective-permute-start(bf16[2,256,256]{2,1,0:T(8,128)(2,1)S(1)} %collective-permute-done.5.refs_6_), channel_id=1, source_target_pairs={{0,4},{4,0},{8,12},{12,8},{16,20},{20,16},{24,28},{28,24},{1,5},{5... | collective-permute-start | bytes 786440 | tf_op jit(solution)/shard_map/ppermute | solution.py:57
  32.4 5.3 %collective-permute-done.11.refs_7_ = bf16[2,256,256]{2,1,0:T(8,128)(2,1)S(1)} collective-permute-done((bf16[2,256,256]{2,1,0:T(8,128)(2,1)S(1)}, bf16[2,256,256]{2,1,0:T(8,128)(2,1)S(1)}, u32[]{:S(2)}, u32[]{:S(2)}) %collective-permute-start.11) | collective-permute-done | bytes 262176 | tf_op jit(solution)/shard_map/ppermute | solution.py:57
  37.6 1.6 %forward_product.1 = (bf16[512,256]{1,0:T(8,128)(2,1)S(1)}, bf16[512,256]{1,0:T(8,128)(2,1)S(1)}) custom-call(s32[25]{0:T(128)S(1)} %pad_add_fusion.io_ref.idx, s32[25]{0:T(128)S(1)} %collective-permute-done.8.ix_ref, bf16[12,128,128]{2,1,0:T(8,128)(2,1)S(1)} %bitcast.22, bf16[12,128,128]{2,1,0:T(8,128)(2,1)S(1)} %collective-permute-done.9.ax_ref, ...), custom_call_target="tpu_custom_call" | custom-call | flops 201326592 | bytes 2097152 | tf_op jit(solution)/shard_map/forward_product/pallas_call | solution.py:100
  39.3 0.0 copy-start.3
  39.3 3.1 %collective-permute-start.14 = (bf16[512,256]{1,0:T(8,128)(2,1)S(1)}, bf16[512,256]{1,0:T(8,128)(2,1)S(1)}, u32[]{:S(2)}, u32[]{:S(2)}) collective-permute-start(bf16[512,256]{1,0:T(8,128)(2,1)S(1)} %get-tuple-element.54.refs_3_), channel_id=1, source_target_pairs={{0,2},{1,3},{2,0},{3,1},{4,6},{5,7},{6,4},{7,5},{8,10},{9,11},{10,... | collective-permute-start | bytes 786440 | tf_op jit(solution)/shard_map/ppermute | solution.py:61
  42.4 0.1 collective-permute-start.15
  42.4 0.5 collective-permute-start.13
  43.0 4.6 %collective-permute-done.14.refs_7_ = bf16[512,256]{1,0:T(8,128)(2,1)S(1)} collective-permute-done((bf16[512,256]{1,0:T(8,128)(2,1)S(1)}, bf16[512,256]{1,0:T(8,128)(2,1)S(1)}, u32[]{:S(2)}, u32[]{:S(2)}) %collective-permute-start.14) | collective-permute-done | bytes 262176 | tf_op jit(solution)/shard_map/ppermute | solution.py:61
  47.5 2.8 %collective-permute-done.15.refs_8_ = bf16[512,256]{1,0:T(8,128)(2,1)S(1)} collective-permute-done((bf16[512,256]{1,0:T(8,128)(2,1)S(1)}, bf16[512,256]{1,0:T(8,128)(2,1)S(1)}, u32[]{:S(2)}, u32[]{:S(2)}) %collective-permute-start.15) | collective-permute-done | bytes 262176 | tf_op jit(solution)/shard_map/ppermute | solution.py:61
  50.4 1.5 %collective-permute-done.17.refs_10_ = bf16[512,256]{1,0:T(8,128)(2,1)S(1)} collective-permute-done((bf16[512,256]{1,0:T(8,128)(2,1)S(1)}, bf16[512,256]{1,0:T(8,128)(2,1)S(1)}, u32[]{:S(2)}, u32[]{:S(2)}) %collective-permute-start.17) | collective-permute-done | bytes 262176 | tf_op jit(solution)/shard_map/ppermute | solution.py:61
  51.9 5.3 %dense_and_backward.1 = (bf16[256,512]{1,0:T(8,128)(2,1)}, bf16[144,512]{1,0:T(8,128)(2,1)S(1)}, bf16[256,512]{1,0:T(8,128)(2,1)S(1)}, bf16[256,512]{1,0:T(8,128...) custom-call(bf16[512,512]{1,0:T(8,128)(2,1)S(1)} %copy-done.2, ...), custom_call_target="tpu_custom_call" | custom-call | flops 1342177280 | bytes 4194304 | tf_op jit(solution)/shard_map/dense_and_backward/pallas_call | solution.py:202
  57.2 0.5 collective-permute-start.18
  57.7 1.1 %collective-permute-start.20 = (bf16[256,512]{1,0:T(8,128)(2,1)S(1)}, bf16[256,512]{1,0:T(8,128)(2,1)S(1)}, u32[]{:S(2)}, u32[]{:S(2)}) collective-permute-start(bf16[256,512]{1,0:T(8,128)(2,1)S(1)} %get-tuple-element.62), channel_id=1, source_target_pairs={{0,4},{4,0},{8,12},{12,8},{16,20},{20,16},{24,28},{28,24},{1,5},{5... | collective-permute-start | bytes 786440 | tf_op jit(solution)/shard_map/ppermute | solution.py:57
  58.8 4.7 %collective-permute-done.18 = bf16[144,512]{1,0:T(8,128)(2,1)S(1)} collective-permute-done((bf16[144,512]{1,0:T(8,128)(2,1)S(1)}, bf16[144,512]{1,0:T(8,128)(2,1)S(1)}, u32[]{:S(2)}, u32[]{:S(2)}) %collective-permute-start.18) | collective-permute-done | bytes 147488 | tf_op jit(solution)/shard_map/ppermute | solution.py:57
  63.6 0.1 select_select_fusion.1
  63.7 0.8 collective-permute-start.19
  64.5 1.5 %collective-permute-done.20 = bf16[256,512]{1,0:T(8,128)(2,1)S(1)} collective-permute-done((bf16[256,512]{1,0:T(8,128)(2,1)S(1)}, bf16[256,512]{1,0:T(8,128)(2,1)S(1)}, u32[]{:S(2)}, u32[]{:S(2)}) %collective-permute-start.20) | collective-permute-done | bytes 262176 | tf_op jit(solution)/shard_map/ppermute | solution.py:57
  66.0 0.1 add_convert_fusion.2
  66.1 1.1 %collective-permute-start.21 = (bf16[256,512]{1,0:T(8,128)(2,1)S(1)}, bf16[256,512]{1,0:T(8,128)(2,1)S(1)}, u32[]{:S(2)}, u32[]{:S(2)}) collective-permute-start(bf16[256,512]{1,0:T(8,128)(2,1)S(1)} %get-tuple-element.64), channel_id=1, source_target_pairs={{0,4},{4,0},{8,12},{12,8},{16,20},{20,16},{24,28},{28,24},{1,5},{5... | collective-permute-start | bytes 786440 | tf_op jit(solution)/shard_map/ppermute | solution.py:57
  67.2 1.7 %collective-permute-start.22 = (bf16[256,512]{1,0:T(8,128)(2,1)S(1)}, bf16[256,512]{1,0:T(8,128)(2,1)S(1)}, u32[]{:S(2)}, u32[]{:S(2)}) collective-permute-start(bf16[256,512]{1,0:T(8,128)(2,1)S(1)} %add_convert_fusion.2), channel_id=1, source_target_pairs={{0,8},{4,12},{8,0},{12,4},{16,24},{20,28},{24,16},{28,20},{1,9},{5... | collective-permute-start | bytes 786440 | tf_op jit(solution)/shard_map/ppermute | solution.py:57
  68.8 4.1 %collective-permute-done.19 = bf16[144,512]{1,0:T(8,128)(2,1)S(1)} collective-permute-done((bf16[144,512]{1,0:T(8,128)(2,1)S(1)}, bf16[144,512]{1,0:T(8,128)(2,1)S(1)}, u32[]{:S(2)}, u32[]{:S(2)}) %collective-permute-start.19) | collective-permute-done | bytes 147488 | tf_op jit(solution)/shard_map/ppermute | solution.py:57
  73.0 0.1 select_select_fusion
  73.1 1.0 %collective-permute-start.28 = (bf16[256,512]{1,0:T(8,128)(2,1)S(1)}, bf16[256,512]{1,0:T(8,128)(2,1)S(1)}, u32[]{:S(2)}, u32[]{:S(2)}) collective-permute-start(bf16[256,512]{1,0:T(8,128)(2,1)S(1)} %get-tuple-element.73), channel_id=1, source_target_pairs={{0,4},{4,0},{8,12},{12,8},{16,20},{20,16},{24,28},{28,24},{1,5},{5... | collective-permute-start | bytes 786440 | tf_op jit(solution)/shard_map/ppermute | solution.py:57
  74.1 3.3 %collective-permute-done.22 = bf16[256,512]{1,0:T(8,128)(2,1)S(1)} collective-permute-done((bf16[256,512]{1,0:T(8,128)(2,1)S(1)}, bf16[256,512]{1,0:T(8,128)(2,1)S(1)}, u32[]{:S(2)}, u32[]{:S(2)}) %collective-permute-start.22) | collective-permute-done | bytes 262176 | tf_op jit(solution)/shard_map/ppermute | solution.py:57
  77.4 0.1 convert_add_fusion
  77.5 1.2 %collective-permute-start.23 = (bf16[144,512]{1,0:T(8,128)(2,1)S(1)}, bf16[144,512]{1,0:T(8,128)(2,1)S(1)}, u32[]{:S(2)}, u32[]{:S(2)}) collective-permute-start(bf16[144,512]{1,0:T(8,128)(2,1)S(1)} %pad_maximum_fusion.4), channel_id=1, source_target_pairs={{0,4},{4,0},{8,12},{12,8},{16,20},{20,16},{24,28},{28,24},{1,5},{5... | collective-permute-start | bytes 442376 | tf_op jit(solution)/shard_map/ppermute | solution.py:57
  78.7 3.7 %collective-permute-done.28 = bf16[256,512]{1,0:T(8,128)(2,1)S(1)} collective-permute-done((bf16[256,512]{1,0:T(8,128)(2,1)S(1)}, bf16[256,512]{1,0:T(8,128)(2,1)S(1)}, u32[]{:S(2)}, u32[]{:S(2)}) %collective-permute-start.28) | collective-permute-done | bytes 262176 | tf_op jit(solution)/shard_map/ppermute | solution.py:57
  82.3 0.1 add_convert_fusion.1
  82.4 0.1 collective-permute-start.29
  82.5 2.0 %collective-permute-done.23 = bf16[144,512]{1,0:T(8,128)(2,1)S(1)} collective-permute-done((bf16[144,512]{1,0:T(8,128)(2,1)S(1)}, bf16[144,512]{1,0:T(8,128)(2,1)S(1)}, u32[]{:S(2)}, u32[]{:S(2)}) %collective-permute-start.23) | collective-permute-done | bytes 147488 | tf_op jit(solution)/shard_map/ppermute | solution.py:57
  84.5 0.9 collective-permute-start.26
  85.5 0.8 collective-permute-start.24
  86.3 4.2 %collective-permute-done.24.refs_1_ = bf16[128,512]{1,0:T(8,128)(2,1)S(1)} collective-permute-done((bf16[128,512]{1,0:T(8,128)(2,1)S(1)}, bf16[128,512]{1,0:T(8,128)(2,1)S(1)}, u32[]{:S(2)}, u32[]{:S(2)}) %collective-permute-start.24) | collective-permute-done | bytes 131104 | tf_op jit(solution)/shard_map/ppermute | solution.py:61
  90.5 0.1 collective-permute-start.25
  90.6 0.6 slice_add_fusion
  91.2 0.1 collective-permute-done.27
  91.3 3.0 %collective-permute-done.29 = bf16[256,512]{1,0:T(8,128)(2,1)S(1)} collective-permute-done((bf16[256,512]{1,0:T(8,128)(2,1)S(1)}, bf16[256,512]{1,0:T(8,128)(2,1)S(1)}, u32[]{:S(2)}, u32[]{:S(2)}) %collective-permute-start.29) | collective-permute-done | bytes 262176 | tf_op jit(solution)/shard_map/ppermute | solution.py:57
  94.3 0.8 add_convert_fusion
  95.2 1.1 %place_weight_gradient.1 = f32[512,512]{1,0:T(8,128)} custom-call(bf16[128,512]{1,0:T(8,128)(2,1)S(1)} %slice.109.refs_0_, bf16[128,512]{1,0:T(8,128)(2,1)S(1)} %collective-permute-done.24.refs_1_, bf16[128,512]{1,0:T(8,128)(2,1)S(1)} %get-tuple-element.79.refs_2_, bf16[128,512]{1,0:T(8,128)(2,1)S(1)} %get-tuple-element.78.refs_3_), custom_call_target="tpu_custom_call" | custom-call | flops 262144 | bytes 1572864 | tf_op jit(solution)/shard_map/place_weight_gradient/pallas_call | solution.py:239
  (37 shorter events, 0.4 us)
Async XLA Ops:
  0.6 1.9 %collective-permute-start = (bf16[256,512]{1,0:T(8,128)(2,1)}, bf16[256,512]{1,0:T(8,128)(2,1)S(1)}, u32[]{:S(2)}, u32[]{:S(2)}) collective-permute-start(bf16[256,512]{1,0:T(8,128)(2,1)} %param.8), channel_id=1, source_target_pairs={{0,1},{1,0},{2,3},{3,2},{4,5},{5,4},{6,7},{7,6},{8,9},{9,8},{10,11... | collective-permute-start | bytes 786440 | tf_op jit(solution)/shard_map/ppermute | solution.py:61
  2.5 4.6 %copy-start.1 = (bf16[256,512]{1,0:T(8,128)(2,1)S(1)}, bf16[256,512]{1,0:T(8,128)(2,1)}, u32[]{:S(2)}) copy-start(bf16[256,512]{1,0:T(8,128)(2,1)} %refs_0_) | copy-start | bytes 786436
  2.6 9.6 %collective-permute-start.1 = (bf16[2,256,256]{2,1,0:T(8,128)(2,1)S(1)}, bf16[2,256,256]{2,1,0:T(8,128)(2,1)S(1)}, u32[]{:S(2)}, u32[]{:S(2)}) collective-permute-start(bf16[2,256,256]{2,1,0:T(8,128)(2,1)S(1)} %pad_maximum_fusion.1.refs_0_), channel_id=1, source_target_pairs={{0,4},{4,0},{8,12},{12,8},{16,20},{20,16},{24,28},{28,24},{1,5},{5... | collective-permute-start | bytes 786440 | tf_op jit(solution)/shard_map/ppermute | solution.py:57
  5.5 12.4 %collective-permute-start.2 = (bf16[2,256,256]{2,1,0:T(8,128)(2,1)S(1)}, bf16[2,256,256]{2,1,0:T(8,128)(2,1)S(1)}, u32[]{:S(2)}, u32[]{:S(2)}) collective-permute-start(bf16[2,256,256]{2,1,0:T(8,128)(2,1)S(1)} %pad_maximum_fusion.1.refs_0_), channel_id=1, source_target_pairs={{0,8},{4,12},{8,0},{12,4},{16,24},{20,28},{24,16},{28,20},{1,9},{5... | collective-permute-start | bytes 786440 | tf_op jit(solution)/shard_map/ppermute | solution.py:57
  7.1 11.1 %collective-permute-start.3 = (bf16[256,512]{1,0:T(8,128)(2,1)S(1)}, bf16[256,512]{1,0:T(8,128)(2,1)S(1)}, u32[]{:S(2)}, u32[]{:S(2)}) collective-permute-start(bf16[256,512]{1,0:T(8,128)(2,1)S(1)} %copy-done.1), channel_id=1, source_target_pairs={{0,2},{1,3},{2,0},{3,1},{4,6},{5,7},{6,4},{7,5},{8,10},{9,11},{10,... | collective-permute-start | bytes 786440 | tf_op jit(solution)/shard_map/ppermute | solution.py:61
  8.6 14.1 %collective-permute-start.4 = (bf16[2,256,256]{2,1,0:T(8,128)(2,1)S(1)}, bf16[2,256,256]{2,1,0:T(8,128)(2,1)S(1)}, u32[]{:S(2)}, u32[]{:S(2)}) collective-permute-start(bf16[2,256,256]{2,1,0:T(8,128)(2,1)S(1)} %pad_maximum_fusion.1.refs_0_), channel_id=1, source_target_pairs={{0,16},{4,20},{8,24},{12,28},{16,0},{20,4},{24,8},{28,12},{1,17},{... | collective-permute-start | bytes 786440 | tf_op jit(solution)/shard_map/ppermute | solution.py:57
  17.9 7.0 %collective-permute-start.6 = (bf16[2,256,256]{2,1,0:T(8,128)(2,1)S(1)}, bf16[2,256,256]{2,1,0:T(8,128)(2,1)S(1)}, u32[]{:S(2)}, u32[]{:S(2)}) collective-permute-start(bf16[2,256,256]{2,1,0:T(8,128)(2,1)S(1)} %collective-permute-done.2.refs_2_), channel_id=1, source_target_pairs={{0,4},{4,0},{8,12},{12,8},{16,20},{20,16},{24,28},{28,24},{1,5},{5... | collective-permute-start | bytes 786440 | tf_op jit(solution)/shard_map/ppermute | solution.py:57
  18.3 1.0 %copy-start = (bf16[1,1,12,128,128]{4,3,2,1,0:T(8,128)(2,1)S(1)}, bf16[1,1,12,128,128]{4,3,2,1,0:T(8,128)(2,1)}, u32[]{:S(2)}) copy-start(bf16[1,1,12,128,128]{4,3,2,1,0:T(8,128)(2,1)} %param.9) | copy-start | bytes 1179652
  18.3 10.8 %collective-permute-start.10 = (bf16[2,256,512]{2,1,0:T(8,128)(2,1)S(1)}, bf16[2,256,512]{2,1,0:T(8,128)(2,1)S(1)}, u32[]{:S(2)}, u32[]{:S(2)}) collective-permute-start(bf16[2,256,512]{2,1,0:T(8,128)(2,1)S(1)} %pad_maximum_fusion), channel_id=1, source_target_pairs={{0,1},{1,0},{2,3},{3,2},{4,5},{5,4},{6,7},{7,6},{8,9},{9,8},{10,11... | collective-permute-start | bytes 1572872 | tf_op jit(solution)/shard_map/ppermute | solution.py:61
  19.3 9.8 %collective-permute-start.9 = (bf16[12,128,128]{2,1,0:T(8,128)(2,1)S(1)}, bf16[12,128,128]{2,1,0:T(8,128)(2,1)S(1)}, u32[]{:S(2)}, u32[]{:S(2)}) collective-permute-start(bf16[12,128,128]{2,1,0:T(8,128)(2,1)S(1)} %bitcast.21), channel_id=1, source_target_pairs={{0,1},{1,0},{2,3},{3,2},{4,5},{5,4},{6,7},{7,6},{8,9},{9,8},{10,11... | collective-permute-start | bytes 1179656 | tf_op jit(solution)/shard_map/ppermute | solution.py:61
  22.7 6.4 %collective-permute-start.5 = (bf16[2,256,256]{2,1,0:T(8,128)(2,1)S(1)}, bf16[2,256,256]{2,1,0:T(8,128)(2,1)S(1)}, u32[]{:S(2)}, u32[]{:S(2)}) collective-permute-start(bf16[2,256,256]{2,1,0:T(8,128)(2,1)S(1)} %collective-permute-done.4.refs_4_), channel_id=1, source_target_pairs={{0,8},{4,12},{8,0},{12,4},{16,24},{20,28},{24,16},{28,20},{1,9},{5... | collective-permute-start | bytes 786440 | tf_op jit(solution)/shard_map/ppermute | solution.py:57
  24.9 6.4 %collective-permute-start.7 = (bf16[2,256,256]{2,1,0:T(8,128)(2,1)S(1)}, bf16[2,256,256]{2,1,0:T(8,128)(2,1)S(1)}, u32[]{:S(2)}, u32[]{:S(2)}) collective-permute-start(bf16[2,256,256]{2,1,0:T(8,128)(2,1)S(1)} %collective-permute-done.4.refs_4_), channel_id=1, source_target_pairs={{0,4},{4,0},{8,12},{12,8},{16,20},{20,16},{24,28},{28,24},{1,5},{5... | collective-permute-start | bytes 786440 | tf_op jit(solution)/shard_map/ppermute | solution.py:57
  26.4 0.7 copy-start.4
  26.4 0.7 copy-start.5
  27.2 24.7 %copy-start.2 = (bf16[512,512]{1,0:T(8,128)(2,1)S(1)}, bf16[512,512]{1,0:T(8,128)(2,1)}, u32[]{:S(2)}) copy-start(bf16[512,512]{1,0:T(8,128)(2,1)} %w_ref.1) | copy-start | bytes 1572868
  27.2 1.1 %collective-permute-start.8 = (s32[25]{0:T(128)S(1)}, s32[25]{0:T(128)S(1)}, u32[]{:S(2)}, u32[]{:S(2)}) collective-permute-start(s32[25]{0:T(128)S(1)} %pad_add_fusion.io_ref.idx), channel_id=1, source_target_pairs={{0,1},{1,0},{2,3},{3,2},{4,5},{5,4},{6,7},{7,6},{8,9},{9,8},{10,11... | collective-permute-start | bytes 308 | tf_op jit(solution)/shard_map/ppermute | solution.py:61
  31.3 6.4 %collective-permute-start.11 = (bf16[2,256,256]{2,1,0:T(8,128)(2,1)S(1)}, bf16[2,256,256]{2,1,0:T(8,128)(2,1)S(1)}, u32[]{:S(2)}, u32[]{:S(2)}) collective-permute-start(bf16[2,256,256]{2,1,0:T(8,128)(2,1)S(1)} %collective-permute-done.5.refs_6_), channel_id=1, source_target_pairs={{0,4},{4,0},{8,12},{12,8},{16,20},{20,16},{24,28},{28,24},{1,5},{5... | collective-permute-start | bytes 786440 | tf_op jit(solution)/shard_map/ppermute | solution.py:57
  39.3 12.6 %copy-start.3 = (f32[512]{0:T(512)S(1)}, f32[512]{0:T(512)}, u32[]{:S(2)}) copy-start(f32[512]{0:T(512)} %param.14) | copy-start | bytes 6148
  39.3 8.2 %collective-permute-start.14 = (bf16[512,256]{1,0:T(8,128)(2,1)S(1)}, bf16[512,256]{1,0:T(8,128)(2,1)S(1)}, u32[]{:S(2)}, u32[]{:S(2)}) collective-permute-start(bf16[512,256]{1,0:T(8,128)(2,1)S(1)} %get-tuple-element.54.refs_3_), channel_id=1, source_target_pairs={{0,2},{1,3},{2,0},{3,1},{4,6},{5,7},{6,4},{7,5},{8,10},{9,11},{10,... | collective-permute-start | bytes 786440 | tf_op jit(solution)/shard_map/ppermute | solution.py:61
  42.4 8.0 %collective-permute-start.15 = (bf16[512,256]{1,0:T(8,128)(2,1)S(1)}, bf16[512,256]{1,0:T(8,128)(2,1)S(1)}, u32[]{:S(2)}, u32[]{:S(2)}) collective-permute-start(bf16[512,256]{1,0:T(8,128)(2,1)S(1)} %get-tuple-element.55.refs_4_), channel_id=1, source_target_pairs={{0,2},{1,3},{2,0},{3,1},{4,6},{5,7},{6,4},{7,5},{8,10},{9,11},{10,... | collective-permute-start | bytes 786440 | tf_op jit(solution)/shard_map/ppermute | solution.py:61
  42.4 7.9 %collective-permute-start.12 = (bf16[512,256]{1,0:T(8,128)(2,1)S(1)}, bf16[512,256]{1,0:T(8,128)(2,1)S(1)}, u32[]{:S(2)}, u32[]{:S(2)}) collective-permute-start(bf16[512,256]{1,0:T(8,128)(2,1)S(1)} %get-tuple-element.54.refs_3_), channel_id=1, source_target_pairs={{0,1},{1,0},{2,3},{3,2},{4,5},{5,4},{6,7},{7,6},{8,9},{9,8},{10,11... | collective-permute-start | bytes 786440 | tf_op jit(solution)/shard_map/ppermute | solution.py:61
  42.4 7.9 %collective-permute-start.13 = (bf16[512,256]{1,0:T(8,128)(2,1)S(1)}, bf16[512,256]{1,0:T(8,128)(2,1)S(1)}, u32[]{:S(2)}, u32[]{:S(2)}) collective-permute-start(bf16[512,256]{1,0:T(8,128)(2,1)S(1)} %get-tuple-element.55.refs_4_), channel_id=1, source_target_pairs={{0,1},{1,0},{2,3},{3,2},{4,5},{5,4},{6,7},{7,6},{8,9},{9,8},{10,11... | collective-permute-start | bytes 786440 | tf_op jit(solution)/shard_map/ppermute | solution.py:61
  47.5 2.8 %collective-permute-start.16 = (bf16[512,256]{1,0:T(8,128)(2,1)S(1)}, bf16[512,256]{1,0:T(8,128)(2,1)S(1)}, u32[]{:S(2)}, u32[]{:S(2)}) collective-permute-start(bf16[512,256]{1,0:T(8,128)(2,1)S(1)} %collective-permute-done.14.refs_7_), channel_id=1, source_target_pairs={{0,1},{1,0},{2,3},{3,2},{4,5},{5,4},{6,7},{7,6},{8,9},{9,8},{10,11... | collective-permute-start | bytes 786440 | tf_op jit(solution)/shard_map/ppermute | solution.py:61
  50.3 1.5 %collective-permute-start.17 = (bf16[512,256]{1,0:T(8,128)(2,1)S(1)}, bf16[512,256]{1,0:T(8,128)(2,1)S(1)}, u32[]{:S(2)}, u32[]{:S(2)}) collective-permute-start(bf16[512,256]{1,0:T(8,128)(2,1)S(1)} %collective-permute-done.15.refs_8_), channel_id=1, source_target_pairs={{0,1},{1,0},{2,3},{3,2},{4,5},{5,4},{6,7},{7,6},{8,9},{9,8},{10,11... | collective-permute-start | bytes 786440 | tf_op jit(solution)/shard_map/ppermute | solution.py:61
  57.2 6.3 %collective-permute-start.18 = (bf16[144,512]{1,0:T(8,128)(2,1)S(1)}, bf16[144,512]{1,0:T(8,128)(2,1)S(1)}, u32[]{:S(2)}, u32[]{:S(2)}) collective-permute-start(bf16[144,512]{1,0:T(8,128)(2,1)S(1)} %get-tuple-element.57), channel_id=1, source_target_pairs={{0,8},{4,12},{8,0},{12,4},{16,24},{20,28},{24,16},{28,20},{1,9},{5... | collective-permute-start | bytes 442376 | tf_op jit(solution)/shard_map/ppermute | solution.py:57
  57.7 8.3 %collective-permute-start.20 = (bf16[256,512]{1,0:T(8,128)(2,1)S(1)}, bf16[256,512]{1,0:T(8,128)(2,1)S(1)}, u32[]{:S(2)}, u32[]{:S(2)}) collective-permute-start(bf16[256,512]{1,0:T(8,128)(2,1)S(1)} %get-tuple-element.62), channel_id=1, source_target_pairs={{0,4},{4,0},{8,12},{12,8},{16,20},{20,16},{24,28},{28,24},{1,5},{5... | collective-permute-start | bytes 786440 | tf_op jit(solution)/shard_map/ppermute | solution.py:57
  63.7 9.2 %collective-permute-start.19 = (bf16[144,512]{1,0:T(8,128)(2,1)S(1)}, bf16[144,512]{1,0:T(8,128)(2,1)S(1)}, u32[]{:S(2)}, u32[]{:S(2)}) collective-permute-start(bf16[144,512]{1,0:T(8,128)(2,1)S(1)} %pad_maximum_fusion.3), channel_id=1, source_target_pairs={{0,16},{4,20},{8,24},{12,28},{16,0},{20,4},{24,8},{28,12},{1,17},{... | collective-permute-start | bytes 442376 | tf_op jit(solution)/shard_map/ppermute | solution.py:57
  66.1 8.0 %collective-permute-start.21 = (bf16[256,512]{1,0:T(8,128)(2,1)S(1)}, bf16[256,512]{1,0:T(8,128)(2,1)S(1)}, u32[]{:S(2)}, u32[]{:S(2)}) collective-permute-start(bf16[256,512]{1,0:T(8,128)(2,1)S(1)} %get-tuple-element.64), channel_id=1, source_target_pairs={{0,4},{4,0},{8,12},{12,8},{16,20},{20,16},{24,28},{28,24},{1,5},{5... | collective-permute-start | bytes 786440 | tf_op jit(solution)/shard_map/ppermute | solution.py:57
  67.2 10.2 %collective-permute-start.22 = (bf16[256,512]{1,0:T(8,128)(2,1)S(1)}, bf16[256,512]{1,0:T(8,128)(2,1)S(1)}, u32[]{:S(2)}, u32[]{:S(2)}) collective-permute-start(bf16[256,512]{1,0:T(8,128)(2,1)S(1)} %add_convert_fusion.2), channel_id=1, source_target_pairs={{0,8},{4,12},{8,0},{12,4},{16,24},{20,28},{24,16},{28,20},{1,9},{5... | collective-permute-start | bytes 786440 | tf_op jit(solution)/shard_map/ppermute | solution.py:57
  73.1 9.2 %collective-permute-start.28 = (bf16[256,512]{1,0:T(8,128)(2,1)S(1)}, bf16[256,512]{1,0:T(8,128)(2,1)S(1)}, u32[]{:S(2)}, u32[]{:S(2)}) collective-permute-start(bf16[256,512]{1,0:T(8,128)(2,1)S(1)} %get-tuple-element.73), channel_id=1, source_target_pairs={{0,4},{4,0},{8,12},{12,8},{16,20},{20,16},{24,28},{28,24},{1,5},{5... | collective-permute-start | bytes 786440 | tf_op jit(solution)/shard_map/ppermute | solution.py:57
  77.5 7.0 %collective-permute-start.23 = (bf16[144,512]{1,0:T(8,128)(2,1)S(1)}, bf16[144,512]{1,0:T(8,128)(2,1)S(1)}, u32[]{:S(2)}, u32[]{:S(2)}) collective-permute-start(bf16[144,512]{1,0:T(8,128)(2,1)S(1)} %pad_maximum_fusion.4), channel_id=1, source_target_pairs={{0,4},{4,0},{8,12},{12,8},{16,20},{20,16},{24,28},{28,24},{1,5},{5... | collective-permute-start | bytes 442376 | tf_op jit(solution)/shard_map/ppermute | solution.py:57
  78.7 12.7 %collective-permute-start.27 = (bf16[256,512]{1,0:T(8,128)(2,1)S(1)}, bf16[256,512]{1,0:T(8,128)(2,1)S(1)}, u32[]{:S(2)}, u32[]{:S(2)}) collective-permute-start(bf16[256,512]{1,0:T(8,128)(2,1)S(1)} %convert_add_fusion), channel_id=1, source_target_pairs={{0,16},{4,20},{8,24},{12,28},{16,0},{20,4},{24,8},{28,12},{1,17},{... | collective-permute-start | bytes 786440 | tf_op jit(solution)/shard_map/ppermute | solution.py:57
  82.4 11.9 %collective-permute-start.29 = (bf16[256,512]{1,0:T(8,128)(2,1)S(1)}, bf16[256,512]{1,0:T(8,128)(2,1)S(1)}, u32[]{:S(2)}, u32[]{:S(2)}) collective-permute-start(bf16[256,512]{1,0:T(8,128)(2,1)S(1)} %add_convert_fusion.1), channel_id=1, source_target_pairs={{0,8},{4,12},{8,0},{12,4},{16,24},{20,28},{24,16},{28,20},{1,9},{5... | collective-permute-start | bytes 786440 | tf_op jit(solution)/shard_map/ppermute | solution.py:57
  84.5 9.8 %collective-permute-start.26 = (bf16[256,512]{1,0:T(8,128)(2,1)S(1)}, bf16[256,512]{1,0:T(8,128)(2,1)S(1)}, u32[]{:S(2)}, u32[]{:S(2)}) collective-permute-start(bf16[256,512]{1,0:T(8,128)(2,1)S(1)} %get-tuple-element.70), channel_id=1, source_target_pairs={{0,4},{4,0},{8,12},{12,8},{16,20},{20,16},{24,28},{28,24},{1,5},{5... | collective-permute-start | bytes 786440 | tf_op jit(solution)/shard_map/ppermute | solution.py:57
  85.5 5.0 %collective-permute-start.24 = (bf16[128,512]{1,0:T(8,128)(2,1)S(1)}, bf16[128,512]{1,0:T(8,128)(2,1)S(1)}, u32[]{:S(2)}, u32[]{:S(2)}) collective-permute-start(bf16[128,512]{1,0:T(8,128)(2,1)S(1)} %slice.109.refs_0_), channel_id=1, source_target_pairs={{0,2},{1,3},{2,0},{3,1},{4,6},{5,7},{6,4},{7,5},{8,10},{9,11},{10,... | collective-permute-start | bytes 393224 | tf_op jit(solution)/shard_map/ppermute | solution.py:61
  90.5 4.6 %collective-permute-start.25 = (bf16[2,128,512]{2,1,0:T(8,128)(2,1)S(1)}, bf16[2,128,512]{2,1,0:T(8,128)(2,1)S(1)}, u32[]{:S(2)}, u32[]{:S(2)}) collective-permute-start(bf16[2,128,512]{2,1,0:T(8,128)(2,1)S(1)} %pad_maximum_fusion.2), channel_id=1, source_target_pairs={{0,1},{1,0},{2,3},{3,2},{4,5},{5,4},{6,7},{7,6},{8,9},{9,8},{10,11... | collective-permute-start | bytes 786440 | tf_op jit(solution)/shard_map/ppermute | solution.py:61
